TPU v7x, 32 devices: a whole 2x2x4 slice. The times are simulated.
32 devices in a mesh: tok: 8 (over z, x), feat: 4 (over y, core).
Axes of the slice: x: 2, y: 2, z: 4, core: 2. Of those that a mesh axis runs over, the one named last changes fastest.
Arguments:
- patches: bfloat16 [96, 6144], P('tok', 'feat'), may hold values from -640 to 640
- frame_counts: int32 [8], P('tok'), may hold values from 1 to 3
- patch_mask: int32 [96], P('tok'), may hold values 0 or 1
- norm_gain: float32 [6144], P('feat'), may hold values from 0.1 to 1.9
- up_weight: bfloat16 [6144, 24576], P('feat', 'tok'), may hold values from -0.078125 to 0.078125
- up_bias: float32 [24576], P('tok'), may hold values from -3 to 3
- down_weight: bfloat16 [24576, 6144], P('tok', 'feat'), may hold values from -0.0390625 to 0.0390625
- down_bias: float32 [6144], P('feat'), may hold values from -3 to 3
Outputs:
- block_output: bfloat16 [96, 6144], P('tok', 'feat')
All inputs are finite; a program needn't handle non-finite values. No bound on the sum of `patch_mask` on one device may be relied on, other than what follows from the above.
Results may differ from a plain program's by a relative error of at most 0.0053.
Values may be sent and summed in bfloat16 or wider, within the bound.
No kernel may reach another device: no remote copies, remote signals or barrier semaphores. Data moves between devices by JAX's collectives and lax.ppermute only.
A program may use at most 64 MiB of HBM per device.

v0:
```python
import jax
import jax.numpy as jnp
from jax import lax
from jax.sharding import PartitionSpec as P

FRAME_TOK = 4


epsilon = 1e-06


def normalize(values, row_sums, squares, full_width, norm_gain):
    row_mean = row_sums / full_width
    spread = squares / full_width - row_mean * row_mean
    scaled = (values - row_mean[:, None]) * lax.rsqrt(spread + epsilon)[:, None]
    return (scaled * norm_gain[None, :]).astype(jnp.bfloat16)


def per_device(
    patches, frame_counts, patch_mask, norm_gain, up_weight, up_bias, down_weight, down_bias
):
    tok_rows = patches.shape[0]
    full_width = patches.shape[1] * lax.axis_size("feat")
    raw_values = lax.all_gather(patches, "tok", axis=0, tiled=True)
    values = raw_values.astype(jnp.float32)
    row_sums, squares = lax.psum(
        (jnp.sum(values, axis=1), jnp.sum(values * values, axis=1)), "feat"
    )
    gathered = normalize(values, row_sums, squares, full_width, norm_gain)
    row_block = gathered
    preact = lax.psum_scatter(
        jnp.dot(row_block, up_weight, preferred_element_type=jnp.float32),
        "feat",
        scatter_dimension=0,
        tiled=True,
    )
    active = jax.nn.gelu(preact + up_bias[None, :], approximate=True).astype(jnp.bfloat16)
    hidden = lax.all_gather(active, "feat", axis=0, tiled=True)
    row_block = hidden
    summed = lax.psum_scatter(
        jnp.dot(row_block, down_weight, preferred_element_type=jnp.float32),
        "tok",
        scatter_dimension=0,
        tiled=True,
    )
    positions = jnp.arange(tok_rows, dtype=jnp.int32)
    valid_rows = ((positions // FRAME_TOK < frame_counts[0]) & (patch_mask == 1)).astype(
        jnp.float32
    )
    return (valid_rows[:, None] * (summed + down_bias[None, :])).astype(jnp.bfloat16)


def solution(mesh):
    in_specs = (
        P("tok", "feat"),
        P("tok"),
        P("tok"),
        P("feat"),
        P("feat", "tok"),
        P("tok"),
        P("tok", "feat"),
        P("feat"),
    )
    out_specs = P("tok", "feat")
    return jax.shard_map(
        per_device, mesh=mesh, in_specs=in_specs, out_specs=out_specs, check_vma=False
    )
```

profile of v0, /device:TPU:0, one launch (start us, length us, event | category | flops | bytes accessed | tf_op | source)
XLA Modules:
  0.0 134.4 jit_solution(9619309032814327910)
XLA Ops:
  6.5 0.0 reduce-scatter.4.cloned.1.call-start
  6.5 32.9 %all-gather = bf16[8,12,1536]{2,1,0:T(8,128)(2,1)S(1)} all-gather(bf16[1,12,1536]{2,1,0:T(8,128)(2,1)} %bitcast.9), channel_id=1, replica_groups=mesh['tok'=8,'feat'=4] {'tok'}, dimensions={0}, use_global_device_ids=true | all-gather | bytes 331776 | tf_op jit(solution)/shard_map/all_gather | solution.py:24
  39.5 0.1 reshape.8
  39.5 0.1 convert_reduce_fusion
  39.7 0.1 multiply_reduce_fusion
  39.8 0.1 reshape.9
  39.9 5.6 %all-reduce.2 = (f32[96]{0:T(128)S(1)}, f32[96]{0:T(128)S(1)}) all-reduce(f32[96]{0:T(128)S(1)} %multiply_reduce_fusion, f32[96]{0:T(128)S(1)} %reshape.9), channel_id=1, replica_groups=mesh['tok'=8,'feat'=4] {'feat'}, use_global_device_ids=true, to_apply=%region_3.0 | all-reduce | flops 192 | bytes 1536 | tf_op jit(solution)/shard_map/psum | solution.py:26
  45.6 0.0 copy-start
  45.6 6.4 %fusion.9 = f32[96,3072]{1,0:T(8,128)} fusion(bf16[1536,3072]{1,0:T(8,128)(2,1)} %param.12, f32[96,1536]{1,0:T(8,128)S(1)} %reshape.8, f32[1536]{0:T(1024)} %param.11, f32[96]{0:T(128)S(1)} %get-tuple-element.8, f32[96]{0:T(128)S(1)} %get-tuple-element.7), kind=kOutput, calls=%fused_computation.11 | convolution fusion | flops 906559488 | bytes 11213568 | tf_op jit(solution)/shard_map/dot_general | solution.py:32
  52.0 0.0 reduce-scatter.4.cloned.1.call-update
  52.7 26.5 %reduce-scatter.4.cloned.1.call-done = f32[24,3072]{1,0:T(8,128)} async-done(((f32[96,3072]{1,0:T(8,128)}), f32[24,3072]{1,0:T(8,128)}) %reduce-scatter.4.cloned.1.call-update) | async-done | bytes 294928 | tf_op jit(solution)/shard_map/reduce_scatter | solution.py:31
  79.1 0.0 copy-done
  79.1 1.1 fusion.8
  80.2 7.1 %all_gather.7 = bf16[96,3072]{1,0:T(8,128)(2,1)S(1)} all-gather(bf16[24,3072]{1,0:T(8,128)(2,1)S(1)} %fusion.8), channel_id=1, replica_groups=mesh['tok'=8,'feat'=4] {'feat'}, dimensions={0}, use_global_device_ids=true | all-gather | bytes 737280 | tf_op jit(solution)/shard_map/all_gather | solution.py:38
  87.4 0.0 copy-start.3
  87.4 0.0 copy-start.2
  87.4 0.0 copy-start.1
  87.4 5.3 %fusion.15 = f32[96,1536]{1,0:T(8,128)S(1)} fusion(bf16[96,3072]{1,0:T(8,128)(2,1)S(1)} %all_gather.7, bf16[3072,1536]{1,0:T(8,128)(2,1)} %param.14), kind=kOutput, calls=%fused_computation.26 | convolution fusion | flops 905969664 | bytes 10616832 | tf_op jit(solution)/shard_map/dot_general | solution.py:41
  92.7 26.6 %fusion = f32[16,1536]{1,0:T(8,128)S(1)} fusion(f32[96,1536]{1,0:T(8,128)S(1)} %fusion.15), kind=kCustom, calls=%all-reduce-scatter | all-reduce-scatter fusion | flops 196609 | bytes 688640
  119.3 2.3 %collective-permute-start = (f32[16,1536]{1,0:T(8,128)S(1)}, f32[16,1536]{1,0:T(8,128)S(1)}, u32[]{:S(2)}, u32[]{:S(2)}) collective-permute-start(f32[16,1536]{1,0:T(8,128)S(1)} %fusion), channel_id=1, source_target_pairs={{0,4},{4,8},{8,12},{12,16},{16,20},{20,24},{24,28},{1,5},{5,9},{9,... | collective-permute-start | bytes 294920
  121.7 2.6 %collective-permute-start.1 = (f32[12,1536]{1,0:T(8,128)S(1)}, f32[12,1536]{1,0:T(8,128)S(1)}, u32[]{:S(2)}, u32[]{:S(2)}) collective-permute-start(f32[12,1536]{1,0:T(8,128)S(1)} %slice), channel_id=1, source_target_pairs={{0,8},{4,12},{8,16},{12,20},{16,24},{20,28},{1,9},{5,13},{9,17},{1... | collective-permute-start | bytes 221192
  124.3 0.0 copy-done.3
  124.3 0.0 copy-done.2
  124.4 0.6 dynamic-slice.4
  125.6 0.9 collective-permute-done.1
  126.5 0.0 collective-permute-done
  126.5 0.3 concatenate
  126.8 0.0 copy-done.1
  126.9 0.7 fusion.14
  (3 shorter events, 0.0 us)
Async XLA Ops:
  6.5 72.6 %reduce-scatter.4.cloned.1.call-start = ((), (), s32[]{:S(2)}) async-start(), calls=%async_computation.1 | async-start | bytes 1474560 | tf_op jit(solution)/shard_map/reduce_scatter | solution.py:31
  45.6 33.6 %copy-start = (f32[3072]{0:T(1024)S(1)}, f32[3072]{0:T(1024)}, u32[]{:S(2)}) copy-start(f32[3072]{0:T(1024)} %param.13) | copy-start | bytes 36868
  87.4 37.0 %copy-start.3 = (s32[12]{0:T(128)S(1)}, s32[12]{0:T(128)}, u32[]{:S(2)}) copy-start(s32[12]{0:T(128)} %param.10) | copy-start | bytes 148
  87.4 37.0 %copy-start.2 = (u32[32]{0:T(128)S(1)}, u32[32]{0:T(128)}, u32[]{:S(2)}) copy-start(u32[32]{0:T(128)} %constant.40) | copy-start | bytes 388
  87.4 39.5 %copy-start.1 = (f32[1536]{0:T(1024)S(1)}, f32[1536]{0:T(1024)}, u32[]{:S(2)}) copy-start(f32[1536]{0:T(1024)} %param.15) | copy-start | bytes 18436
  119.3 7.2 %collective-permute-start = (f32[16,1536]{1,0:T(8,128)S(1)}, f32[16,1536]{1,0:T(8,128)S(1)}, u32[]{:S(2)}, u32[]{:S(2)}) collective-permute-start(f32[16,1536]{1,0:T(8,128)S(1)} %fusion), channel_id=1, source_target_pairs={{0,4},{4,8},{8,12},{12,16},{16,20},{20,24},{24,28},{1,5},{5,9},{9,... | collective-permute-start | bytes 294920
  121.7 4.8 %collective-permute-start.1 = (f32[12,1536]{1,0:T(8,128)S(1)}, f32[12,1536]{1,0:T(8,128)S(1)}, u32[]{:S(2)}, u32[]{:S(2)}) collective-permute-start(f32[12,1536]{1,0:T(8,128)S(1)} %slice), channel_id=1, source_target_pairs={{0,8},{4,12},{8,16},{12,20},{16,24},{20,28},{1,9},{5,13},{9,17},{1... | collective-permute-start | bytes 221192
Sparse Core Ops, SparseCore 0:
  52.1 26.9 reduce-scatter.3
where the time goes:
time: 135 us; the launch traced here: 134 us
  blocking collectives  72.3 us (54%)
  waiting for transfers between devices  27.4 us (20%)
  between operations  14.8 us (11%)
  matrix products  11.7 us (9%)
  starting transfers between devices  4.98 us (4%)
  other arithmetic  2.06 us (2%)
    all_gather x1, blocking collectives, per_device(): raw_values = lax.all_gather(patches, 'tok', axis=0, tiled=True)  32.9 us
    unnamed x1, blocking collectives  26.6 us
    reduce_scatter x1, waiting for transfers between devices, per_device(): lax.psum_scatter(jnp.dot(row_block, up_weight, preferred_element_type=jnp...  26.5 us
    all_gather x1, blocking collectives, per_device(): hidden = lax.all_gather(active, 'feat', axis=0, tiled=True)  7.14 us
    dot_general x1, matrix products, per_device(): jnp.dot(row_block, up_weight, preferred_element_type=jnp.float32)  6.42 us
    psum x1, blocking collectives, per_device(): lax.psum((jnp.sum(values, axis=1), jnp.sum(values * values, axis=1)), 'fe...  5.64 us
    dot_general x1, matrix products, per_device(): jnp.dot(row_block, down_weight, preferred_element_type=jnp.float32)  5.32 us
    unnamed x2, starting transfers between devices  4.98 us
  transfers between devices with their start and end apart: 3, of which 2 were waited for; matrix products, arithmetic and copies ran while one was open for 0% of the time, Pallas kernels for 0%

commit v1 on v0

v1 whole, which is shorter than its diff:
```python
import jax
import jax.numpy as jnp
from jax import lax
from jax.sharding import PartitionSpec as P

FRAME_TOK = 4

epsilon = 1e-06


def swap(block, axis, mask):
    size = lax.axis_size(axis)
    return lax.ppermute(block, axis, [(i, i ^ mask) for i in range(size)])


def per_device(
    patches, frame_counts, patch_mask, norm_gain, up_weight, up_bias, down_weight, down_bias
):
    tok_rows = patches.shape[0]
    tok_size = lax.axis_size("tok")
    feat_size = lax.axis_size("feat")
    full_width = patches.shape[1] * feat_size
    first_core = lax.axis_index("feat") % 2 == 0

    values = patches.astype(jnp.float32)
    sums = jnp.stack([jnp.sum(values, axis=1), jnp.sum(values * values, axis=1)])
    parts = [swap(sums, "feat", mask) for mask in range(1, feat_size)]
    for part in parts:
        sums = sums + part
    row_mean = sums[0] / full_width
    spread = sums[1] / full_width - row_mean * row_mean
    scaled = (values - row_mean[:, None]) * lax.rsqrt(spread + epsilon)[:, None]
    normed = (scaled * norm_gain[None, :]).astype(jnp.bfloat16)

    masks = range(2, tok_size, 2)
    near = jnp.concatenate([normed] + [swap(normed, "tok", mask) for mask in masks])
    far = swap(near, "tok", 1)
    half = near.shape[0]

    kept = jnp.where(first_core, near, far)
    given = jnp.where(first_core, far, near)
    product = jnp.dot(
        jnp.concatenate([kept, given]), up_weight, preferred_element_type=jnp.float32
    )
    preact = product[:half] + swap(product[half:].astype(jnp.bfloat16), "feat", 1)
    sent = preact.astype(jnp.bfloat16)
    for part in [swap(sent, "feat", mask) for mask in range(2, feat_size, 2)]:
        preact = preact + part
    active = jax.nn.gelu(preact + up_bias[None, :], approximate=True).astype(jnp.bfloat16)
    hidden = jnp.concatenate([active, swap(active, "feat", 1)])
    product = jnp.dot(hidden, down_weight, preferred_element_type=jnp.float32)

    near_sum = jnp.where(first_core, product[:half], product[half:])
    far_sum = jnp.where(first_core, product[half:], product[:half])
    near_sum = near_sum + swap(far_sum.astype(jnp.bfloat16), "tok", 1)
    blocks = near_sum.reshape(tok_size // 2, tok_rows, near_sum.shape[1])
    summed = blocks[0]
    sent = blocks.astype(jnp.bfloat16)
    for part in [swap(sent[mask // 2], "tok", mask) for mask in masks]:
        summed = summed + part

    positions = jnp.arange(tok_rows, dtype=jnp.int32)
    valid_rows = ((positions // FRAME_TOK < frame_counts[0]) & (patch_mask == 1)).astype(
        jnp.float32
    )
    return (valid_rows[:, None] * (summed + down_bias[None, :])).astype(jnp.bfloat16)


def solution(mesh):
    in_specs = (
        P("tok", "feat"),
        P("tok"),
        P("tok"),
        P("feat"),
        P("feat", "tok"),
        P("tok"),
        P("tok", "feat"),
        P("feat"),
    )
    out_specs = P("tok", "feat")
    return jax.shard_map(
        per_device, mesh=mesh, in_specs=in_specs, out_specs=out_specs, check_vma=False
    )
```

time: 135 us -> 58.1 us (0.43)
  blocking collectives: 72.3 us -> 0 us
  between operations: 14.8 us -> 0.8 us
  starting transfers between devices: 4.98 us -> 16 us
  matrix products: 11.7 us -> 7.16 us
  waiting for transfers between devices: 27.4 us -> 30.7 us
    all_gather x2 -> x0, blocking collectives: 40.1 us -> none  [the longest x1 32.9 us: per_device(): raw_values = lax.all_gather(patches, 'tok', axis=0, tiled=True)]
    ppermute x0 -> x14, waiting for transfers between devices: none -> 30.7 us  [swap(): return lax.ppermute(block, axis, [(i, i ^ mask) for i in range(size)])]
    unnamed x1 -> x0, blocking collectives: 26.6 us -> none
    reduce_scatter x1 -> x0, waiting for transfers between devices: 26.5 us -> none  [per_device(): lax.psum_scatter(jnp.dot(row_block, up_weight, preferred_element_type=jnp...]
    ppermute x0 -> x14, starting transfers between devices: none -> 16 us  [swap(): return lax.ppermute(block, axis, [(i, i ^ mask) for i in range(size)])]
    psum x1 -> x0, blocking collectives: 5.64 us -> none  [per_device(): lax.psum((jnp.sum(values, axis=1), jnp.sum(values * values, axis=1)), 'fe...]
    unnamed x2 -> x0, starting transfers between devices: 4.98 us -> none
    dot_general x2, matrix products: 11.7 us -> 7.16 us  [the longest x1 5.55 us: per_device(): jnp.dot(jnp.concatenate([kept, given]), up_weight, preferred_element_type...]
  transfers between devices with their start and end apart: 3 -> 14, of which waited for: 2 -> 11; matrix products, arithmetic and copies ran while one was open for 0% -> 0% of each run, Pallas kernels for 0% -> 0%
where the time goes in v1:
time: 58.1 us; the launch traced here: 57.9 us
  waiting for transfers between devices  30.7 us (53%)
  starting transfers between devices  16 us (28%)
  matrix products  7.16 us (12%)
  other arithmetic  3.13 us (5%)
  between operations  0.8 us (1%)
    ppermute x14, waiting for transfers between devices, swap(): return lax.ppermute(block, axis, [(i, i ^ mask) for i in range(size)])  30.7 us
    ppermute x14, starting transfers between devices, swap(): return lax.ppermute(block, axis, [(i, i ^ mask) for i in range(size)])  16 us
    dot_general x1, matrix products, per_device(): jnp.dot(jnp.concatenate([kept, given]), up_weight, preferred_element_type...  5.55 us
    dot_general x1, matrix products, per_device(): product = jnp.dot(hidden, down_weight, preferred_element_type=jnp.float32)  1.61 us
  transfers between devices with their start and end apart: 14, of which 11 were waited for; matrix products, arithmetic and copies ran while one was open for 0% of the time, Pallas kernels for 0%

profile of v1, /device:TPU:0, one launch (start us, length us, event | category | flops | bytes accessed | tf_op | source)
XLA Modules:
  0.0 57.9 jit_solution(4047801704965764458)
XLA Ops:
  0.0 0.0 copy-start
  0.0 0.9 %convert_reduce_fusion = (f32[12]{0:T(128)S(1)}, f32[12]{0:T(128)S(1)}) fusion(bf16[12,1536]{1,0:T(8,128)(2,1)} %param.8), kind=kLoop, calls=%fused_computation.24 | loop fusion | flops 73704 | bytes 36960 | tf_op jit(solution)/shard_map/reduce_sum | solution.py:26
  1.0 0.5 collective-permute-start
  1.5 2.6 %collective-permute-start.1 = (f32[2,12]{1,0:T(2,128)S(1)}, f32[2,12]{1,0:T(2,128)S(1)}, u32[]{:S(2)}, u32[]{:S(2)}) collective-permute-start(f32[2,12]{1,0:T(2,128)S(1)} %pad_maximum_fusion.1), channel_id=1, source_target_pairs={{0,2},{1,3},{2,0},{3,1},{4,6},{5,7},{6,4},{7,5},{8,10},{9,11},{10,... | collective-permute-start | bytes 296 | tf_op jit(solution)/shard_map/ppermute | solution.py:13
  4.1 0.1 collective-permute-start.2
  4.1 0.0 collective-permute-done
  4.1 1.5 %collective-permute-done.1 = f32[2,12]{1,0:T(2,128)S(1)} collective-permute-done((f32[2,12]{1,0:T(2,128)S(1)}, f32[2,12]{1,0:T(2,128)S(1)}, u32[]{:S(2)}, u32[]{:S(2)}) %collective-permute-start.1) | collective-permute-done | bytes 128 | tf_op jit(solution)/shard_map/ppermute | solution.py:13
  5.6 1.4 %collective-permute-done.2 = f32[2,12]{1,0:T(2,128)S(1)} collective-permute-done((f32[2,12]{1,0:T(2,128)S(1)}, f32[2,12]{1,0:T(2,128)S(1)}, u32[]{:S(2)}, u32[]{:S(2)}) %collective-permute-start.2) | collective-permute-done | bytes 128 | tf_op jit(solution)/shard_map/ppermute | solution.py:13
  7.1 0.9 %fusion.20 = bf16[12,1536]{1,0:T(8,128)(2,1)S(1)} fusion(bf16[12,1536]{1,0:T(8,128)(2,1)} %param.8, f32[1536]{0:T(1024)} %param.11, f32[12]{0:T(128)S(1)} %fusion.27, f32[12]{0:T(128)S(1)} %multiply_bitcast_fusion), kind=kLoop, calls=%fused_computation.31 | loop fusion | flops 92160 | bytes 79968 | tf_op jit(solution)/shard_map/convert_element_type | solution.py:33
  8.0 1.6 %collective-permute-start.3 = (bf16[12,1536]{1,0:T(8,128)(2,1)S(1)}, bf16[12,1536]{1,0:T(8,128)(2,1)S(1)}, u32[]{:S(2)}, u32[]{:S(2)}) collective-permute-start(bf16[12,1536]{1,0:T(8,128)(2,1)S(1)} %fusion.20), channel_id=1, source_target_pairs={{0,8},{4,12},{8,0},{12,4},{16,24},{20,28},{24,16},{28,20},{1,9},{5... | collective-permute-start | bytes 110600 | tf_op jit(solution)/shard_map/ppermute | solution.py:13
  9.6 2.6 %collective-permute-start.4 = (bf16[12,1536]{1,0:T(8,128)(2,1)S(1)}, bf16[12,1536]{1,0:T(8,128)(2,1)S(1)}, u32[]{:S(2)}, u32[]{:S(2)}) collective-permute-start(bf16[12,1536]{1,0:T(8,128)(2,1)S(1)} %fusion.20), channel_id=1, source_target_pairs={{0,16},{4,20},{8,24},{12,28},{16,0},{20,4},{24,8},{28,12},{1,17},{... | collective-permute-start | bytes 110600 | tf_op jit(solution)/shard_map/ppermute | solution.py:13
  12.2 0.2 collective-permute-start.5
  12.4 0.0 collective-permute-done.3
  12.4 3.1 %collective-permute-done.4 = bf16[12,1536]{1,0:T(8,128)(2,1)S(1)} collective-permute-done((bf16[12,1536]{1,0:T(8,128)(2,1)S(1)}, bf16[12,1536]{1,0:T(8,128)(2,1)S(1)}, u32[]{:S(2)}, u32[]{:S(2)}) %collective-permute-start.4) | collective-permute-done | bytes 36896 | tf_op jit(solution)/shard_map/ppermute | solution.py:13
  15.5 2.6 %collective-permute-done.5 = bf16[12,1536]{1,0:T(8,128)(2,1)S(1)} collective-permute-done((bf16[12,1536]{1,0:T(8,128)(2,1)S(1)}, bf16[12,1536]{1,0:T(8,128)(2,1)S(1)}, u32[]{:S(2)}, u32[]{:S(2)}) %collective-permute-start.5) | collective-permute-done | bytes 36896 | tf_op jit(solution)/shard_map/ppermute | solution.py:13
  18.2 1.6 %collective-permute-start.6 = (bf16[48,1536]{1,0:T(8,128)(2,1)S(1)}, bf16[48,1536]{1,0:T(8,128)(2,1)S(1)}, u32[]{:S(2)}, u32[]{:S(2)}) collective-permute-start(bf16[48,1536]{1,0:T(8,128)(2,1)S(1)} %pad_maximum_fusion), channel_id=1, source_target_pairs={{0,4},{4,0},{8,12},{12,8},{16,20},{20,16},{24,28},{28,24},{1,5},{5... | collective-permute-start | bytes 442376 | tf_op jit(solution)/shard_map/ppermute | solution.py:13
  19.7 3.7 %collective-permute-done.6 = bf16[48,1536]{1,0:T(8,128)(2,1)S(1)} collective-permute-done((bf16[48,1536]{1,0:T(8,128)(2,1)S(1)}, bf16[48,1536]{1,0:T(8,128)(2,1)S(1)}, u32[]{:S(2)}, u32[]{:S(2)}) %collective-permute-start.6) | collective-permute-done | bytes 147488 | tf_op jit(solution)/shard_map/ppermute | solution.py:13
  23.4 0.0 slice-start
  23.4 0.1 broadcast_select_fusion.1
  23.5 0.0 slice-start.1
  23.5 0.0 slice-start.2
  23.5 5.6 %fusion.13 = f32[96,3072]{1,0:T(8,128)S(1)} fusion(bf16[1536,3072]{1,0:T(8,128)(2,1)} %param.12, bf16[48,1536]{1,0:T(8,128)(2,1)S(1)} %get-tuple-element.10, bf16[48,1536]{1,0:T(8,128)(2,1)S(1)} %get-tuple-element.9), kind=kOutput, calls=%fused_computation.16 | convolution fusion | flops 906559488 | bytes 10911744 | tf_op jit(solution)/shard_map/dot_general | solution.py:42
  29.1 0.1 collective-permute-start.7
  29.1 1.6 %collective-permute-done.7 = bf16[48,3072]{1,0:T(8,128)(2,1)S(1)} collective-permute-done((bf16[48,3072]{1,0:T(8,128)(2,1)S(1)}, bf16[48,3072]{1,0:T(8,128)(2,1)S(1)}, u32[]{:S(2)}, u32[]{:S(2)}) %collective-permute-start.7) | collective-permute-done | bytes 294944 | tf_op jit(solution)/shard_map/ppermute | solution.py:13
  30.7 0.1 fusion.12
  30.8 0.6 %collective-permute-start.8 = (bf16[48,3072]{1,0:T(8,128)(2,1)S(1)}, bf16[48,3072]{1,0:T(8,128)(2,1)S(1)}, u32[]{:S(2)}, u32[]{:S(2)}) collective-permute-start(bf16[48,3072]{1,0:T(8,128)(2,1)S(1)} %fusion.12), channel_id=1, source_target_pairs={{0,2},{1,3},{2,0},{3,1},{4,6},{5,7},{6,4},{7,5},{8,10},{9,11},{10,... | collective-permute-start | bytes 884744 | tf_op jit(solution)/shard_map/ppermute | solution.py:13
  31.4 8.5 %collective-permute-done.8 = bf16[48,3072]{1,0:T(8,128)(2,1)S(1)} collective-permute-done((bf16[48,3072]{1,0:T(8,128)(2,1)S(1)}, bf16[48,3072]{1,0:T(8,128)(2,1)S(1)}, u32[]{:S(2)}, u32[]{:S(2)}) %collective-permute-start.8) | collective-permute-done | bytes 294944 | tf_op jit(solution)/shard_map/ppermute | solution.py:13
  39.9 0.0 copy-done
  39.9 0.3 fusion.7
  40.2 0.0 copy-start.2
  40.2 0.0 copy-start.1
  40.2 0.1 collective-permute-start.9
  40.3 1.6 %collective-permute-done.9 = bf16[48,3072]{1,0:T(8,128)(2,1)S(1)} collective-permute-done((bf16[48,3072]{1,0:T(8,128)(2,1)S(1)}, bf16[48,3072]{1,0:T(8,128)(2,1)S(1)}, u32[]{:S(2)}, u32[]{:S(2)}) %collective-permute-start.9) | collective-permute-done | bytes 294944 | tf_op jit(solution)/shard_map/ppermute | solution.py:13
  41.9 0.0 slice-done
  41.9 0.0 slice-done.1
  41.9 0.0 slice-done.2
  41.9 1.6 %fusion.8 = f32[96,1536]{1,0:T(8,128)S(1)} fusion(bf16[3072,1536]{1,0:T(8,128)(2,1)S(1)} %bitcast.17, bf16[48,3072]{1,0:T(8,128)(2,1)S(1)} %collective-permute-done.9, bf16[48,3072]{1,0:T(8,128)(2,1)S(1)} %fusion.7), kind=kOutput, calls=%fused_computation.11 | convolution fusion | flops 907149312 | bytes 10616832 | tf_op jit(solution)/shard_map/dot_general | solution.py:51
  43.6 1.6 %collective-permute-start.10 = (bf16[48,1536]{1,0:T(8,128)(2,1)S(1)}, bf16[48,1536]{1,0:T(8,128)(2,1)S(1)}, u32[]{:S(2)}, u32[]{:S(2)}) collective-permute-start(bf16[48,1536]{1,0:T(8,128)(2,1)S(1)} %select_convert_fusion), channel_id=1, source_target_pairs={{0,4},{4,0},{8,12},{12,8},{16,20},{20,16},{24,28},{28,24},{1,5},{5... | collective-permute-start | bytes 442376 | tf_op jit(solution)/shard_map/ppermute | solution.py:13
  45.8 3.7 %collective-permute-done.10 = bf16[48,1536]{1,0:T(8,128)(2,1)S(1)} collective-permute-done((bf16[48,1536]{1,0:T(8,128)(2,1)S(1)}, bf16[48,1536]{1,0:T(8,128)(2,1)S(1)}, u32[]{:S(2)}, u32[]{:S(2)}) %collective-permute-start.10) | collective-permute-done | bytes 147488 | tf_op jit(solution)/shard_map/ppermute | solution.py:13
  49.6 0.1 collective-permute-start.11
  49.7 1.6 %collective-permute-start.12 = (bf16[12,1536]{1,0:T(8,128)(2,1)S(1)}, bf16[12,1536]{1,0:T(8,128)(2,1)S(1)}, u32[]{:S(2)}, u32[]{:S(2)}) collective-permute-start(bf16[12,1536]{1,0:T(8,128)(2,1)S(1)} %get-tuple-element.13), channel_id=1, source_target_pairs={{0,16},{4,20},{8,24},{12,28},{16,0},{20,4},{24,8},{28,12},{1,17},{... | collective-permute-start | bytes 110600 | tf_op jit(solution)/shard_map/ppermute | solution.py:13
  51.3 2.8 %collective-permute-start.13 = (bf16[12,1536]{1,0:T(8,128)(2,1)S(1)}, bf16[12,1536]{1,0:T(8,128)(2,1)S(1)}, u32[]{:S(2)}, u32[]{:S(2)}) collective-permute-start(bf16[12,1536]{1,0:T(8,128)(2,1)S(1)} %get-tuple-element.12), channel_id=1, source_target_pairs={{0,24},{4,28},{8,16},{12,20},{16,8},{20,12},{24,0},{28,4},{1,25},{... | collective-permute-start | bytes 110600 | tf_op jit(solution)/shard_map/ppermute | solution.py:13
  54.0 0.0 copy-done.2
  54.0 0.0 collective-permute-done.11
  54.1 1.4 %collective-permute-done.12 = bf16[12,1536]{1,0:T(8,128)(2,1)S(1)} collective-permute-done((bf16[12,1536]{1,0:T(8,128)(2,1)S(1)}, bf16[12,1536]{1,0:T(8,128)(2,1)S(1)}, u32[]{:S(2)}, u32[]{:S(2)}) %collective-permute-start.12) | collective-permute-done | bytes 36896 | tf_op jit(solution)/shard_map/ppermute | solution.py:13
  55.4 1.7 %collective-permute-done.13 = bf16[12,1536]{1,0:T(8,128)(2,1)S(1)} collective-permute-done((bf16[12,1536]{1,0:T(8,128)(2,1)S(1)}, bf16[12,1536]{1,0:T(8,128)(2,1)S(1)}, u32[]{:S(2)}, u32[]{:S(2)}) %collective-permute-start.13) | collective-permute-done | bytes 36896 | tf_op jit(solution)/shard_map/ppermute | solution.py:13
  57.2 0.0 copy-done.1
  57.2 0.7 %fusion.25 = bf16[12,1536]{1,0:T(8,128)(2,1)} fusion(f32[48,1536]{1,0:T(8,128)S(1)} %get-tuple-element.8, bf16[12,1536]{1,0:T(8,128)(2,1)S(1)} %collective-permute-done.13, bf16[12,1536]{1,0:T(8,128)(2,1)S(1)} %collective-permute-done.12, bf16[12,1536]{1,0:T(8,128)(2,1)S(1)} %collective-permute-done.11, f32[1536]{0:T(1024)S(1)} %copy-done.1, ...), kind=kLoop, calls=%fused_computation.37 | loop fusion | flops 165888 | bytes 227376 | tf_op jit(solution)/shard_map/convert_element_type | solution.py:66
  (11 shorter events, 0.2 us)
Async XLA Ops:
  0.0 39.9 %copy-start = (f32[3072]{0:T(1024)S(1)}, f32[3072]{0:T(1024)}, u32[]{:S(2)}) copy-start(f32[3072]{0:T(1024)} %param.13) | copy-start | bytes 36868
  1.0 3.2 %collective-permute-start = (f32[2,12]{1,0:T(2,128)S(1)}, f32[2,12]{1,0:T(2,128)S(1)}, u32[]{:S(2)}, u32[]{:S(2)}) collective-permute-start(f32[2,12]{1,0:T(2,128)S(1)} %pad_maximum_fusion.1), channel_id=1, source_target_pairs={{0,1},{1,0},{2,3},{3,2},{4,5},{5,4},{6,7},{7,6},{8,9},{9,8},{10,11... | collective-permute-start | bytes 296 | tf_op jit(solution)/shard_map/ppermute | solution.py:13
  1.5 4.1 %collective-permute-start.1 = (f32[2,12]{1,0:T(2,128)S(1)}, f32[2,12]{1,0:T(2,128)S(1)}, u32[]{:S(2)}, u32[]{:S(2)}) collective-permute-start(f32[2,12]{1,0:T(2,128)S(1)} %pad_maximum_fusion.1), channel_id=1, source_target_pairs={{0,2},{1,3},{2,0},{3,1},{4,6},{5,7},{6,4},{7,5},{8,10},{9,11},{10,... | collective-permute-start | bytes 296 | tf_op jit(solution)/shard_map/ppermute | solution.py:13
  4.1 3.0 %collective-permute-start.2 = (f32[2,12]{1,0:T(2,128)S(1)}, f32[2,12]{1,0:T(2,128)S(1)}, u32[]{:S(2)}, u32[]{:S(2)}) collective-permute-start(f32[2,12]{1,0:T(2,128)S(1)} %pad_maximum_fusion.1), channel_id=1, source_target_pairs={{0,3},{1,2},{2,1},{3,0},{4,7},{5,6},{6,5},{7,4},{8,11},{9,10},{10,... | collective-permute-start | bytes 296 | tf_op jit(solution)/shard_map/ppermute | solution.py:13
  8.0 4.5 %collective-permute-start.3 = (bf16[12,1536]{1,0:T(8,128)(2,1)S(1)}, bf16[12,1536]{1,0:T(8,128)(2,1)S(1)}, u32[]{:S(2)}, u32[]{:S(2)}) collective-permute-start(bf16[12,1536]{1,0:T(8,128)(2,1)S(1)} %fusion.20), channel_id=1, source_target_pairs={{0,8},{4,12},{8,0},{12,4},{16,24},{20,28},{24,16},{28,20},{1,9},{5... | collective-permute-start | bytes 110600 | tf_op jit(solution)/shard_map/ppermute | solution.py:13
  9.6 5.9 %collective-permute-start.4 = (bf16[12,1536]{1,0:T(8,128)(2,1)S(1)}, bf16[12,1536]{1,0:T(8,128)(2,1)S(1)}, u32[]{:S(2)}, u32[]{:S(2)}) collective-permute-start(bf16[12,1536]{1,0:T(8,128)(2,1)S(1)} %fusion.20), channel_id=1, source_target_pairs={{0,16},{4,20},{8,24},{12,28},{16,0},{20,4},{24,8},{28,12},{1,17},{... | collective-permute-start | bytes 110600 | tf_op jit(solution)/shard_map/ppermute | solution.py:13
  12.2 5.9 %collective-permute-start.5 = (bf16[12,1536]{1,0:T(8,128)(2,1)S(1)}, bf16[12,1536]{1,0:T(8,128)(2,1)S(1)}, u32[]{:S(2)}, u32[]{:S(2)}) collective-permute-start(bf16[12,1536]{1,0:T(8,128)(2,1)S(1)} %fusion.20), channel_id=1, source_target_pairs={{0,24},{4,28},{8,16},{12,20},{16,8},{20,12},{24,0},{28,4},{1,25},{... | collective-permute-start | bytes 110600 | tf_op jit(solution)/shard_map/ppermute | solution.py:13
  18.2 5.2 %collective-permute-start.6 = (bf16[48,1536]{1,0:T(8,128)(2,1)S(1)}, bf16[48,1536]{1,0:T(8,128)(2,1)S(1)}, u32[]{:S(2)}, u32[]{:S(2)}) collective-permute-start(bf16[48,1536]{1,0:T(8,128)(2,1)S(1)} %pad_maximum_fusion), channel_id=1, source_target_pairs={{0,4},{4,0},{8,12},{12,8},{16,20},{20,16},{24,28},{28,24},{1,5},{5... | collective-permute-start | bytes 442376 | tf_op jit(solution)/shard_map/ppermute | solution.py:13
  23.4 18.5 %slice-start = ((s8[9437184]{0:T(1024)(128)(4,1)}), s8[4194304]{0:T(1024)(128)(4,1)S(1)}, s32[]{:S(2)}) async-start(s8[9437184]{0:T(1024)(128)(4,1)} %bitcast.16), calls=%async_computation | async-start | bytes 8388608
  23.5 18.4 %slice-start.1 = ((s8[9437184]{0:T(1024)(128)(4,1)}), s8[4194304]{0:T(1024)(128)(4,1)S(1)}, s32[]{:S(2)}) async-start(s8[9437184]{0:T(1024)(128)(4,1)} %bitcast.16), calls=%async_computation.1 | async-start | bytes 8388608
  23.5 18.4 %slice-start.2 = ((s8[9437184]{0:T(1024)(128)(4,1)}), s8[1048576]{0:T(1024)(128)(4,1)S(1)}, s32[]{:S(2)}) async-start(s8[9437184]{0:T(1024)(128)(4,1)} %bitcast.16), calls=%async_computation.2 | async-start | bytes 2097152
  29.1 1.6 %collective-permute-start.7 = (bf16[48,3072]{1,0:T(8,128)(2,1)S(1)}, bf16[48,3072]{1,0:T(8,128)(2,1)S(1)}, u32[]{:S(2)}, u32[]{:S(2)}) collective-permute-start(bf16[48,3072]{1,0:T(8,128)(2,1)S(1)} %slice.80), channel_id=1, source_target_pairs={{0,1},{1,0},{2,3},{3,2},{4,5},{5,4},{6,7},{7,6},{8,9},{9,8},{10,11... | collective-permute-start | bytes 884744 | tf_op jit(solution)/shard_map/ppermute | solution.py:13
  30.8 9.1 %collective-permute-start.8 = (bf16[48,3072]{1,0:T(8,128)(2,1)S(1)}, bf16[48,3072]{1,0:T(8,128)(2,1)S(1)}, u32[]{:S(2)}, u32[]{:S(2)}) collective-permute-start(bf16[48,3072]{1,0:T(8,128)(2,1)S(1)} %fusion.12), channel_id=1, source_target_pairs={{0,2},{1,3},{2,0},{3,1},{4,6},{5,7},{6,4},{7,5},{8,10},{9,11},{10,... | collective-permute-start | bytes 884744 | tf_op jit(solution)/shard_map/ppermute | solution.py:13
  40.2 13.8 %copy-start.2 = (s32[12]{0:T(128)S(1)}, s32[12]{0:T(128)}, u32[]{:S(2)}) copy-start(s32[12]{0:T(128)} %param.10) | copy-start | bytes 148
  40.2 17.0 %copy-start.1 = (f32[1536]{0:T(1024)S(1)}, f32[1536]{0:T(1024)}, u32[]{:S(2)}) copy-start(f32[1536]{0:T(1024)} %param.15) | copy-start | bytes 18436
  40.2 1.6 %collective-permute-start.9 = (bf16[48,3072]{1,0:T(8,128)(2,1)S(1)}, bf16[48,3072]{1,0:T(8,128)(2,1)S(1)}, u32[]{:S(2)}, u32[]{:S(2)}) collective-permute-start(bf16[48,3072]{1,0:T(8,128)(2,1)S(1)} %fusion.7), channel_id=1, source_target_pairs={{0,1},{1,0},{2,3},{3,2},{4,5},{5,4},{6,7},{7,6},{8,9},{9,8},{10,11... | collective-permute-start | bytes 884744 | tf_op jit(solution)/shard_map/ppermute | solution.py:13
  43.6 5.9 %collective-permute-start.10 = (bf16[48,1536]{1,0:T(8,128)(2,1)S(1)}, bf16[48,1536]{1,0:T(8,128)(2,1)S(1)}, u32[]{:S(2)}, u32[]{:S(2)}) collective-permute-start(bf16[48,1536]{1,0:T(8,128)(2,1)S(1)} %select_convert_fusion), channel_id=1, source_target_pairs={{0,4},{4,0},{8,12},{12,8},{16,20},{20,16},{24,28},{28,24},{1,5},{5... | collective-permute-start | bytes 442376 | tf_op jit(solution)/shard_map/ppermute | solution.py:13
  49.6 4.5 %collective-permute-start.11 = (bf16[12,1536]{1,0:T(8,128)(2,1)S(1)}, bf16[12,1536]{1,0:T(8,128)(2,1)S(1)}, u32[]{:S(2)}, u32[]{:S(2)}) collective-permute-start(bf16[12,1536]{1,0:T(8,128)(2,1)S(1)} %get-tuple-element.11), channel_id=1, source_target_pairs={{0,8},{4,12},{8,0},{12,4},{16,24},{20,28},{24,16},{28,20},{1,9},{5... | collective-permute-start | bytes 110600 | tf_op jit(solution)/shard_map/ppermute | solution.py:13
  49.7 5.8 %collective-permute-start.12 = (bf16[12,1536]{1,0:T(8,128)(2,1)S(1)}, bf16[12,1536]{1,0:T(8,128)(2,1)S(1)}, u32[]{:S(2)}, u32[]{:S(2)}) collective-permute-start(bf16[12,1536]{1,0:T(8,128)(2,1)S(1)} %get-tuple-element.13), channel_id=1, source_target_pairs={{0,16},{4,20},{8,24},{12,28},{16,0},{20,4},{24,8},{28,12},{1,17},{... | collective-permute-start | bytes 110600 | tf_op jit(solution)/shard_map/ppermute | solution.py:13
  51.3 5.9 %collective-permute-start.13 = (bf16[12,1536]{1,0:T(8,128)(2,1)S(1)}, bf16[12,1536]{1,0:T(8,128)(2,1)S(1)}, u32[]{:S(2)}, u32[]{:S(2)}) collective-permute-start(bf16[12,1536]{1,0:T(8,128)(2,1)S(1)} %get-tuple-element.12), channel_id=1, source_target_pairs={{0,24},{4,28},{8,16},{12,20},{16,8},{20,12},{24,0},{28,4},{1,25},{... | collective-permute-start | bytes 110600 | tf_op jit(solution)/shard_map/ppermute | solution.py:13

commit v2 on v1

v2 whole, which is shorter than its diff:
```python
import jax
import jax.numpy as jnp
from jax import lax
from jax.experimental import pallas as pl
from jax.experimental.pallas import tpu as pltpu
from jax.sharding import PartitionSpec as P

FRAME_TOK = 4
LANES = 128
MIB = 2**20

epsilon = 1e-06

in_vmem = pl.BlockSpec(memory_space=pltpu.VMEM)


def swap(block, axis, mask):
    size = lax.axis_size(axis)
    return lax.ppermute(block, axis, [(i, i ^ mask) for i in range(size)])


def is_first_core():
    return lax.rem(lax.axis_index("feat"), 2) == 0


def tile_of(width):
    return next((t for t in (512, 384, 256, 128) if width % t == 0), width)


def call(kernel, outs, in_specs, scratch=(), flops=0, limit=4):
    outs = [jax.ShapeDtypeStruct(shape, dtype) for shape, dtype in outs]
    return pl.pallas_call(
        kernel,
        out_shape=outs,
        in_specs=in_specs,
        out_specs=[in_vmem] * len(outs),
        scratch_shapes=list(scratch),
        compiler_params=pltpu.CompilerParams(vmem_limit_bytes=limit * MIB),
        cost_estimate=pl.CostEstimate(
            flops=flops, bytes_accessed=sum(o.size * 4 for o in outs), transcendentals=0
        ),
    )


def pieces(column):
    high = column.astype(jnp.bfloat16).astype(jnp.float32)
    middle = (column - high).astype(jnp.bfloat16).astype(jnp.float32)
    return high, middle, column - high - middle


def pack(sums, squares):
    lane = lax.broadcasted_iota(jnp.int32, (sums.shape[0], LANES), 1)
    packed = jnp.zeros((sums.shape[0], LANES), jnp.float32)
    for at, piece in enumerate(pieces(sums) + pieces(squares)):
        packed = jnp.where(lane == at, piece, packed)
    return packed.astype(jnp.bfloat16)


def unpack(packed):
    packed = packed.astype(jnp.float32)
    column = [packed[:, at:at + 1] for at in range(6)]
    return column[0] + column[1] + column[2], column[3] + column[4] + column[5]


def gain_kernel(gain_ref, weight_ref, row_ref):
    width = weight_ref.shape[1]
    tile = tile_of(width)
    gain = gain_ref[...]
    high = gain.astype(jnp.bfloat16).astype(jnp.float32)
    row = lax.broadcasted_iota(jnp.int32, (16, gain.shape[1]), 0)
    rows = jnp.where(row == 0, high, jnp.where(row == 1, gain - high, 0.0)).astype(jnp.bfloat16)
    for at in range(0, width, tile):
        product = jnp.dot(rows, weight_ref[:, at:at + tile], preferred_element_type=jnp.float32)
        row_ref[:, at:at + tile] = product[0:1] + product[1:2]


def up_kernel(near_ref, far_ref, gain_ref, weight_ref, kept_ref, given_ref, own_ref, rows_ref):
    half, block_width = near_ref.shape
    width = weight_ref.shape[1]
    first = is_first_core()
    near, far = near_ref[...].astype(jnp.float32), far_ref[...].astype(jnp.float32)
    for at, values in enumerate((jnp.where(first, near, far), jnp.where(first, far, near))):
        sums = jnp.sum(values, axis=1, keepdims=True)
        squares = jnp.sum(values * values, axis=1, keepdims=True)
        centred = (values - sums / block_width) * gain_ref[...]
        rows_ref[at * half:(at + 1) * half] = centred.astype(jnp.bfloat16)
        packed = pack(sums, squares)
        if at == 0:
            own_ref[...] = packed
        else:
            given_ref[:, width:] = packed
    tile = tile_of(width)
    for at in range(0, width, tile):
        product = jnp.dot(
            rows_ref[...], weight_ref[:, at:at + tile], preferred_element_type=jnp.float32
        )
        kept_ref[:, at:at + tile] = product[:half]
        given_ref[:, at:at + tile] = product[half:].astype(jnp.bfloat16)


def pair_kernel(block_width, kept_ref, own_ref, other_ref, gain_ref, other_gain_ref, sum_ref, sent_ref):
    width = kept_ref.shape[1]
    sums, squares = unpack(own_ref[...])
    other_sums, other_squares = unpack(other_ref[:, width:])
    shift = (sums - other_sums) / (2 * block_width)
    tile = tile_of(width)
    for at in range(0, width, tile):
        cut = slice(at, at + tile)
        gains = gain_ref[:, cut] - other_gain_ref[:, cut]
        total = kept_ref[:, cut] + other_ref[:, cut].astype(jnp.float32) + shift * gains
        sum_ref[:, cut] = total
        sent_ref[:, cut] = total.astype(jnp.bfloat16)
    sent_ref[:, width:] = pack(sums + other_sums, squares + other_squares)


def gelu_kernel(block_width, full_width, peers, bias_ref, sum_ref, sent_ref, gain_ref, *refs):
    others, gains, out_ref = refs[:peers], refs[peers:2 * peers], refs[2 * peers]
    width = sum_ref.shape[1]
    stats = [unpack(ref[:, width:]) for ref in (sent_ref,) + others]
    row_mean = sum(s[0] for s in stats) / full_width
    spread = sum(s[1] for s in stats) / full_width - row_mean * row_mean
    scale = lax.rsqrt(spread + epsilon)
    shifts = [s[0] / (2 * block_width) - row_mean for s in stats]
    tile = tile_of(width)
    for at in range(0, width, tile):
        cut = slice(at, at + tile)
        total = sum_ref[:, cut] + shifts[0] * gain_ref[:, cut]
        for other, gain, shift in zip(others, gains, shifts[1:]):
            total = total + other[:, cut].astype(jnp.float32) + shift * gain[:, cut]
        active = jax.nn.gelu(total * scale + bias_ref[:, cut], approximate=True)
        out_ref[:, cut] = active.astype(jnp.bfloat16)


def down_kernel(kept_ref, given_ref, weight_ref, near_ref, far_ref, rows_ref):
    half = kept_ref.shape[0]
    rows_ref[:half] = kept_ref[...]
    rows_ref[half:] = given_ref[...]
    first = is_first_core()
    width = weight_ref.shape[1]
    tile = tile_of(width)
    for at in range(0, width, tile):
        product = jnp.dot(
            rows_ref[...], weight_ref[:, at:at + tile], preferred_element_type=jnp.float32
        )
        kept, given = product[:half], product[half:]
        near_ref[:, at:at + tile] = jnp.where(first, kept, given)
        far_ref[:, at:at + tile] = jnp.where(first, given, kept).astype(jnp.bfloat16)


def per_device(
    patches, frame_counts, patch_mask, norm_gain, up_weight, up_bias, down_weight, down_bias
):
    tok_rows, block_width = patches.shape
    hidden_width = up_weight.shape[1]
    tok_size = lax.axis_size("tok")
    feat_size = lax.axis_size("feat")
    full_width = block_width * feat_size
    norm_gain = norm_gain[None, :]
    f32, bf16 = jnp.float32, jnp.bfloat16

    masks = range(2, tok_size, 2)
    (gain_row,) = call(
        gain_kernel, [((1, hidden_width), f32)], [in_vmem] * 2, flops=32 * up_weight.size
    )(norm_gain, up_weight)
    near = jnp.concatenate([patches] + [swap(patches, "tok", mask) for mask in masks])
    near, gain_row = lax.optimization_barrier((near, gain_row))
    far = swap(near, "tok", 1)
    half = near.shape[0]
    other_gain = swap(gain_row, "feat", 1)
    pair_gain = gain_row + other_gain
    peers = range(2, feat_size, 2)
    peer_gains = [swap(pair_gain, "feat", mask) for mask in peers]

    kept, given, own = call(
        up_kernel,
        [((half, hidden_width), f32), ((half, hidden_width + LANES), bf16), ((half, LANES), bf16)],
        [in_vmem] * 4,
        [pltpu.VMEM((2 * half, block_width), bf16)],
        flops=4 * half * up_weight.size,
        limit=4,
    )(near, far, norm_gain, up_weight)
    other = swap(given, "feat", 1)
    pair_sum, sent = call(
        lambda *refs: pair_kernel(block_width, *refs),
        [((half, hidden_width), f32), ((half, hidden_width + LANES), bf16)],
        [in_vmem] * 5,
    )(kept, own, other, gain_row, other_gain)
    others = [swap(sent, "feat", mask) for mask in peers]
    (active,) = call(
        lambda *refs: gelu_kernel(block_width, full_width, len(peers), *refs),
        [((half, hidden_width), bf16)],
        [in_vmem] * (4 + 2 * len(peers)),
        limit=4,
    )(up_bias[None, :], pair_sum, sent, pair_gain, *others, *peer_gains)
    near_sum, far_sum = call(
        down_kernel,
        [((half, block_width), f32), ((half, block_width), bf16)],
        [in_vmem] * 3,
        [pltpu.VMEM((2 * half, hidden_width), bf16)],
        flops=4 * half * down_weight.size,
        limit=4,
    )(active, swap(active, "feat", 1), down_weight)

    near_sum = near_sum + swap(far_sum, "tok", 1)
    blocks = near_sum.reshape(tok_size // 2, tok_rows, block_width)
    summed = blocks[0]
    sent = blocks.astype(bf16)
    for part in [swap(sent[mask // 2], "tok", mask) for mask in masks]:
        summed = summed + part

    positions = jnp.arange(tok_rows, dtype=jnp.int32)
    valid_rows = ((positions // FRAME_TOK < frame_counts[0]) & (patch_mask == 1)).astype(f32)
    return (valid_rows[:, None] * (summed + down_bias[None, :])).astype(bf16)


def solution(mesh):
    in_specs = (
        P("tok", "feat"),
        P("tok"),
        P("tok"),
        P("feat"),
        P("feat", "tok"),
        P("tok"),
        P("tok", "feat"),
        P("feat"),
    )
    out_specs = P("tok", "feat")
    return jax.shard_map(
        per_device, mesh=mesh, in_specs=in_specs, out_specs=out_specs, check_vma=False
    )
```

time: 58.1 us -> 52.5 us (0.904)
  waiting for transfers between devices: 30.7 us -> 23.5 us
  matrix products: 7.16 us -> 0 us
  Pallas kernels: 0 us -> 5.48 us
  local copies, waits for them, and re-layouts: 0.1 us -> 4.43 us
  other arithmetic: 3.13 us -> 2.29 us
    ppermute x14 -> x13, waiting for transfers between devices: 30.7 us -> 23.5 us  [swap(): return lax.ppermute(block, axis, [(i, i ^ mask) for i in range(size)])]
    dot_general x2 -> x0, matrix products: 7.16 us -> none  [the longest x1 5.55 us: per_device(): jnp.dot(jnp.concatenate([kept, given]), up_weight, preferred_element_type...]
    pallas_call x0 -> x5, Pallas kernels: none -> 5.48 us  [the longest x1 1.78 us: per_device(): call(up_kernel, [((half, hidden_width), f32), ((half, hidden_width + LANE...]
    unnamed x12, local copies, waits for them, and re-layouts: 0.03 us -> 3.7 us
    concatenate x1, other arithmetic: 0.05 us -> 1.54 us  [per_device(): jnp.concatenate([patches] + [swap(patches, 'tok', mask) for mask in masks])]
    convert_element_type x7 -> x3, other arithmetic: 2.02 us -> 0.73 us  [the longest x1 0.69 us: per_device(): return (valid_rows[:, None] * (summed + down_bias[None, :])).astype(bf16)]
    reduce_sum x1 -> x0, other arithmetic: 0.94 us -> none  [per_device(): jnp.sum(values, axis=1)]
    broadcast_in_dim x0 -> x1, local copies, waits for them, and re-layouts: none -> 0.7 us  [per_device(): norm_gain = norm_gain[None, :]]
  transfers between devices with their start and end apart: 14 -> 13, of which waited for: 11 -> 8; matrix products, arithmetic and copies ran while one was open for 0% -> 1% of each run, Pallas kernels for 0% -> 3%
where the time goes in v2:
time: 52.5 us; the launch traced here: 52.2 us
  waiting for transfers between devices  23.5 us (45%)
  starting transfers between devices  15.8 us (30%)
  Pallas kernels  5.48 us (10%)
  local copies, waits for them, and re-layouts  4.43 us (8%)
  other arithmetic  2.29 us (4%)
  between operations  0.75 us (1%)
    ppermute x13, waiting for transfers between devices, swap(): return lax.ppermute(block, axis, [(i, i ^ mask) for i in range(size)])  23.5 us
    ppermute x13, starting transfers between devices, swap(): return lax.ppermute(block, axis, [(i, i ^ mask) for i in range(size)])  15.8 us
    unnamed x12, local copies, waits for them, and re-layouts  3.7 us
    pallas_call x1, Pallas kernels, per_device(): call(up_kernel, [((half, hidden_width), f32), ((half, hidden_width + LANE...  1.78 us
    pallas_call x1, Pallas kernels, per_device(): call(down_kernel, [((half, block_width), f32), ((half, block_width), bf16...  1.62 us
    concatenate x1, other arithmetic, per_device(): jnp.concatenate([patches] + [swap(patches, 'tok', mask) for mask in masks])  1.54 us
    pallas_call x1, Pallas kernels, per_device(): call(gain_kernel, [((1, hidden_width), f32)], [in_vmem] * 2, flops=32 * u...  1.33 us
  transfers between devices with their start and end apart: 13, of which 8 were waited for; matrix products, arithmetic and copies ran while one was open for 1% of the time, Pallas kernels for 3%

profile of v2, /device:TPU:0, one launch (start us, length us, event | category | flops | bytes accessed | tf_op | source)
XLA Modules:
  0.0 52.2 jit_solution(2587287893239994134)
XLA Ops:
  0.0 3.0 %collective-permute-start = (bf16[12,1536]{1,0:T(8,128)(2,1)}, bf16[12,1536]{1,0:T(8,128)(2,1)S(1)}, u32[]{:S(2)}, u32[]{:S(2)}) collective-permute-start(bf16[12,1536]{1,0:T(8,128)(2,1)} %param.8), channel_id=1, source_target_pairs={{0,8},{4,12},{8,0},{12,4},{16,24},{20,28},{24,16},{28,20},{1,9},{5... | collective-permute-start | bytes 110600 | tf_op jit(solution)/shard_map/ppermute | solution.py:19
  3.0 2.6 %collective-permute-start.1 = (bf16[12,1536]{1,0:T(8,128)(2,1)}, bf16[12,1536]{1,0:T(8,128)(2,1)S(1)}, u32[]{:S(2)}, u32[]{:S(2)}) collective-permute-start(bf16[12,1536]{1,0:T(8,128)(2,1)} %param.8), channel_id=1, source_target_pairs={{0,16},{4,20},{8,24},{12,28},{16,0},{20,4},{24,8},{28,12},{1,17},{... | collective-permute-start | bytes 110600 | tf_op jit(solution)/shard_map/ppermute | solution.py:19
  5.6 0.0 collective-permute-start.2
  5.6 0.7 %broadcast_in_dim.9.gain_ref = f32[1,1536]{1,0:T(1,128)S(1)} reshape(f32[1536]{0:T(1024)} %param.11) | data formatting | bytes 12288 | tf_op jit(solution)/shard_map/broadcast_in_dim | solution.py:158
  6.3 0.0 copy-start
  6.3 3.7 %copy-done = bf16[1536,3072]{1,0:T(8,128)(2,1)S(1)} copy-done((bf16[1536,3072]{1,0:T(8,128)(2,1)S(1)}, bf16[1536,3072]{1,0:T(8,128)(2,1)}, u32[]{:S(2)}) %copy-start) | copy-done | bytes 9437208
  10.0 0.0 copy-start.1
  10.0 0.0 copy-start.3
  10.0 0.0 copy-start.2
  10.0 1.3 %shard_map.82.refs_3_ = f32[1,3072]{1,0:T(1,128)S(1)} custom-call(f32[1,1536]{1,0:T(1,128)S(1)} %broadcast_in_dim.9.gain_ref, bf16[1536,3072]{1,0:T(8,128)(2,1)S(1)} %copy-done), custom_call_target="tpu_custom_call" | custom-call | flops 150994944 | bytes 12288 | tf_op jit(solution)/shard_map/pallas_call | solution.py:162
  11.3 0.0 collective-permute-done
  11.3 0.0 collective-permute-done.1
  11.4 0.4 collective-permute-done.2
  11.7 1.5 %pad_maximum_fusion.near_ref = bf16[48,1536]{1,0:T(8,128)(2,1)S(1)} fusion(bf16[12,1536]{1,0:T(8,128)(2,1)S(1)} %collective-permute-done.2, bf16[12,1536]{1,0:T(8,128)(2,1)S(1)} %collective-permute-done.1, bf16[12,1536]{1,0:T(8,128)(2,1)S(1)} %collective-permute-done, bf16[12,1536]{1,0:T(8,128)(2,1)} %param.8), kind=kLoop, calls=%fused_computation.1 | loop fusion | flops 589824 | bytes 294912 | tf_op jit(solution)/shard_map/concatenate | solution.py:165
  13.3 0.0 copy-start.5
  13.3 0.0 copy-start.4
  13.3 1.5 %collective-permute-start.3 = (bf16[48,1536]{1,0:T(8,128)(2,1)S(1)}, bf16[48,1536]{1,0:T(8,128)(2,1)S(1)}, u32[]{:S(2)}, u32[]{:S(2)}) collective-permute-start(bf16[48,1536]{1,0:T(8,128)(2,1)S(1)} %pad_maximum_fusion.near_ref), channel_id=1, source_target_pairs={{0,4},{4,0},{8,12},{12,8},{16,20},{20,16},{24,28},{28,24},{1,5},{5... | collective-permute-start | bytes 442376 | tf_op jit(solution)/shard_map/ppermute | solution.py:19
  14.7 3.7 %collective-permute-done.3.far_ref = bf16[48,1536]{1,0:T(8,128)(2,1)S(1)} collective-permute-done((bf16[48,1536]{1,0:T(8,128)(2,1)S(1)}, bf16[48,1536]{1,0:T(8,128)(2,1)S(1)}, u32[]{:S(2)}, u32[]{:S(2)}) %collective-permute-start.3) | collective-permute-done | bytes 147488 | tf_op jit(solution)/shard_map/ppermute | solution.py:19
  18.5 0.0 copy-done.1
  18.5 1.8 %shard_map.83 = (f32[48,3072]{1,0:T(8,128)S(1)}, bf16[48,3200]{1,0:T(8,128)(2,1)S(1)}, bf16[48,128]{1,0:T(8,128)(2,1)S(1)}) custom-call(bf16[48,1536]{1,0:T(8,128)(2,1)S(1)} %pad_maximum_fusion.near_ref, bf16[48,1536]{1,0:T(8,128)(2,1)S(1)} %collective-permute-done.3.far_ref, f32[1,1536]{1,0:T(1,128)S(1)} %broadcast_in_dim.9.gain_ref, ...), custom_call_target="tpu_custom_call" | custom-call | flops 905969664 | bytes 1228800 | tf_op jit(solution)/shard_map/pallas_call | solution.py:174
  20.3 0.1 collective-permute-start.4
  20.4 0.5 collective-permute-start.5
  20.8 1.1 %collective-permute-done.5.refs_4_ = f32[1,3072]{1,0:T(1,128)S(1)} collective-permute-done((f32[1,3072]{1,0:T(1,128)S(1)}, f32[1,3072]{1,0:T(1,128)S(1)}, u32[]{:S(2)}, u32[]{:S(2)}) %collective-permute-start.5) | collective-permute-done | bytes 12320 | tf_op jit(solution)/shard_map/ppermute | solution.py:19
  22.0 0.0 collective-permute-done.4.refs_2_
  22.0 0.2 shard_map.84
  22.2 1.5 %collective-permute-start.6 = (bf16[48,3200]{1,0:T(8,128)(2,1)S(1)}, bf16[48,3200]{1,0:T(8,128)(2,1)S(1)}, u32[]{:S(2)}, u32[]{:S(2)}) collective-permute-start(bf16[48,3200]{1,0:T(8,128)(2,1)S(1)} %get-tuple-element.20.refs_2_), channel_id=1, source_target_pairs={{0,2},{1,3},{2,0},{3,1},{4,6},{5,7},{6,4},{7,5},{8,10},{9,11},{10,... | collective-permute-start | bytes 921608 | tf_op jit(solution)/shard_map/ppermute | solution.py:19
  23.7 0.7 %collective-permute-start.7 = (f32[1,3072]{1,0:T(1,128)S(1)}, f32[1,3072]{1,0:T(1,128)S(1)}, u32[]{:S(2)}, u32[]{:S(2)}) collective-permute-start(f32[1,3072]{1,0:T(1,128)S(1)} %add.24.refs_3_), channel_id=1, source_target_pairs={{0,2},{1,3},{2,0},{3,1},{4,6},{5,7},{6,4},{7,5},{8,10},{9,11},{10,... | collective-permute-start | bytes 36872 | tf_op jit(solution)/shard_map/ppermute | solution.py:19
  24.4 7.5 %collective-permute-done.7.refs_5_ = f32[1,3072]{1,0:T(1,128)S(1)} collective-permute-done((f32[1,3072]{1,0:T(1,128)S(1)}, f32[1,3072]{1,0:T(1,128)S(1)}, u32[]{:S(2)}, u32[]{:S(2)}) %collective-permute-start.7) | collective-permute-done | bytes 12320 | tf_op jit(solution)/shard_map/ppermute | solution.py:19
  31.8 0.0 collective-permute-done.6.refs_4_
  31.8 0.0 copy-done.3
  31.8 0.5 %shard_map.85.kept_ref = bf16[48,3072]{1,0:T(8,128)(2,1)S(1)} custom-call(f32[1,3072]{1,0:T(1,128)S(1)} %bitcast.3, f32[48,3072]{1,0:T(8,128)S(1)} %get-tuple-element.19.refs_1_, bf16[48,3200]{1,0:T(8,128)(2,1)S(1)} %get-tuple-element.20.refs_2_, f32[1,3072]{1,0:T(1,128)S(1)} %add.24.refs_3_, bf16[48,3200]{1,0:T(8,128)(2,1)S(1)} %collective-permute-done.6.refs_4_, ...), custom_call_target="tpu_custom_call" | custom-call | bytes 589824 | tf_op jit(solution)/shard_map/pallas_call | solution.py:189
  32.4 0.1 collective-permute-start.8
  32.5 1.6 %collective-permute-done.8.given_ref = bf16[48,3072]{1,0:T(8,128)(2,1)S(1)} collective-permute-done((bf16[48,3072]{1,0:T(8,128)(2,1)S(1)}, bf16[48,3072]{1,0:T(8,128)(2,1)S(1)}, u32[]{:S(2)}, u32[]{:S(2)}) %collective-permute-start.8) | collective-permute-done | bytes 294944 | tf_op jit(solution)/shard_map/ppermute | solution.py:19
  34.0 0.0 copy-done.2
  34.0 1.6 %shard_map.86 = (f32[48,1536]{1,0:T(8,128)S(1)}, bf16[48,1536]{1,0:T(8,128)(2,1)S(1)}) custom-call(bf16[48,3072]{1,0:T(8,128)(2,1)S(1)} %shard_map.85.kept_ref, bf16[48,3072]{1,0:T(8,128)(2,1)S(1)} %collective-permute-done.8.given_ref, bf16[3072,1536]{1,0:T(8,128)(2,1)S(1)} %copy-done.2), custom_call_target="tpu_custom_call" | custom-call | flops 905969664 | bytes 589824 | tf_op jit(solution)/shard_map/pallas_call | solution.py:195
  35.7 1.5 %collective-permute-start.9 = (bf16[48,1536]{1,0:T(8,128)(2,1)S(1)}, bf16[48,1536]{1,0:T(8,128)(2,1)S(1)}, u32[]{:S(2)}, u32[]{:S(2)}) collective-permute-start(bf16[48,1536]{1,0:T(8,128)(2,1)S(1)} %get-tuple-element.22), channel_id=1, source_target_pairs={{0,4},{4,0},{8,12},{12,8},{16,20},{20,16},{24,28},{28,24},{1,5},{5... | collective-permute-start | bytes 442376 | tf_op jit(solution)/shard_map/ppermute | solution.py:19
  37.8 3.8 %collective-permute-done.9 = bf16[48,1536]{1,0:T(8,128)(2,1)S(1)} collective-permute-done((bf16[48,1536]{1,0:T(8,128)(2,1)S(1)}, bf16[48,1536]{1,0:T(8,128)(2,1)S(1)}, u32[]{:S(2)}, u32[]{:S(2)}) %collective-permute-start.9) | collective-permute-done | bytes 147488 | tf_op jit(solution)/shard_map/ppermute | solution.py:19
  41.7 0.5 collective-permute-start.10
  42.2 3.5 %collective-permute-start.11 = (bf16[12,1536]{1,0:T(8,128)(2,1)S(1)}, bf16[12,1536]{1,0:T(8,128)(2,1)S(1)}, u32[]{:S(2)}, u32[]{:S(2)}) collective-permute-start(bf16[12,1536]{1,0:T(8,128)(2,1)S(1)} %get-tuple-element.27), channel_id=1, source_target_pairs={{0,16},{4,20},{8,24},{12,28},{16,0},{20,4},{24,8},{28,12},{1,17},{... | collective-permute-start | bytes 110600 | tf_op jit(solution)/shard_map/ppermute | solution.py:19
  45.7 0.5 collective-permute-start.12
  46.1 0.0 copy-done.5
  46.1 0.0 collective-permute-done.10
  46.2 2.2 %collective-permute-done.11 = bf16[12,1536]{1,0:T(8,128)(2,1)S(1)} collective-permute-done((bf16[12,1536]{1,0:T(8,128)(2,1)S(1)}, bf16[12,1536]{1,0:T(8,128)(2,1)S(1)}, u32[]{:S(2)}, u32[]{:S(2)}) %collective-permute-start.11) | collective-permute-done | bytes 36896 | tf_op jit(solution)/shard_map/ppermute | solution.py:19
  48.4 3.2 %collective-permute-done.12 = bf16[12,1536]{1,0:T(8,128)(2,1)S(1)} collective-permute-done((bf16[12,1536]{1,0:T(8,128)(2,1)S(1)}, bf16[12,1536]{1,0:T(8,128)(2,1)S(1)}, u32[]{:S(2)}, u32[]{:S(2)}) %collective-permute-start.12) | collective-permute-done | bytes 36896 | tf_op jit(solution)/shard_map/ppermute | solution.py:19
  51.5 0.0 copy-done.4
  51.6 0.7 %fusion.4 = bf16[12,1536]{1,0:T(8,128)(2,1)} fusion(f32[48,1536]{1,0:T(8,128)S(1)} %get-tuple-element.24, bf16[12,1536]{1,0:T(8,128)(2,1)S(1)} %collective-permute-done.12, bf16[12,1536]{1,0:T(8,128)(2,1)S(1)} %collective-permute-done.11, bf16[12,1536]{1,0:T(8,128)(2,1)S(1)} %collective-permute-done.10, f32[1536]{0:T(1024)S(1)} %copy-done.4, ...), kind=kLoop, calls=%fused_computation.7 | loop fusion | flops 165888 | bytes 227376 | tf_op jit(solution)/shard_map/convert_element_type | solution.py:213
  (4 shorter events, 0.1 us)
Async XLA Ops:
  0.0 11.3 %collective-permute-start = (bf16[12,1536]{1,0:T(8,128)(2,1)}, bf16[12,1536]{1,0:T(8,128)(2,1)S(1)}, u32[]{:S(2)}, u32[]{:S(2)}) collective-permute-start(bf16[12,1536]{1,0:T(8,128)(2,1)} %param.8), channel_id=1, source_target_pairs={{0,8},{4,12},{8,0},{12,4},{16,24},{20,28},{24,16},{28,20},{1,9},{5... | collective-permute-start | bytes 110600 | tf_op jit(solution)/shard_map/ppermute | solution.py:19
  3.0 8.3 %collective-permute-start.1 = (bf16[12,1536]{1,0:T(8,128)(2,1)}, bf16[12,1536]{1,0:T(8,128)(2,1)S(1)}, u32[]{:S(2)}, u32[]{:S(2)}) collective-permute-start(bf16[12,1536]{1,0:T(8,128)(2,1)} %param.8), channel_id=1, source_target_pairs={{0,16},{4,20},{8,24},{12,28},{16,0},{20,4},{24,8},{28,12},{1,17},{... | collective-permute-start | bytes 110600 | tf_op jit(solution)/shard_map/ppermute | solution.py:19
  5.6 6.1 %collective-permute-start.2 = (bf16[12,1536]{1,0:T(8,128)(2,1)}, bf16[12,1536]{1,0:T(8,128)(2,1)S(1)}, u32[]{:S(2)}, u32[]{:S(2)}) collective-permute-start(bf16[12,1536]{1,0:T(8,128)(2,1)} %param.8), channel_id=1, source_target_pairs={{0,24},{4,28},{8,16},{12,20},{16,8},{20,12},{24,0},{28,4},{1,25},{... | collective-permute-start | bytes 110600 | tf_op jit(solution)/shard_map/ppermute | solution.py:19
  6.3 3.7 %copy-start = (bf16[1536,3072]{1,0:T(8,128)(2,1)S(1)}, bf16[1536,3072]{1,0:T(8,128)(2,1)}, u32[]{:S(2)}) copy-start(bf16[1536,3072]{1,0:T(8,128)(2,1)} %weight_ref.4) | copy-start | bytes 28311556
  10.0 8.5 %copy-start.1 = (bf16[1536,3072]{1,0:T(8,128)(2,1)S(1)}, bf16[1536,3072]{1,0:T(8,128)(2,1)}, u32[]{:S(2)}) copy-start(bf16[1536,3072]{1,0:T(8,128)(2,1)} %weight_ref.4) | copy-start | bytes 28311556
  10.0 21.8 %copy-start.3 = (f32[3072]{0:T(1024)S(1)}, f32[3072]{0:T(1024)}, u32[]{:S(2)}) copy-start(f32[3072]{0:T(1024)} %param.13) | copy-start | bytes 36868
  10.0 24.0 %copy-start.2 = (bf16[3072,1536]{1,0:T(8,128)(2,1)S(1)}, bf16[3072,1536]{1,0:T(8,128)(2,1)}, u32[]{:S(2)}) copy-start(bf16[3072,1536]{1,0:T(8,128)(2,1)} %weight_ref.5) | copy-start | bytes 28311556
  13.3 32.9 %copy-start.5 = (s32[12]{0:T(128)S(1)}, s32[12]{0:T(128)}, u32[]{:S(2)}) copy-start(s32[12]{0:T(128)} %param.10) | copy-start | bytes 148
  13.3 38.3 %copy-start.4 = (f32[1536]{0:T(1024)S(1)}, f32[1536]{0:T(1024)}, u32[]{:S(2)}) copy-start(f32[1536]{0:T(1024)} %param.15) | copy-start | bytes 18436
  13.3 5.2 %collective-permute-start.3 = (bf16[48,1536]{1,0:T(8,128)(2,1)S(1)}, bf16[48,1536]{1,0:T(8,128)(2,1)S(1)}, u32[]{:S(2)}, u32[]{:S(2)}) collective-permute-start(bf16[48,1536]{1,0:T(8,128)(2,1)S(1)} %pad_maximum_fusion.near_ref), channel_id=1, source_target_pairs={{0,4},{4,0},{8,12},{12,8},{16,20},{20,16},{24,28},{28,24},{1,5},{5... | collective-permute-start | bytes 442376 | tf_op jit(solution)/shard_map/ppermute | solution.py:19
  20.3 1.7 %collective-permute-start.4 = (bf16[48,3200]{1,0:T(8,128)(2,1)S(1)}, bf16[48,3200]{1,0:T(8,128)(2,1)S(1)}, u32[]{:S(2)}, u32[]{:S(2)}) collective-permute-start(bf16[48,3200]{1,0:T(8,128)(2,1)S(1)} %get-tuple-element.17), channel_id=1, source_target_pairs={{0,1},{1,0},{2,3},{3,2},{4,5},{5,4},{6,7},{7,6},{8,9},{9,8},{10,11... | collective-permute-start | bytes 921608 | tf_op jit(solution)/shard_map/ppermute | solution.py:19
  20.4 1.6 %collective-permute-start.5 = (f32[1,3072]{1,0:T(1,128)S(1)}, f32[1,3072]{1,0:T(1,128)S(1)}, u32[]{:S(2)}, u32[]{:S(2)}) collective-permute-start(f32[1,3072]{1,0:T(1,128)S(1)} %shard_map.82.refs_3_), channel_id=1, source_target_pairs={{0,1},{1,0},{2,3},{3,2},{4,5},{5,4},{6,7},{7,6},{8,9},{9,8},{10,11... | collective-permute-start | bytes 36872 | tf_op jit(solution)/shard_map/ppermute | solution.py:19
  22.2 9.6 %collective-permute-start.6 = (bf16[48,3200]{1,0:T(8,128)(2,1)S(1)}, bf16[48,3200]{1,0:T(8,128)(2,1)S(1)}, u32[]{:S(2)}, u32[]{:S(2)}) collective-permute-start(bf16[48,3200]{1,0:T(8,128)(2,1)S(1)} %get-tuple-element.20.refs_2_), channel_id=1, source_target_pairs={{0,2},{1,3},{2,0},{3,1},{4,6},{5,7},{6,4},{7,5},{8,10},{9,11},{10,... | collective-permute-start | bytes 921608 | tf_op jit(solution)/shard_map/ppermute | solution.py:19
  23.7 8.1 %collective-permute-start.7 = (f32[1,3072]{1,0:T(1,128)S(1)}, f32[1,3072]{1,0:T(1,128)S(1)}, u32[]{:S(2)}, u32[]{:S(2)}) collective-permute-start(f32[1,3072]{1,0:T(1,128)S(1)} %add.24.refs_3_), channel_id=1, source_target_pairs={{0,2},{1,3},{2,0},{3,1},{4,6},{5,7},{6,4},{7,5},{8,10},{9,11},{10,... | collective-permute-start | bytes 36872 | tf_op jit(solution)/shard_map/ppermute | solution.py:19
  32.4 1.6 %collective-permute-start.8 = (bf16[48,3072]{1,0:T(8,128)(2,1)S(1)}, bf16[48,3072]{1,0:T(8,128)(2,1)S(1)}, u32[]{:S(2)}, u32[]{:S(2)}) collective-permute-start(bf16[48,3072]{1,0:T(8,128)(2,1)S(1)} %shard_map.85.kept_ref), channel_id=1, source_target_pairs={{0,1},{1,0},{2,3},{3,2},{4,5},{5,4},{6,7},{7,6},{8,9},{9,8},{10,11... | collective-permute-start | bytes 884744 | tf_op jit(solution)/shard_map/ppermute | solution.py:19
  35.7 6.0 %collective-permute-start.9 = (bf16[48,1536]{1,0:T(8,128)(2,1)S(1)}, bf16[48,1536]{1,0:T(8,128)(2,1)S(1)}, u32[]{:S(2)}, u32[]{:S(2)}) collective-permute-start(bf16[48,1536]{1,0:T(8,128)(2,1)S(1)} %get-tuple-element.22), channel_id=1, source_target_pairs={{0,4},{4,0},{8,12},{12,8},{16,20},{20,16},{24,28},{28,24},{1,5},{5... | collective-permute-start | bytes 442376 | tf_op jit(solution)/shard_map/ppermute | solution.py:19
  41.7 4.5 %collective-permute-start.10 = (bf16[12,1536]{1,0:T(8,128)(2,1)S(1)}, bf16[12,1536]{1,0:T(8,128)(2,1)S(1)}, u32[]{:S(2)}, u32[]{:S(2)}) collective-permute-start(bf16[12,1536]{1,0:T(8,128)(2,1)S(1)} %get-tuple-element.25), channel_id=1, source_target_pairs={{0,8},{4,12},{8,0},{12,4},{16,24},{20,28},{24,16},{28,20},{1,9},{5... | collective-permute-start | bytes 110600 | tf_op jit(solution)/shard_map/ppermute | solution.py:19
  42.2 6.2 %collective-permute-start.11 = (bf16[12,1536]{1,0:T(8,128)(2,1)S(1)}, bf16[12,1536]{1,0:T(8,128)(2,1)S(1)}, u32[]{:S(2)}, u32[]{:S(2)}) collective-permute-start(bf16[12,1536]{1,0:T(8,128)(2,1)S(1)} %get-tuple-element.27), channel_id=1, source_target_pairs={{0,16},{4,20},{8,24},{12,28},{16,0},{20,4},{24,8},{28,12},{1,17},{... | collective-permute-start | bytes 110600 | tf_op jit(solution)/shard_map/ppermute | solution.py:19
  45.7 5.9 %collective-permute-start.12 = (bf16[12,1536]{1,0:T(8,128)(2,1)S(1)}, bf16[12,1536]{1,0:T(8,128)(2,1)S(1)}, u32[]{:S(2)}, u32[]{:S(2)}) collective-permute-start(bf16[12,1536]{1,0:T(8,128)(2,1)S(1)} %get-tuple-element.26), channel_id=1, source_target_pairs={{0,24},{4,28},{8,16},{12,20},{16,8},{20,12},{24,0},{28,4},{1,25},{... | collective-permute-start | bytes 110600 | tf_op jit(solution)/shard_map/ppermute | solution.py:19

commit v3 on v2

v3 whole, which is shorter than its diff:
```python
import functools

import jax
import jax.numpy as jnp
from jax import lax
from jax.experimental import pallas as pl
from jax.experimental.pallas import tpu as pltpu
from jax.sharding import PartitionSpec as P

FRAME_TOK = 4
LANES = 128
MIB = 2**20
PARTS = 2

epsilon = 1e-06

in_vmem = pl.BlockSpec(memory_space=pltpu.VMEM)
in_hbm = pl.BlockSpec(memory_space=pltpu.HBM)


def swap(block, axis, mask):
    size = lax.axis_size(axis)
    return lax.ppermute(block, axis, [(i, i ^ mask) for i in range(size)])


def is_first_core():
    return lax.rem(lax.axis_index("feat"), 2) == 0


def tile_of(width):
    return next((t for t in (512, 384, 256, 128) if width % t == 0), width)


def call(kernel, outs, in_specs, scratch=(), flops=0, limit=4):
    outs = [jax.ShapeDtypeStruct(shape, dtype) for shape, dtype in outs]
    return pl.pallas_call(
        kernel,
        out_shape=outs,
        in_specs=in_specs,
        out_specs=[in_vmem] * len(outs),
        scratch_shapes=list(scratch),
        compiler_params=pltpu.CompilerParams(vmem_limit_bytes=limit * MIB),
        cost_estimate=pl.CostEstimate(
            flops=flops, bytes_accessed=sum(o.size * 4 for o in outs), transcendentals=0
        ),
    )


def pieces(column):
    high = column.astype(jnp.bfloat16).astype(jnp.float32)
    middle = (column - high).astype(jnp.bfloat16).astype(jnp.float32)
    return high, middle, column - high - middle


def pack(sums, squares):
    lane = lax.broadcasted_iota(jnp.int32, (sums.shape[0], LANES), 1)
    packed = jnp.zeros((sums.shape[0], LANES), jnp.float32)
    for at, piece in enumerate(pieces(sums) + pieces(squares)):
        packed = jnp.where(lane == at, piece, packed)
    return packed.astype(jnp.bfloat16)


def unpack(packed):
    packed = packed.astype(jnp.float32)
    column = [packed[:, at:at + 1] for at in range(6)]
    return column[0] + column[1] + column[2], column[3] + column[4] + column[5]


def pack_row(row_of, width, scratch, out_ref):
    count = width // LANES
    scratch[...] = jnp.zeros_like(scratch)
    for at in range(count):
        piece = row_of(at * LANES)
        high = piece.astype(jnp.bfloat16).astype(jnp.float32)
        for place, value in ((at, high), (count + at, piece - high)):
            group, line = divmod(place, scratch.shape[0])
            scratch[line:line + 1, group * LANES:(group + 1) * LANES] = value
    out_ref[...] = scratch[...].astype(jnp.bfloat16)


def unpack_row(packed, start, stop, width):
    count = width // LANES
    pieces = []
    for at in range(start // LANES, stop // LANES):
        piece = 0
        for place in (at, count + at):
            group, line = divmod(place, packed.shape[0])
            piece = piece + packed[line:line + 1, group * LANES:(group + 1) * LANES]
        pieces.append(piece)
    return jnp.concatenate(pieces, axis=1)


def load_up_kernel(gain_ref, weight_ref, out_ref, row_ref, packed_ref, scratch, sems):
    width = weight_ref.shape[1]
    tile = tile_of(width)
    copies = [
        pltpu.make_async_copy(
            weight_ref.at[:, pl.ds(at, tile)], out_ref.at[:, pl.ds(at, tile)], sems.at[at // tile]
        )
        for at in range(0, width, tile)
    ]
    for copy in copies:
        copy.start()
    gain = gain_ref[...][None, :]
    high = gain.astype(jnp.bfloat16).astype(jnp.float32)
    row = lax.broadcasted_iota(jnp.int32, (16, gain.shape[1]), 0)
    rows = jnp.where(row == 0, high, jnp.where(row == 1, gain - high, 0.0)).astype(jnp.bfloat16)
    for at, copy in zip(range(0, width, tile), copies):
        copy.wait()
        product = jnp.dot(rows, out_ref[:, at:at + tile], preferred_element_type=jnp.float32)
        row_ref[:, at:at + tile] = product[0:1] + product[1:2]
    pack_row(lambda at: row_ref[:, at:at + LANES], width, scratch, packed_ref)


def up_kernel(start, near_ref, far_ref, gain_ref, packed_ref, weight_ref, rows_ref, own_ref, kept_ref, given_ref):
    half, block_width = near_ref.shape
    width = kept_ref.shape[1]
    first = is_first_core()
    near, far = near_ref[...].astype(jnp.float32), far_ref[...].astype(jnp.float32)
    for at, values in enumerate((jnp.where(first, near, far), jnp.where(first, far, near))):
        sums = jnp.sum(values, axis=1, keepdims=True)
        squares = jnp.sum(values * values, axis=1, keepdims=True)
        centred = (values - sums / block_width) * gain_ref[...][None, :]
        rows_ref[at * half:(at + 1) * half] = centred.astype(jnp.bfloat16)
        packed = pack(sums, squares)
        if at == 0:
            own_ref[...] = packed
        else:
            given_ref[:, width:width + LANES] = packed
    given_ref[:, width + LANES:] = packed_ref[...]
    up_products(start, rows_ref, weight_ref, kept_ref, given_ref)


def up_products(start, rows_ref, weight_ref, kept_ref, given_ref):
    half, width = kept_ref.shape
    tile = tile_of(width)
    for at in range(0, width, tile):
        product = jnp.dot(
            rows_ref[...], weight_ref[:, start + at:start + at + tile], preferred_element_type=jnp.float32
        )
        kept_ref[:, at:at + tile] = product[:half]
        given_ref[:, at:at + tile] = product[half:].astype(jnp.bfloat16)


def pair_kernel(start, full, block_width, kept_ref, own_ref, gain_ref, packed_ref, other_ref, sum_ref, sent_ref, scratch):
    width = kept_ref.shape[1]
    side = other_ref if start == 0 else packed_ref
    sums, squares = unpack(own_ref[...])
    other_sums, other_squares = unpack(side[:, width:width + LANES])
    shift = (sums - other_sums) / (2 * block_width)
    scratch[...] = side[:, width + LANES:].astype(jnp.float32)
    tile = tile_of(width)
    for at in range(0, width, tile):
        cut, there = slice(at, at + tile), slice(start + at, start + at + tile)
        gains = gain_ref[:, there] - unpack_row(scratch, there.start, there.stop, full)
        total = kept_ref[:, cut] + other_ref[:, cut].astype(jnp.float32) + shift * gains
        sum_ref[:, cut] = total
        sent_ref[:, cut] = total.astype(jnp.bfloat16)
    if start == 0:
        sent_ref[:, width:width + LANES] = pack(sums + other_sums, squares + other_squares)
        rows = [gain_ref[:, at:at + LANES] + unpack_row(scratch, at, at + LANES, full) for at in range(0, full, LANES)]
        pack_row(lambda at: rows[at // LANES], full, scratch, sent_ref.at[:, width + LANES:])


def gelu_kernel(start, full, block_width, full_width, peers, bias_ref, sum_ref, *refs):
    out_ref, scratch = refs[-2:]
    packed, others = refs[:peers + 1], refs[peers + 1:-2] or refs[1:peers + 1]
    width = sum_ref.shape[1]
    stats = [unpack(ref[:, width:width + LANES]) for ref in packed]
    row_mean = sum(s[0] for s in stats) / full_width
    spread = sum(s[1] for s in stats) / full_width - row_mean * row_mean
    scale = lax.rsqrt(spread + epsilon)
    shifts = [s[0] / (2 * block_width) - row_mean for s in stats]
    for at, ref in enumerate(packed):
        scratch[at] = ref[:, width + LANES:].astype(jnp.float32)
    tile = tile_of(width)
    for at in range(0, width, tile):
        cut, there = slice(at, at + tile), slice(start + at, start + at + tile)
        total = sum_ref[:, cut]
        for other in others:
            total = total + other[:, cut].astype(jnp.float32)
        for at, shift in enumerate(shifts):
            total = total + shift * unpack_row(scratch.at[at], there.start, there.stop, full)
        active = jax.nn.gelu(total * scale + bias_ref[:, there], approximate=True)
        out_ref[:, cut] = active.astype(jnp.bfloat16)


def down_kernel(start, last, kept_ref, given_ref, weight_ref, *refs):
    half, depth = kept_ref.shape
    rows_ref = refs[-1]
    rows_ref[:half] = kept_ref[...]
    rows_ref[half:] = given_ref[...]
    first = is_first_core()
    width = weight_ref.shape[1]
    tile = tile_of(width)
    for at in range(0, width, tile):
        cut = slice(at, at + tile)
        product = jnp.dot(
            rows_ref[...], weight_ref[start:start + depth, cut], preferred_element_type=jnp.float32
        )
        if start:
            product = product + refs[0][:, cut]
        if last:
            kept, given = product[:half], product[half:]
            refs[-3][:, cut] = jnp.where(first, kept, given)
            refs[-2][:, cut] = jnp.where(first, given, kept).astype(jnp.bfloat16)
        else:
            refs[-2][:, cut] = product


def per_device(
    patches, frame_counts, patch_mask, norm_gain, up_weight, up_bias, down_weight, down_bias
):
    tok_rows, block_width = patches.shape
    hidden_width = up_weight.shape[1]
    tok_size = lax.axis_size("tok")
    feat_size = lax.axis_size("feat")
    full_width = block_width * feat_size
    f32, bf16 = jnp.float32, jnp.bfloat16

    parts = PARTS if hidden_width % (PARTS * LANES) == 0 else 1
    width = hidden_width // parts
    starts = range(0, hidden_width, width)

    masks = range(2, tok_size, 2)
    peers = range(2, feat_size, 2)
    half = tok_rows * tok_size // 2
    side = LANES * -(-2 * hidden_width // (LANES * half))
    extra = [LANES + side if start == 0 else 0 for start in starts]
    loaded, gain_row, gain_packed = call(
        load_up_kernel,
        [(up_weight.shape, bf16), ((1, hidden_width), f32), ((half, side), bf16)],
        [in_vmem, in_hbm],
        [
            pltpu.VMEM((half, side), f32),
            pltpu.SemaphoreType.DMA((hidden_width // tile_of(hidden_width),)),
        ],
        flops=32 * up_weight.size,
        limit=40,
    )(norm_gain, up_weight)
    near = jnp.concatenate([patches] + [swap(patches, "tok", mask) for mask in masks])
    near, gain_row = lax.optimization_barrier((near, gain_row))
    far = swap(near, "tok", 1)

    kepts, givens = [], []
    for start, more in zip(starts, extra):
        outs = [((half, width), f32), ((half, width + more), bf16)]
        flops = 4 * half * block_width * width
        if start == 0:
            rows, own, kept, given = call(
                functools.partial(up_kernel, start),
                [((2 * half, block_width), bf16), ((half, LANES), bf16)] + outs,
                [in_vmem] * 5,
                flops=flops,
            )(near, far, norm_gain, gain_packed, loaded)
        else:
            kept, given = call(
                functools.partial(up_products, start), outs, [in_vmem] * 2, flops=flops
            )(rows, loaded)
        kepts.append(kept)
        givens.append(given)
    others = [swap(given, "feat", 1) for given in givens]
    sums, sents = [], []
    for start, more, kept, other in zip(starts, extra, kepts, others):
        pair_sum, sent = call(
            functools.partial(pair_kernel, start, hidden_width, block_width),
            [((half, width), f32), ((half, width + more), bf16)],
            [in_vmem] * 5,
            [pltpu.VMEM((half, side), f32)],
        )(kept, own, gain_row, others[0], other)
        sums.append(pair_sum)
        sents.append(sent)
    arrived = [[swap(sent, "feat", mask) for mask in peers] for sent in sents]
    total = ()
    for start, pair_sum, partners in zip(starts, sums, arrived):
        partners = partners if start else []
        (active,) = call(
            functools.partial(gelu_kernel, start, hidden_width, block_width, full_width, len(peers)),
            [((half, width), bf16)],
            [in_vmem] * (3 + len(peers) + len(partners)),
            [pltpu.VMEM((1 + len(peers), half, side), f32)],
        )(up_bias[None, :], pair_sum, sents[0], *arrived[0], *partners)
        last = start == starts[-1]
        total = call(
            functools.partial(down_kernel, start, last),
            [((half, block_width), f32), ((half, block_width), bf16)]
            if last
            else [((2 * half, block_width), f32)],
            [in_vmem] * (3 + len(total)),
            [pltpu.VMEM((2 * half, width), bf16)],
            flops=4 * half * width * block_width,
        )(active, swap(active, "feat", 1), down_weight, *total)
    near_sum, far_sum = total

    near_sum = near_sum + swap(far_sum, "tok", 1)
    blocks = near_sum.reshape(tok_size // 2, tok_rows, block_width)
    summed = blocks[0]
    sent = blocks.astype(bf16)
    for part in [swap(sent[mask // 2], "tok", mask) for mask in masks]:
        summed = summed + part

    positions = jnp.arange(tok_rows, dtype=jnp.int32)
    valid_rows = ((positions // FRAME_TOK < frame_counts) & (patch_mask == 1)).astype(f32)
    return (valid_rows[:, None] * (summed + down_bias[None, :])).astype(bf16)


def solution(mesh):
    in_specs = (
        P("tok", "feat"),
        P("tok"),
        P("tok"),
        P("feat"),
        P("feat", "tok"),
        P("tok"),
        P("tok", "feat"),
        P("feat"),
    )
    out_specs = P("tok", "feat")
    return jax.shard_map(
        per_device, mesh=mesh, in_specs=in_specs, out_specs=out_specs, check_vma=False
    )
```

time: 52.5 us -> 46.8 us (0.89)
  waiting for transfers between devices: 23.5 us -> 18.1 us
  local copies, waits for them, and re-layouts: 4.43 us -> 0.76 us
  Pallas kernels: 5.48 us -> 8.98 us
  other arithmetic: 2.29 us -> 0.79 us
  starting transfers between devices: 15.8 us -> 17.1 us
    ppermute x13 -> x14, waiting for transfers between devices: 23.5 us -> 18.1 us  [swap(): return lax.ppermute(block, axis, [(i, i ^ mask) for i in range(size)])]
    pallas_call x5 -> x9, Pallas kernels: 5.48 us -> 8.98 us  [the longest x1 4.19 us: per_device(): call(load_up_kernel, [(up_weight.shape, bf16), ((1, hidden_width), f32),...]
    unnamed x12 -> x16, local copies, waits for them, and re-layouts: 3.7 us -> 0.73 us
    concatenate x1, other arithmetic: 1.54 us -> 0.05 us  [per_device(): jnp.concatenate([patches] + [swap(patches, 'tok', mask) for mask in masks])]
    ppermute x13 -> x14, starting transfers between devices: 15.8 us -> 17.1 us  [swap(): return lax.ppermute(block, axis, [(i, i ^ mask) for i in range(size)])]
    broadcast_in_dim x1 -> x0, local copies, waits for them, and re-layouts: 0.7 us -> none  [per_device(): norm_gain = norm_gain[None, :]]
  transfers between devices with their start and end apart: 13 -> 14, of which waited for: 8 -> 7; matrix products, arithmetic and copies ran while one was open for 1% -> 0% of each run, Pallas kernels for 3% -> 15%
where the time goes in v3:
time: 46.8 us; the launch traced here: 46.5 us
  waiting for transfers between devices  18.1 us (39%)
  starting transfers between devices  17.1 us (37%)
  Pallas kernels  8.98 us (19%)
  between operations  0.86 us (2%)
  other arithmetic  0.79 us (2%)
  local copies, waits for them, and re-layouts  0.76 us (2%)
    ppermute x14, waiting for transfers between devices, swap(): return lax.ppermute(block, axis, [(i, i ^ mask) for i in range(size)])  18.1 us
    ppermute x14, starting transfers between devices, swap(): return lax.ppermute(block, axis, [(i, i ^ mask) for i in range(size)])  17.1 us
    pallas_call x1, Pallas kernels, per_device(): call(load_up_kernel, [(up_weight.shape, bf16), ((1, hidden_width), f32),...  4.19 us
    pallas_call x2, Pallas kernels, per_device(): call(functools.partial(down_kernel, start, last), [((half, block_width),...  1.79 us
    pallas_call x1, Pallas kernels, per_device(): call(functools.partial(up_kernel, start), [((2 * half, block_width), bf16...  1.05 us
  transfers between devices with their start and end apart: 14, of which 7 were waited for; matrix products, arithmetic and copies ran while one was open for 0% of the time, Pallas kernels for 15%

profile of v3, /device:TPU:0, one launch (start us, length us, event | category | flops | bytes accessed | tf_op | source)
XLA Modules:
  0.0 46.5 jit_solution(7474335544290663665)
XLA Ops:
  0.0 5.0 %collective-permute-start.2 = (bf16[12,1536]{1,0:T(8,128)(2,1)}, bf16[12,1536]{1,0:T(8,128)(2,1)S(1)}, u32[]{:S(2)}, u32[]{:S(2)}) collective-permute-start(bf16[12,1536]{1,0:T(8,128)(2,1)} %param.8), channel_id=1, source_target_pairs={{0,24},{4,28},{8,16},{12,20},{16,8},{20,12},{24,0},{28,4},{1,25},{... | collective-permute-start | bytes 110600 | tf_op jit(solution)/shard_map/ppermute | solution.py:23
  5.0 0.0 collective-permute-start.1
  5.1 0.6 %collective-permute-start = (bf16[12,1536]{1,0:T(8,128)(2,1)}, bf16[12,1536]{1,0:T(8,128)(2,1)S(1)}, u32[]{:S(2)}, u32[]{:S(2)}) collective-permute-start(bf16[12,1536]{1,0:T(8,128)(2,1)} %param.8), channel_id=1, source_target_pairs={{0,8},{4,12},{8,0},{12,4},{16,24},{20,28},{24,16},{28,20},{1,9},{5... | collective-permute-start | bytes 110600 | tf_op jit(solution)/shard_map/ppermute | solution.py:23
  5.6 0.0 copy-start.1
  5.6 0.7 %copy-done.1 = f32[1536]{0:T(1024)S(1)} copy-done((f32[1536]{0:T(1024)S(1)}, f32[1536]{0:T(1024)}, u32[]{:S(2)}) %copy-start.1) | copy-done | bytes 6168
  6.3 0.0 copy-start.2
  6.3 4.2 %shard_map.82 = (bf16[1536,3072]{1,0:T(8,128)(2,1)S(1)}, f32[1,3072]{1,0:T(1,128)S(1)}, bf16[48,128]{1,0:T(8,128)(2,1)S(1)}) custom-call(f32[1536]{0:T(1024)S(1)} %copy-done.1, bf16[1536,3072]{1,0:T(8,128)(2,1)} %weight_ref.3), custom_call_target="tpu_custom_call" | custom-call | flops 150994944 | bytes 18911232 | tf_op jit(solution)/shard_map/pallas_call | solution.py:230
  10.5 0.0 collective-permute-done.2
  10.5 0.0 collective-permute-done.1
  10.5 0.0 collective-permute-done
  10.5 0.0 copy-done.2
  10.6 1.8 %collective-permute-start.3 = (bf16[48,1536]{1,0:T(8,128)(2,1)S(1)}, bf16[48,1536]{1,0:T(8,128)(2,1)S(1)}, u32[]{:S(2)}, u32[]{:S(2)}) collective-permute-start(bf16[48,1536]{1,0:T(8,128)(2,1)S(1)} %pad_maximum_fusion.near_ref), channel_id=1, source_target_pairs={{0,4},{4,0},{8,12},{12,8},{16,20},{20,16},{24,28},{28,24},{1,5},{5... | collective-permute-start | bytes 442376 | tf_op jit(solution)/shard_map/ppermute | solution.py:23
  12.4 3.4 %collective-permute-done.3.far_ref = bf16[48,1536]{1,0:T(8,128)(2,1)S(1)} collective-permute-done((bf16[48,1536]{1,0:T(8,128)(2,1)S(1)}, bf16[48,1536]{1,0:T(8,128)(2,1)S(1)}, u32[]{:S(2)}, u32[]{:S(2)}) %collective-permute-start.3) | collective-permute-done | bytes 147488 | tf_op jit(solution)/shard_map/ppermute | solution.py:23
  15.8 0.0 copy-start
  15.8 0.0 slice-start
  15.8 0.0 slice-start.1
  15.8 1.1 %shard_map.83 = (bf16[96,1536]{1,0:T(8,128)(2,1)S(1)}, bf16[48,128]{1,0:T(8,128)(2,1)S(1)}, f32[48,1536]{1,0:T(8,128)S(1)}, bf16[48,1792]{1,0:T(8,128)(2,1)S(1)}) custom-call(bf16[48,1536]{1,0:T(8,128)(2,1)S(1)} %pad_maximum_fusion.near_ref, bf16[48,1536]{1,0:T(8,128)(2,1)S(1)} %collective-permute-done.3.far_ref, f32[1536]{0:T(1024)S(1)} %copy-done.1, ...), custom_call_target="tpu_custom_call" | custom-call | flops 452984832 | bytes 1253376 | tf_op jit(solution)/shard_map/pallas_call | solution.py:250
  16.9 0.1 collective-permute-start.4
  17.0 0.0 slice-start.2
  17.0 0.9 %shard_map.84 = (f32[48,1536]{1,0:T(8,128)S(1)}, bf16[48,1536]{1,0:T(8,128)(2,1)S(1)}) custom-call(bf16[96,1536]{1,0:T(8,128)(2,1)S(1)} %get-tuple-element.26.rows_ref, bf16[1536,3072]{1,0:T(8,128)(2,1)S(1)} %get-tuple-element.25.weight_ref), custom_call_target="tpu_custom_call" | custom-call | flops 452984832 | bytes 589824 | tf_op jit(solution)/shard_map/pallas_call | solution.py:257
  17.9 0.5 %collective-permute-start.5 = (bf16[48,1536]{1,0:T(8,128)(2,1)S(1)}, bf16[48,1536]{1,0:T(8,128)(2,1)S(1)}, u32[]{:S(2)}, u32[]{:S(2)}) collective-permute-start(bf16[48,1536]{1,0:T(8,128)(2,1)S(1)} %get-tuple-element.31), channel_id=1, source_target_pairs={{0,1},{1,0},{2,3},{3,2},{4,5},{5,4},{6,7},{7,6},{8,9},{9,8},{10,11... | collective-permute-start | bytes 442376 | tf_op jit(solution)/shard_map/ppermute | solution.py:23
  18.4 0.0 collective-permute-done.4.packed_ref.other_ref
  18.4 0.2 shard_map.86
  18.6 1.8 %collective-permute-start.6 = (bf16[48,1792]{1,0:T(8,128)(2,1)S(1)}, bf16[48,1792]{1,0:T(8,128)(2,1)S(1)}, u32[]{:S(2)}, u32[]{:S(2)}) collective-permute-start(bf16[48,1792]{1,0:T(8,128)(2,1)S(1)} %get-tuple-element.34.refs_0_), channel_id=1, source_target_pairs={{0,2},{1,3},{2,0},{3,1},{4,6},{5,7},{6,4},{7,5},{8,10},{9,11},{10,... | collective-permute-start | bytes 516104 | tf_op jit(solution)/shard_map/ppermute | solution.py:23
  20.4 0.0 collective-permute-done.5.other_ref
  20.4 0.2 shard_map.85
  20.6 0.8 %collective-permute-start.7 = (bf16[48,1536]{1,0:T(8,128)(2,1)S(1)}, bf16[48,1536]{1,0:T(8,128)(2,1)S(1)}, u32[]{:S(2)}, u32[]{:S(2)}) collective-permute-start(bf16[48,1536]{1,0:T(8,128)(2,1)S(1)} %get-tuple-element.35), channel_id=1, source_target_pairs={{0,2},{1,3},{2,0},{3,1},{4,6},{5,7},{6,4},{7,5},{8,10},{9,11},{10,... | collective-permute-start | bytes 442376 | tf_op jit(solution)/shard_map/ppermute | solution.py:23
  21.4 4.5 %collective-permute-done.6.refs_1_ = bf16[48,1792]{1,0:T(8,128)(2,1)S(1)} collective-permute-done((bf16[48,1792]{1,0:T(8,128)(2,1)S(1)}, bf16[48,1792]{1,0:T(8,128)(2,1)S(1)}, u32[]{:S(2)}, u32[]{:S(2)}) %collective-permute-start.6) | collective-permute-done | bytes 172064 | tf_op jit(solution)/shard_map/ppermute | solution.py:23
  25.9 0.0 copy-done
  25.9 0.3 shard_map.88.kept_ref
  26.3 0.1 collective-permute-start.9
  26.3 1.9 %collective-permute-done.7.refs_2_ = bf16[48,1536]{1,0:T(8,128)(2,1)S(1)} collective-permute-done((bf16[48,1536]{1,0:T(8,128)(2,1)S(1)}, bf16[48,1536]{1,0:T(8,128)(2,1)S(1)}, u32[]{:S(2)}, u32[]{:S(2)}) %collective-permute-start.7) | collective-permute-done | bytes 147488 | tf_op jit(solution)/shard_map/ppermute | solution.py:23
  28.2 0.3 shard_map.87.kept_ref
  28.6 0.0 copy-start.4
  28.6 0.0 copy-start.3
  28.6 0.1 collective-permute-start.8
  28.7 0.0 collective-permute-done.9.given_ref
  28.7 0.0 slice-done
  28.7 0.0 slice-done.1
  28.7 0.0 slice-done.2
  28.7 0.9 %shard_map.89.refs_0_ = f32[96,1536]{1,0:T(8,128)S(1)} custom-call(bf16[48,1536]{1,0:T(8,128)(2,1)S(1)} %shard_map.88.kept_ref, bf16[48,1536]{1,0:T(8,128)(2,1)S(1)} %collective-permute-done.9.given_ref, bf16[3072,1536]{1,0:T(8,128)(2,1)S(1)} %bitcast.4), custom_call_target="tpu_custom_call" | custom-call | flops 452984832 | bytes 589824 | tf_op jit(solution)/shard_map/pallas_call | solution.py:284
  29.6 0.4 collective-permute-done.8.given_ref
  30.0 0.9 %shard_map.90 = (f32[48,1536]{1,0:T(8,128)S(1)}, bf16[48,1536]{1,0:T(8,128)(2,1)S(1)}) custom-call(bf16[48,1536]{1,0:T(8,128)(2,1)S(1)} %shard_map.87.kept_ref, bf16[48,1536]{1,0:T(8,128)(2,1)S(1)} %collective-permute-done.8.given_ref, bf16[3072,1536]{1,0:T(8,128)(2,1)S(1)} %bitcast.4, f32[96,1536]{1,0:T(8,128)S(1)} %shard_map.89.refs_0_), custom_call_target="tpu_custom_call" | custom-call | flops 452984832 | bytes 589824 | tf_op jit(solution)/shard_map/pallas_call | solution.py:284
  30.9 1.8 %collective-permute-start.10 = (bf16[48,1536]{1,0:T(8,128)(2,1)S(1)}, bf16[48,1536]{1,0:T(8,128)(2,1)S(1)}, u32[]{:S(2)}, u32[]{:S(2)}) collective-permute-start(bf16[48,1536]{1,0:T(8,128)(2,1)S(1)} %get-tuple-element.38), channel_id=1, source_target_pairs={{0,4},{4,0},{8,12},{12,8},{16,20},{20,16},{24,28},{28,24},{1,5},{5... | collective-permute-start | bytes 442376 | tf_op jit(solution)/shard_map/ppermute | solution.py:23
  33.4 3.5 %collective-permute-done.10 = bf16[48,1536]{1,0:T(8,128)(2,1)S(1)} collective-permute-done((bf16[48,1536]{1,0:T(8,128)(2,1)S(1)}, bf16[48,1536]{1,0:T(8,128)(2,1)S(1)}, u32[]{:S(2)}, u32[]{:S(2)}) %collective-permute-start.10) | collective-permute-done | bytes 147488 | tf_op jit(solution)/shard_map/ppermute | solution.py:23
  37.0 3.9 %collective-permute-start.13 = (bf16[12,1536]{1,0:T(8,128)(2,1)S(1)}, bf16[12,1536]{1,0:T(8,128)(2,1)S(1)}, u32[]{:S(2)}, u32[]{:S(2)}) collective-permute-start(bf16[12,1536]{1,0:T(8,128)(2,1)S(1)} %get-tuple-element.42), channel_id=1, source_target_pairs={{0,24},{4,28},{8,16},{12,20},{16,8},{20,12},{24,0},{28,4},{1,25},{... | collective-permute-start | bytes 110600 | tf_op jit(solution)/shard_map/ppermute | solution.py:23
  40.9 0.0 collective-permute-start.12
  40.9 0.6 %collective-permute-start.11 = (bf16[12,1536]{1,0:T(8,128)(2,1)S(1)}, bf16[12,1536]{1,0:T(8,128)(2,1)S(1)}, u32[]{:S(2)}, u32[]{:S(2)}) collective-permute-start(bf16[12,1536]{1,0:T(8,128)(2,1)S(1)} %get-tuple-element.41), channel_id=1, source_target_pairs={{0,8},{4,12},{8,0},{12,4},{16,24},{20,28},{24,16},{28,20},{1,9},{5... | collective-permute-start | bytes 110600 | tf_op jit(solution)/shard_map/ppermute | solution.py:23
  41.5 0.0 copy-done.4
  41.5 1.6 %collective-permute-done.13 = bf16[12,1536]{1,0:T(8,128)(2,1)S(1)} collective-permute-done((bf16[12,1536]{1,0:T(8,128)(2,1)S(1)}, bf16[12,1536]{1,0:T(8,128)(2,1)S(1)}, u32[]{:S(2)}, u32[]{:S(2)}) %collective-permute-start.13) | collective-permute-done | bytes 36896 | tf_op jit(solution)/shard_map/ppermute | solution.py:23
  43.1 2.8 %collective-permute-done.12 = bf16[12,1536]{1,0:T(8,128)(2,1)S(1)} collective-permute-done((bf16[12,1536]{1,0:T(8,128)(2,1)S(1)}, bf16[12,1536]{1,0:T(8,128)(2,1)S(1)}, u32[]{:S(2)}, u32[]{:S(2)}) %collective-permute-start.12) | collective-permute-done | bytes 36896 | tf_op jit(solution)/shard_map/ppermute | solution.py:23
  45.8 0.0 collective-permute-done.11
  45.9 0.0 copy-done.3
  45.9 0.7 %fusion.4 = bf16[12,1536]{1,0:T(8,128)(2,1)} fusion(f32[48,1536]{1,0:T(8,128)S(1)} %get-tuple-element.40, bf16[12,1536]{1,0:T(8,128)(2,1)S(1)} %collective-permute-done.13, bf16[12,1536]{1,0:T(8,128)(2,1)S(1)} %collective-permute-done.12, bf16[12,1536]{1,0:T(8,128)(2,1)S(1)} %collective-permute-done.11, f32[1536]{0:T(1024)S(1)} %copy-done.3, ...), kind=kLoop, calls=%fused_computation.7 | loop fusion | flops 165888 | bytes 227376 | tf_op jit(solution)/shard_map/convert_element_type | solution.py:304
  (5 shorter events, 0.1 us)
Async XLA Ops:
  0.0 10.5 %collective-permute-start.2 = (bf16[12,1536]{1,0:T(8,128)(2,1)}, bf16[12,1536]{1,0:T(8,128)(2,1)S(1)}, u32[]{:S(2)}, u32[]{:S(2)}) collective-permute-start(bf16[12,1536]{1,0:T(8,128)(2,1)} %param.8), channel_id=1, source_target_pairs={{0,24},{4,28},{8,16},{12,20},{16,8},{20,12},{24,0},{28,4},{1,25},{... | collective-permute-start | bytes 110600 | tf_op jit(solution)/shard_map/ppermute | solution.py:23
  5.0 5.5 %collective-permute-start.1 = (bf16[12,1536]{1,0:T(8,128)(2,1)}, bf16[12,1536]{1,0:T(8,128)(2,1)S(1)}, u32[]{:S(2)}, u32[]{:S(2)}) collective-permute-start(bf16[12,1536]{1,0:T(8,128)(2,1)} %param.8), channel_id=1, source_target_pairs={{0,16},{4,20},{8,24},{12,28},{16,0},{20,4},{24,8},{28,12},{1,17},{... | collective-permute-start | bytes 110600 | tf_op jit(solution)/shard_map/ppermute | solution.py:23
  5.1 5.5 %collective-permute-start = (bf16[12,1536]{1,0:T(8,128)(2,1)}, bf16[12,1536]{1,0:T(8,128)(2,1)S(1)}, u32[]{:S(2)}, u32[]{:S(2)}) collective-permute-start(bf16[12,1536]{1,0:T(8,128)(2,1)} %param.8), channel_id=1, source_target_pairs={{0,8},{4,12},{8,0},{12,4},{16,24},{20,28},{24,16},{28,20},{1,9},{5... | collective-permute-start | bytes 110600 | tf_op jit(solution)/shard_map/ppermute | solution.py:23
  5.6 0.7 %copy-start.1 = (f32[1536]{0:T(1024)S(1)}, f32[1536]{0:T(1024)}, u32[]{:S(2)}) copy-start(f32[1536]{0:T(1024)} %gain_ref.3) | copy-start | bytes 18436
  6.3 4.2 %copy-start.2 = (bf16[12,1536]{1,0:T(8,128)(2,1)S(1)}, bf16[12,1536]{1,0:T(8,128)(2,1)}, u32[]{:S(2)}) copy-start(bf16[12,1536]{1,0:T(8,128)(2,1)} %param.8) | copy-start | bytes 110596
  10.6 5.2 %collective-permute-start.3 = (bf16[48,1536]{1,0:T(8,128)(2,1)S(1)}, bf16[48,1536]{1,0:T(8,128)(2,1)S(1)}, u32[]{:S(2)}, u32[]{:S(2)}) collective-permute-start(bf16[48,1536]{1,0:T(8,128)(2,1)S(1)} %pad_maximum_fusion.near_ref), channel_id=1, source_target_pairs={{0,4},{4,0},{8,12},{12,8},{16,20},{20,16},{24,28},{28,24},{1,5},{5... | collective-permute-start | bytes 442376 | tf_op jit(solution)/shard_map/ppermute | solution.py:23
  15.8 10.1 %copy-start = (f32[3072]{0:T(1024)S(1)}, f32[3072]{0:T(1024)}, u32[]{:S(2)}) copy-start(f32[3072]{0:T(1024)} %param.13) | copy-start | bytes 36868
  15.8 12.8 %slice-start = ((s8[9437184]{0:T(1024)(128)(4,1)}), s8[4194304]{0:T(1024)(128)(4,1)S(1)}, s32[]{:S(2)}) async-start(s8[9437184]{0:T(1024)(128)(4,1)} %bitcast.3), calls=%async_computation | async-start | bytes 8388608
  15.8 12.9 %slice-start.1 = ((s8[9437184]{0:T(1024)(128)(4,1)}), s8[4194304]{0:T(1024)(128)(4,1)S(1)}, s32[]{:S(2)}) async-start(s8[9437184]{0:T(1024)(128)(4,1)} %bitcast.3), calls=%async_computation.1 | async-start | bytes 8388608
  16.9 1.5 %collective-permute-start.4 = (bf16[48,1792]{1,0:T(8,128)(2,1)S(1)}, bf16[48,1792]{1,0:T(8,128)(2,1)S(1)}, u32[]{:S(2)}, u32[]{:S(2)}) collective-permute-start(bf16[48,1792]{1,0:T(8,128)(2,1)S(1)} %get-tuple-element.30), channel_id=1, source_target_pairs={{0,1},{1,0},{2,3},{3,2},{4,5},{5,4},{6,7},{7,6},{8,9},{9,8},{10,11... | collective-permute-start | bytes 516104 | tf_op jit(solution)/shard_map/ppermute | solution.py:23
  17.0 11.7 %slice-start.2 = ((s8[9437184]{0:T(1024)(128)(4,1)}), s8[1048576]{0:T(1024)(128)(4,1)S(1)}, s32[]{:S(2)}) async-start(s8[9437184]{0:T(1024)(128)(4,1)} %bitcast.3), calls=%async_computation.2 | async-start | bytes 2097152
  17.9 2.6 %collective-permute-start.5 = (bf16[48,1536]{1,0:T(8,128)(2,1)S(1)}, bf16[48,1536]{1,0:T(8,128)(2,1)S(1)}, u32[]{:S(2)}, u32[]{:S(2)}) collective-permute-start(bf16[48,1536]{1,0:T(8,128)(2,1)S(1)} %get-tuple-element.31), channel_id=1, source_target_pairs={{0,1},{1,0},{2,3},{3,2},{4,5},{5,4},{6,7},{7,6},{8,9},{9,8},{10,11... | collective-permute-start | bytes 442376 | tf_op jit(solution)/shard_map/ppermute | solution.py:23
  18.6 7.3 %collective-permute-start.6 = (bf16[48,1792]{1,0:T(8,128)(2,1)S(1)}, bf16[48,1792]{1,0:T(8,128)(2,1)S(1)}, u32[]{:S(2)}, u32[]{:S(2)}) collective-permute-start(bf16[48,1792]{1,0:T(8,128)(2,1)S(1)} %get-tuple-element.34.refs_0_), channel_id=1, source_target_pairs={{0,2},{1,3},{2,0},{3,1},{4,6},{5,7},{6,4},{7,5},{8,10},{9,11},{10,... | collective-permute-start | bytes 516104 | tf_op jit(solution)/shard_map/ppermute | solution.py:23
  20.6 7.6 %collective-permute-start.7 = (bf16[48,1536]{1,0:T(8,128)(2,1)S(1)}, bf16[48,1536]{1,0:T(8,128)(2,1)S(1)}, u32[]{:S(2)}, u32[]{:S(2)}) collective-permute-start(bf16[48,1536]{1,0:T(8,128)(2,1)S(1)} %get-tuple-element.35), channel_id=1, source_target_pairs={{0,2},{1,3},{2,0},{3,1},{4,6},{5,7},{6,4},{7,5},{8,10},{9,11},{10,... | collective-permute-start | bytes 442376 | tf_op jit(solution)/shard_map/ppermute | solution.py:23
  26.3 2.4 %collective-permute-start.9 = (bf16[48,1536]{1,0:T(8,128)(2,1)S(1)}, bf16[48,1536]{1,0:T(8,128)(2,1)S(1)}, u32[]{:S(2)}, u32[]{:S(2)}) collective-permute-start(bf16[48,1536]{1,0:T(8,128)(2,1)S(1)} %shard_map.88.kept_ref), channel_id=1, source_target_pairs={{0,1},{1,0},{2,3},{3,2},{4,5},{5,4},{6,7},{7,6},{8,9},{9,8},{10,11... | collective-permute-start | bytes 442376 | tf_op jit(solution)/shard_map/ppermute | solution.py:23
  28.6 12.9 %copy-start.4 = (s32[12]{0:T(128)S(1)}, s32[12]{0:T(128)}, u32[]{:S(2)}) copy-start(s32[12]{0:T(128)} %param.10) | copy-start | bytes 148
  28.6 17.3 %copy-start.3 = (f32[1536]{0:T(1024)S(1)}, f32[1536]{0:T(1024)}, u32[]{:S(2)}) copy-start(f32[1536]{0:T(1024)} %param.15) | copy-start | bytes 18436
  28.6 1.4 %collective-permute-start.8 = (bf16[48,1536]{1,0:T(8,128)(2,1)S(1)}, bf16[48,1536]{1,0:T(8,128)(2,1)S(1)}, u32[]{:S(2)}, u32[]{:S(2)}) collective-permute-start(bf16[48,1536]{1,0:T(8,128)(2,1)S(1)} %shard_map.87.kept_ref), channel_id=1, source_target_pairs={{0,1},{1,0},{2,3},{3,2},{4,5},{5,4},{6,7},{7,6},{8,9},{9,8},{10,11... | collective-permute-start | bytes 442376 | tf_op jit(solution)/shard_map/ppermute | solution.py:23
  30.9 6.0 %collective-permute-start.10 = (bf16[48,1536]{1,0:T(8,128)(2,1)S(1)}, bf16[48,1536]{1,0:T(8,128)(2,1)S(1)}, u32[]{:S(2)}, u32[]{:S(2)}) collective-permute-start(bf16[48,1536]{1,0:T(8,128)(2,1)S(1)} %get-tuple-element.38), channel_id=1, source_target_pairs={{0,4},{4,0},{8,12},{12,8},{16,20},{20,16},{24,28},{28,24},{1,5},{5... | collective-permute-start | bytes 442376 | tf_op jit(solution)/shard_map/ppermute | solution.py:23
  37.0 6.1 %collective-permute-start.13 = (bf16[12,1536]{1,0:T(8,128)(2,1)S(1)}, bf16[12,1536]{1,0:T(8,128)(2,1)S(1)}, u32[]{:S(2)}, u32[]{:S(2)}) collective-permute-start(bf16[12,1536]{1,0:T(8,128)(2,1)S(1)} %get-tuple-element.42), channel_id=1, source_target_pairs={{0,24},{4,28},{8,16},{12,20},{16,8},{20,12},{24,0},{28,4},{1,25},{... | collective-permute-start | bytes 110600 | tf_op jit(solution)/shard_map/ppermute | solution.py:23
  40.9 5.0 %collective-permute-start.12 = (bf16[12,1536]{1,0:T(8,128)(2,1)S(1)}, bf16[12,1536]{1,0:T(8,128)(2,1)S(1)}, u32[]{:S(2)}, u32[]{:S(2)}) collective-permute-start(bf16[12,1536]{1,0:T(8,128)(2,1)S(1)} %get-tuple-element.43), channel_id=1, source_target_pairs={{0,16},{4,20},{8,24},{12,28},{16,0},{20,4},{24,8},{28,12},{1,17},{... | collective-permute-start | bytes 110600 | tf_op jit(solution)/shard_map/ppermute | solution.py:23
  40.9 5.0 %collective-permute-start.11 = (bf16[12,1536]{1,0:T(8,128)(2,1)S(1)}, bf16[12,1536]{1,0:T(8,128)(2,1)S(1)}, u32[]{:S(2)}, u32[]{:S(2)}) collective-permute-start(bf16[12,1536]{1,0:T(8,128)(2,1)S(1)} %get-tuple-element.41), channel_id=1, source_target_pairs={{0,8},{4,12},{8,0},{12,4},{16,24},{20,28},{24,16},{28,20},{1,9},{5... | collective-permute-start | bytes 110600 | tf_op jit(solution)/shard_map/ppermute | solution.py:23

commit v4 on v3

--- a/solution.py
+++ b/solution.py
@@ -90,29 +90,32 @@
     return jnp.concatenate(pieces, axis=1)
 
 
-def load_up_kernel(gain_ref, weight_ref, out_ref, row_ref, packed_ref, scratch, sems):
-    width = weight_ref.shape[1]
-    tile = tile_of(width)
-    copies = [
-        pltpu.make_async_copy(
-            weight_ref.at[:, pl.ds(at, tile)], out_ref.at[:, pl.ds(at, tile)], sems.at[at // tile]
-        )
-        for at in range(0, width, tile)
-    ]
-    for copy in copies:
-        copy.start()
+def load_kernel(start, weight_ref, out_ref, sem):
+    copy = pltpu.make_async_copy(weight_ref.at[:, pl.ds(start, out_ref.shape[1])], out_ref, sem)
+    copy.start()
+    copy.wait()
+
+
+def load_last_kernel(start, gain_ref, *refs):
+    weight_ref, out_ref, row_ref, packed_ref, scratch, sem = refs[-6:]
+    width = out_ref.shape[1]
+    copy = pltpu.make_async_copy(weight_ref.at[:, pl.ds(start, width)], out_ref, sem)
+    copy.start()
     gain = gain_ref[...][None, :]
     high = gain.astype(jnp.bfloat16).astype(jnp.float32)
     row = lax.broadcasted_iota(jnp.int32, (16, gain.shape[1]), 0)
     rows = jnp.where(row == 0, high, jnp.where(row == 1, gain - high, 0.0)).astype(jnp.bfloat16)
-    for at, copy in zip(range(0, width, tile), copies):
-        copy.wait()
-        product = jnp.dot(rows, out_ref[:, at:at + tile], preferred_element_type=jnp.float32)
-        row_ref[:, at:at + tile] = product[0:1] + product[1:2]
-    pack_row(lambda at: row_ref[:, at:at + LANES], width, scratch, packed_ref)
-
-
-def up_kernel(start, near_ref, far_ref, gain_ref, packed_ref, weight_ref, rows_ref, own_ref, kept_ref, given_ref):
+    tile = tile_of(width)
+    for part, loaded in enumerate(refs[:-6] + (out_ref,)):
+        if loaded is out_ref:
+            copy.wait()
+        for at in range(0, width, tile):
+            product = jnp.dot(rows, loaded[:, at:at + tile], preferred_element_type=jnp.float32)
+            row_ref[:, part * width + at:part * width + at + tile] = product[0:1] + product[1:2]
+    pack_row(lambda at: row_ref[:, at:at + LANES], row_ref.shape[1], scratch, packed_ref)
+
+
+def up_kernel(near_ref, far_ref, gain_ref, packed_ref, weight_ref, rows_ref, own_ref, kept_ref, given_ref):
     half, block_width = near_ref.shape
     width = kept_ref.shape[1]
     first = is_first_core()
@@ -128,15 +131,15 @@
         else:
             given_ref[:, width:width + LANES] = packed
     given_ref[:, width + LANES:] = packed_ref[...]
-    up_products(start, rows_ref, weight_ref, kept_ref, given_ref)
-
-
-def up_products(start, rows_ref, weight_ref, kept_ref, given_ref):
+    up_products(rows_ref, weight_ref, kept_ref, given_ref)
+
+
+def up_products(rows_ref, weight_ref, kept_ref, given_ref):
     half, width = kept_ref.shape
     tile = tile_of(width)
     for at in range(0, width, tile):
         product = jnp.dot(
-            rows_ref[...], weight_ref[:, start + at:start + at + tile], preferred_element_type=jnp.float32
+            rows_ref[...], weight_ref[:, at:at + tile], preferred_element_type=jnp.float32
         )
         kept_ref[:, at:at + tile] = product[:half]
         given_ref[:, at:at + tile] = product[half:].astype(jnp.bfloat16)
@@ -227,36 +230,46 @@
     half = tok_rows * tok_size // 2
     side = LANES * -(-2 * hidden_width // (LANES * half))
     extra = [LANES + side if start == 0 else 0 for start in starts]
-    loaded, gain_row, gain_packed = call(
-        load_up_kernel,
-        [(up_weight.shape, bf16), ((1, hidden_width), f32), ((half, side), bf16)],
-        [in_vmem, in_hbm],
-        [
-            pltpu.VMEM((half, side), f32),
-            pltpu.SemaphoreType.DMA((hidden_width // tile_of(hidden_width),)),
-        ],
+    copied = pltpu.SemaphoreType.DMA
+    loaded = [
+        call(
+            functools.partial(load_kernel, start),
+            [((block_width, width), bf16)],
+            [in_hbm],
+            [copied],
+            limit=46,
+        )(up_weight)[0]
+        for start in starts[:-1]
+    ]
+    order = [0] + list(reversed(masks))
+    near = jnp.concatenate([patches] + [swap(patches, "tok", mask) for mask in order[1:]])
+    near, loaded, norm_gain = lax.optimization_barrier((near, loaded, norm_gain))
+    far = swap(near, "tok", 1)
+    last, gain_row, gain_packed = call(
+        functools.partial(load_last_kernel, starts[-1]),
+        [((block_width, width), bf16), ((1, hidden_width), f32), ((half, side), bf16)],
+        [in_vmem] * parts + [in_hbm],
+        [pltpu.VMEM((half, side), f32), copied],
         flops=32 * up_weight.size,
         limit=40,
-    )(norm_gain, up_weight)
-    near = jnp.concatenate([patches] + [swap(patches, "tok", mask) for mask in masks])
-    near, gain_row = lax.optimization_barrier((near, gain_row))
-    far = swap(near, "tok", 1)
+    )(norm_gain, *loaded, up_weight)
+    loaded = loaded + [last]
 
     kepts, givens = [], []
-    for start, more in zip(starts, extra):
+    for start, more, weight in zip(starts, extra, loaded):
         outs = [((half, width), f32), ((half, width + more), bf16)]
         flops = 4 * half * block_width * width
         if start == 0:
             rows, own, kept, given = call(
-                functools.partial(up_kernel, start),
+                up_kernel,
                 [((2 * half, block_width), bf16), ((half, LANES), bf16)] + outs,
                 [in_vmem] * 5,
                 flops=flops,
-            )(near, far, norm_gain, gain_packed, loaded)
+            )(near, far, norm_gain, gain_packed, weight)
         else:
             kept, given = call(
-                functools.partial(up_products, start), outs, [in_vmem] * 2, flops=flops
-            )(rows, loaded)
+                up_products, outs, [in_vmem] * 2, flops=flops
+            )(rows, weight)
         kepts.append(kept)
         givens.append(given)
     others = [swap(given, "feat", 1) for given in givens]
@@ -296,7 +309,7 @@
     blocks = near_sum.reshape(tok_size // 2, tok_rows, block_width)
     summed = blocks[0]
     sent = blocks.astype(bf16)
-    for part in [swap(sent[mask // 2], "tok", mask) for mask in masks]:
+    for part in [swap(sent[order.index(mask)], "tok", mask) for mask in reversed(masks)]:
         summed = summed + part
 
     positions = jnp.arange(tok_rows, dtype=jnp.int32)

time: 46.8 us -> 45.1 us (0.964)
  waiting for transfers between devices: 18.1 us -> 16.4 us
  Pallas kernels: 8.98 us -> 10.4 us
  starting transfers between devices: 17.1 us -> 16.4 us
  local copies, waits for them, and re-layouts: 0.76 us -> 0.07 us
    ppermute x14, waiting for transfers between devices: 18.1 us -> 16.4 us  [swap(): return lax.ppermute(block, axis, [(i, i ^ mask) for i in range(size)])]
    pallas_call x3 -> x4, Pallas kernels: 6.12 us -> 7.59 us  [the longest x1 3.36 us: per_device(): call(functools.partial(load_last_kernel, starts[-1]), [((block_width, wid...]
    unnamed x16, local copies, waits for them, and re-layouts: 0.73 us -> 0.04 us
    ppermute x14, starting transfers between devices: 17.1 us -> 16.4 us  [swap(): return lax.ppermute(block, axis, [(i, i ^ mask) for i in range(size)])]
  transfers between devices with their start and end apart: 14 -> 14, of which waited for: 7 -> 8; matrix products, arithmetic and copies ran while one was open for 0% -> 0% of each run, Pallas kernels for 15% -> 19%
where the time goes in v4:
time: 45.1 us; the launch traced here: 45 us
  starting transfers between devices  16.4 us (36%)
  waiting for transfers between devices  16.4 us (36%)
  Pallas kernels  10.4 us (23%)
  between operations  0.84 us (2%)
  other arithmetic  0.79 us (2%)
    ppermute x14, starting transfers between devices, swap(): return lax.ppermute(block, axis, [(i, i ^ mask) for i in range(size)])  16.4 us
    ppermute x14, waiting for transfers between devices, swap(): return lax.ppermute(block, axis, [(i, i ^ mask) for i in range(size)])  16.4 us
    pallas_call x1, Pallas kernels, per_device(): call(functools.partial(load_last_kernel, starts[-1]), [((block_width, wid...  3.36 us
    pallas_call x1, Pallas kernels, per_device(): call(functools.partial(load_kernel, start), [((block_width, width), bf16)...  2.34 us
    pallas_call x2, Pallas kernels, per_device(): call(functools.partial(down_kernel, start, last), [((half, block_width),...  1.78 us
    pallas_call x1, Pallas kernels, per_device(): call(up_kernel, [((2 * half, block_width), bf16), ((half, LANES), bf16)]...  1.01 us
  transfers between devices with their start and end apart: 14, of which 8 were waited for; matrix products, arithmetic and copies ran while one was open for 0% of the time, Pallas kernels for 19%

profile of v4, /device:TPU:0, one launch (start us, length us, event | category | flops | bytes accessed | tf_op | source)
XLA Modules:
  0.0 45.0 jit_solution(2098017356198090237)
XLA Ops:
  0.0 0.0 copy-start.2
  0.0 0.0 copy-start.1
  0.0 5.0 %collective-permute-start = (bf16[12,1536]{1,0:T(8,128)(2,1)}, bf16[12,1536]{1,0:T(8,128)(2,1)S(1)}, u32[]{:S(2)}, u32[]{:S(2)}) collective-permute-start(bf16[12,1536]{1,0:T(8,128)(2,1)} %param.8), channel_id=1, source_target_pairs={{0,24},{4,28},{8,16},{12,20},{16,8},{20,12},{24,0},{28,4},{1,25},{... | collective-permute-start | bytes 110600 | tf_op jit(solution)/shard_map/ppermute | solution.py:23
  5.1 0.0 collective-permute-start.1
  5.1 0.6 %collective-permute-start.2 = (bf16[12,1536]{1,0:T(8,128)(2,1)}, bf16[12,1536]{1,0:T(8,128)(2,1)S(1)}, u32[]{:S(2)}, u32[]{:S(2)}) collective-permute-start(bf16[12,1536]{1,0:T(8,128)(2,1)} %param.8), channel_id=1, source_target_pairs={{0,8},{4,12},{8,0},{12,4},{16,24},{20,28},{24,16},{28,20},{1,9},{5... | collective-permute-start | bytes 110600 | tf_op jit(solution)/shard_map/ppermute | solution.py:23
  5.7 2.3 %shard_map.82.refs_0_.weight_ref = bf16[1536,1536]{1,0:T(8,128)(2,1)S(1)} custom-call(bf16[1536,3072]{1,0:T(8,128)(2,1)} %refs_1_.1), custom_call_target="tpu_custom_call" | custom-call | bytes 9437184 | tf_op jit(solution)/shard_map/pallas_call | solution.py:235
  8.0 0.0 collective-permute-done
  8.1 2.2 %collective-permute-done.1 = bf16[12,1536]{1,0:T(8,128)(2,1)S(1)} collective-permute-done((bf16[12,1536]{1,0:T(8,128)(2,1)}, bf16[12,1536]{1,0:T(8,128)(2,1)S(1)}, u32[]{:S(2)}, u32[]{:S(2)}) %collective-permute-start.1) | collective-permute-done | bytes 36896 | tf_op jit(solution)/shard_map/ppermute | solution.py:23
  10.3 0.0 collective-permute-done.2
  10.3 0.0 copy-done.2
  10.3 0.0 copy-start
  10.3 1.6 %collective-permute-start.3 = (bf16[48,1536]{1,0:T(8,128)(2,1)S(1)}, bf16[48,1536]{1,0:T(8,128)(2,1)S(1)}, u32[]{:S(2)}, u32[]{:S(2)}) collective-permute-start(bf16[48,1536]{1,0:T(8,128)(2,1)S(1)} %pad_maximum_fusion.near_ref), channel_id=1, source_target_pairs={{0,4},{4,0},{8,12},{12,8},{16,20},{20,16},{24,28},{28,24},{1,5},{5... | collective-permute-start | bytes 442376 | tf_op jit(solution)/shard_map/ppermute | solution.py:23
  11.9 0.0 copy-done.1
  11.9 0.0 slice-start
  11.9 0.0 slice-start.1
  11.9 3.4 %shard_map.83 = (bf16[1536,1536]{1,0:T(8,128)(2,1)S(1)}, f32[1,3072]{1,0:T(1,128)S(1)}, bf16[48,128]{1,0:T(8,128)(2,1)S(1)}) custom-call(f32[1536]{0:T(1024)S(1)} %copy-done.1, bf16[1536,1536]{1,0:T(8,128)(2,1)S(1)} %shard_map.82.refs_0_.weight_ref, bf16[1536,3072]{1,0:T(8,128)(2,1)} %refs_1_.1), custom_call_target="tpu_custom_call" | custom-call | flops 150994944 | bytes 9474048 | tf_op jit(solution)/shard_map/pallas_call | solution.py:248
  15.3 0.3 collective-permute-done.3.far_ref
  15.5 0.0 slice-start.2
  15.5 1.0 %shard_map.84 = (bf16[96,1536]{1,0:T(8,128)(2,1)S(1)}, bf16[48,128]{1,0:T(8,128)(2,1)S(1)}, f32[48,1536]{1,0:T(8,128)S(1)}, bf16[48,1792]{1,0:T(8,128)(2,1)S(1)}) custom-call(bf16[48,1536]{1,0:T(8,128)(2,1)S(1)} %pad_maximum_fusion.near_ref, bf16[48,1536]{1,0:T(8,128)(2,1)S(1)} %collective-permute-done.3.far_ref, f32[1536]{0:T(1024)S(1)} %copy-done.1, ...), custom_call_target="tpu_custom_call" | custom-call | flops 452984832 | bytes 1253376 | tf_op jit(solution)/shard_map/pallas_call | solution.py:263
  16.6 0.1 collective-permute-start.4
  16.6 0.9 %shard_map.85 = (f32[48,1536]{1,0:T(8,128)S(1)}, bf16[48,1536]{1,0:T(8,128)(2,1)S(1)}) custom-call(bf16[96,1536]{1,0:T(8,128)(2,1)S(1)} %get-tuple-element.27.rows_ref, bf16[1536,1536]{1,0:T(8,128)(2,1)S(1)} %get-tuple-element.28.weight_ref), custom_call_target="tpu_custom_call" | custom-call | flops 452984832 | bytes 589824 | tf_op jit(solution)/shard_map/pallas_call | solution.py:270
  17.5 0.6 %collective-permute-start.5 = (bf16[48,1536]{1,0:T(8,128)(2,1)S(1)}, bf16[48,1536]{1,0:T(8,128)(2,1)S(1)}, u32[]{:S(2)}, u32[]{:S(2)}) collective-permute-start(bf16[48,1536]{1,0:T(8,128)(2,1)S(1)} %get-tuple-element.33), channel_id=1, source_target_pairs={{0,1},{1,0},{2,3},{3,2},{4,5},{5,4},{6,7},{7,6},{8,9},{9,8},{10,11... | collective-permute-start | bytes 442376 | tf_op jit(solution)/shard_map/ppermute | solution.py:23
  18.1 0.0 collective-permute-done.4.packed_ref.other_ref
  18.1 0.2 shard_map.87
  18.3 1.6 %collective-permute-start.6 = (bf16[48,1792]{1,0:T(8,128)(2,1)S(1)}, bf16[48,1792]{1,0:T(8,128)(2,1)S(1)}, u32[]{:S(2)}, u32[]{:S(2)}) collective-permute-start(bf16[48,1792]{1,0:T(8,128)(2,1)S(1)} %get-tuple-element.36.refs_0_), channel_id=1, source_target_pairs={{0,2},{1,3},{2,0},{3,1},{4,6},{5,7},{6,4},{7,5},{8,10},{9,11},{10,... | collective-permute-start | bytes 516104 | tf_op jit(solution)/shard_map/ppermute | solution.py:23
  19.9 0.0 collective-permute-done.5.other_ref
  19.9 0.2 shard_map.86
  20.1 0.8 %collective-permute-start.7 = (bf16[48,1536]{1,0:T(8,128)(2,1)S(1)}, bf16[48,1536]{1,0:T(8,128)(2,1)S(1)}, u32[]{:S(2)}, u32[]{:S(2)}) collective-permute-start(bf16[48,1536]{1,0:T(8,128)(2,1)S(1)} %get-tuple-element.37), channel_id=1, source_target_pairs={{0,2},{1,3},{2,0},{3,1},{4,6},{5,7},{6,4},{7,5},{8,10},{9,11},{10,... | collective-permute-start | bytes 442376 | tf_op jit(solution)/shard_map/ppermute | solution.py:23
  20.9 4.7 %collective-permute-done.6.refs_1_ = bf16[48,1792]{1,0:T(8,128)(2,1)S(1)} collective-permute-done((bf16[48,1792]{1,0:T(8,128)(2,1)S(1)}, bf16[48,1792]{1,0:T(8,128)(2,1)S(1)}, u32[]{:S(2)}, u32[]{:S(2)}) %collective-permute-start.6) | collective-permute-done | bytes 172064 | tf_op jit(solution)/shard_map/ppermute | solution.py:23
  25.6 0.0 copy-done
  25.6 0.3 shard_map.89.kept_ref
  25.9 0.1 collective-permute-start.9
  26.0 1.9 %collective-permute-done.7.refs_2_ = bf16[48,1536]{1,0:T(8,128)(2,1)S(1)} collective-permute-done((bf16[48,1536]{1,0:T(8,128)(2,1)S(1)}, bf16[48,1536]{1,0:T(8,128)(2,1)S(1)}, u32[]{:S(2)}, u32[]{:S(2)}) %collective-permute-start.7) | collective-permute-done | bytes 147488 | tf_op jit(solution)/shard_map/ppermute | solution.py:23
  27.9 0.3 shard_map.88.kept_ref
  28.2 0.0 copy-start.4
  28.2 0.0 copy-start.3
  28.2 0.1 collective-permute-start.8
  28.3 0.0 collective-permute-done.9.given_ref
  28.3 0.0 slice-done
  28.3 0.0 slice-done.1
  28.4 0.0 slice-done.2
  28.4 0.9 %shard_map.90.refs_0_ = f32[96,1536]{1,0:T(8,128)S(1)} custom-call(bf16[48,1536]{1,0:T(8,128)(2,1)S(1)} %shard_map.89.kept_ref, bf16[48,1536]{1,0:T(8,128)(2,1)S(1)} %collective-permute-done.9.given_ref, bf16[3072,1536]{1,0:T(8,128)(2,1)S(1)} %bitcast.4), custom_call_target="tpu_custom_call" | custom-call | flops 452984832 | bytes 589824 | tf_op jit(solution)/shard_map/pallas_call | solution.py:297
  29.3 0.4 collective-permute-done.8.given_ref
  29.7 0.9 %shard_map.91 = (f32[48,1536]{1,0:T(8,128)S(1)}, bf16[48,1536]{1,0:T(8,128)(2,1)S(1)}) custom-call(bf16[48,1536]{1,0:T(8,128)(2,1)S(1)} %shard_map.88.kept_ref, bf16[48,1536]{1,0:T(8,128)(2,1)S(1)} %collective-permute-done.8.given_ref, bf16[3072,1536]{1,0:T(8,128)(2,1)S(1)} %bitcast.4, f32[96,1536]{1,0:T(8,128)S(1)} %shard_map.90.refs_0_), custom_call_target="tpu_custom_call" | custom-call | flops 452984832 | bytes 589824 | tf_op jit(solution)/shard_map/pallas_call | solution.py:297
  30.6 1.6 %collective-permute-start.10 = (bf16[48,1536]{1,0:T(8,128)(2,1)S(1)}, bf16[48,1536]{1,0:T(8,128)(2,1)S(1)}, u32[]{:S(2)}, u32[]{:S(2)}) collective-permute-start(bf16[48,1536]{1,0:T(8,128)(2,1)S(1)} %get-tuple-element.40), channel_id=1, source_target_pairs={{0,4},{4,0},{8,12},{12,8},{16,20},{20,16},{24,28},{28,24},{1,5},{5... | collective-permute-start | bytes 442376 | tf_op jit(solution)/shard_map/ppermute | solution.py:23
  32.8 3.8 %collective-permute-done.10 = bf16[48,1536]{1,0:T(8,128)(2,1)S(1)} collective-permute-done((bf16[48,1536]{1,0:T(8,128)(2,1)S(1)}, bf16[48,1536]{1,0:T(8,128)(2,1)S(1)}, u32[]{:S(2)}, u32[]{:S(2)}) %collective-permute-start.10) | collective-permute-done | bytes 147488 | tf_op jit(solution)/shard_map/ppermute | solution.py:23
  36.6 2.2 %collective-permute-start.11 = (bf16[12,1536]{1,0:T(8,128)(2,1)S(1)}, bf16[12,1536]{1,0:T(8,128)(2,1)S(1)}, u32[]{:S(2)}, u32[]{:S(2)}) collective-permute-start(bf16[12,1536]{1,0:T(8,128)(2,1)S(1)} %get-tuple-element.43), channel_id=1, source_target_pairs={{0,24},{4,28},{8,16},{12,20},{16,8},{20,12},{24,0},{28,4},{1,25},{... | collective-permute-start | bytes 110600 | tf_op jit(solution)/shard_map/ppermute | solution.py:23
  38.8 0.0 collective-permute-start.12
  38.8 2.3 %collective-permute-start.13 = (bf16[12,1536]{1,0:T(8,128)(2,1)S(1)}, bf16[12,1536]{1,0:T(8,128)(2,1)S(1)}, u32[]{:S(2)}, u32[]{:S(2)}) collective-permute-start(bf16[12,1536]{1,0:T(8,128)(2,1)S(1)} %get-tuple-element.44), channel_id=1, source_target_pairs={{0,8},{4,12},{8,0},{12,4},{16,24},{20,28},{24,16},{28,20},{1,9},{5... | collective-permute-start | bytes 110600 | tf_op jit(solution)/shard_map/ppermute | solution.py:23
  41.1 0.0 copy-done.4
  41.1 1.7 %collective-permute-done.11 = bf16[12,1536]{1,0:T(8,128)(2,1)S(1)} collective-permute-done((bf16[12,1536]{1,0:T(8,128)(2,1)S(1)}, bf16[12,1536]{1,0:T(8,128)(2,1)S(1)}, u32[]{:S(2)}, u32[]{:S(2)}) %collective-permute-start.11) | collective-permute-done | bytes 36896 | tf_op jit(solution)/shard_map/ppermute | solution.py:23
  42.8 1.5 %collective-permute-done.12 = bf16[12,1536]{1,0:T(8,128)(2,1)S(1)} collective-permute-done((bf16[12,1536]{1,0:T(8,128)(2,1)S(1)}, bf16[12,1536]{1,0:T(8,128)(2,1)S(1)}, u32[]{:S(2)}, u32[]{:S(2)}) %collective-permute-start.12) | collective-permute-done | bytes 36896 | tf_op jit(solution)/shard_map/ppermute | solution.py:23
  44.2 0.0 collective-permute-done.13
  44.3 0.0 copy-done.3
  44.3 0.7 %fusion.4 = bf16[12,1536]{1,0:T(8,128)(2,1)} fusion(f32[48,1536]{1,0:T(8,128)S(1)} %get-tuple-element.42, bf16[12,1536]{1,0:T(8,128)(2,1)S(1)} %collective-permute-done.13, bf16[12,1536]{1,0:T(8,128)(2,1)S(1)} %collective-permute-done.12, bf16[12,1536]{1,0:T(8,128)(2,1)S(1)} %collective-permute-done.11, f32[1536]{0:T(1024)S(1)} %copy-done.3, ...), kind=kLoop, calls=%fused_computation.7 | loop fusion | flops 165888 | bytes 227376 | tf_op jit(solution)/shard_map/convert_element_type | solution.py:317
  (5 shorter events, 0.1 us)
Async XLA Ops:
  0.0 10.3 %copy-start.2 = (bf16[12,1536]{1,0:T(8,128)(2,1)S(1)}, bf16[12,1536]{1,0:T(8,128)(2,1)}, u32[]{:S(2)}) copy-start(bf16[12,1536]{1,0:T(8,128)(2,1)} %param.8) | copy-start | bytes 110596
  0.0 11.9 %copy-start.1 = (f32[1536]{0:T(1024)S(1)}, f32[1536]{0:T(1024)}, u32[]{:S(2)}) copy-start(f32[1536]{0:T(1024)} %gain_ref.1) | copy-start | bytes 18436
  0.0 8.0 %collective-permute-start = (bf16[12,1536]{1,0:T(8,128)(2,1)}, bf16[12,1536]{1,0:T(8,128)(2,1)S(1)}, u32[]{:S(2)}, u32[]{:S(2)}) collective-permute-start(bf16[12,1536]{1,0:T(8,128)(2,1)} %param.8), channel_id=1, source_target_pairs={{0,24},{4,28},{8,16},{12,20},{16,8},{20,12},{24,0},{28,4},{1,25},{... | collective-permute-start | bytes 110600 | tf_op jit(solution)/shard_map/ppermute | solution.py:23
  5.1 5.2 %collective-permute-start.1 = (bf16[12,1536]{1,0:T(8,128)(2,1)}, bf16[12,1536]{1,0:T(8,128)(2,1)S(1)}, u32[]{:S(2)}, u32[]{:S(2)}) collective-permute-start(bf16[12,1536]{1,0:T(8,128)(2,1)} %param.8), channel_id=1, source_target_pairs={{0,16},{4,20},{8,24},{12,28},{16,0},{20,4},{24,8},{28,12},{1,17},{... | collective-permute-start | bytes 110600 | tf_op jit(solution)/shard_map/ppermute | solution.py:23
  5.1 5.2 %collective-permute-start.2 = (bf16[12,1536]{1,0:T(8,128)(2,1)}, bf16[12,1536]{1,0:T(8,128)(2,1)S(1)}, u32[]{:S(2)}, u32[]{:S(2)}) collective-permute-start(bf16[12,1536]{1,0:T(8,128)(2,1)} %param.8), channel_id=1, source_target_pairs={{0,8},{4,12},{8,0},{12,4},{16,24},{20,28},{24,16},{28,20},{1,9},{5... | collective-permute-start | bytes 110600 | tf_op jit(solution)/shard_map/ppermute | solution.py:23
  10.3 15.3 %copy-start = (f32[3072]{0:T(1024)S(1)}, f32[3072]{0:T(1024)}, u32[]{:S(2)}) copy-start(f32[3072]{0:T(1024)} %param.13) | copy-start | bytes 36868
  10.3 5.2 %collective-permute-start.3 = (bf16[48,1536]{1,0:T(8,128)(2,1)S(1)}, bf16[48,1536]{1,0:T(8,128)(2,1)S(1)}, u32[]{:S(2)}, u32[]{:S(2)}) collective-permute-start(bf16[48,1536]{1,0:T(8,128)(2,1)S(1)} %pad_maximum_fusion.near_ref), channel_id=1, source_target_pairs={{0,4},{4,0},{8,12},{12,8},{16,20},{20,16},{24,28},{28,24},{1,5},{5... | collective-permute-start | bytes 442376 | tf_op jit(solution)/shard_map/ppermute | solution.py:23
  11.9 16.5 %slice-start = ((s8[9437184]{0:T(1024)(128)(4,1)}), s8[4194304]{0:T(1024)(128)(4,1)S(1)}, s32[]{:S(2)}) async-start(s8[9437184]{0:T(1024)(128)(4,1)} %bitcast.3), calls=%async_computation | async-start | bytes 8388608
  11.9 16.5 %slice-start.1 = ((s8[9437184]{0:T(1024)(128)(4,1)}), s8[4194304]{0:T(1024)(128)(4,1)S(1)}, s32[]{:S(2)}) async-start(s8[9437184]{0:T(1024)(128)(4,1)} %bitcast.3), calls=%async_computation.1 | async-start | bytes 8388608
  15.5 12.8 %slice-start.2 = ((s8[9437184]{0:T(1024)(128)(4,1)}), s8[1048576]{0:T(1024)(128)(4,1)S(1)}, s32[]{:S(2)}) async-start(s8[9437184]{0:T(1024)(128)(4,1)} %bitcast.3), calls=%async_computation.2 | async-start | bytes 2097152
  16.6 1.5 %collective-permute-start.4 = (bf16[48,1792]{1,0:T(8,128)(2,1)S(1)}, bf16[48,1792]{1,0:T(8,128)(2,1)S(1)}, u32[]{:S(2)}, u32[]{:S(2)}) collective-permute-start(bf16[48,1792]{1,0:T(8,128)(2,1)S(1)} %get-tuple-element.32), channel_id=1, source_target_pairs={{0,1},{1,0},{2,3},{3,2},{4,5},{5,4},{6,7},{7,6},{8,9},{9,8},{10,11... | collective-permute-start | bytes 516104 | tf_op jit(solution)/shard_map/ppermute | solution.py:23
  17.5 2.4 %collective-permute-start.5 = (bf16[48,1536]{1,0:T(8,128)(2,1)S(1)}, bf16[48,1536]{1,0:T(8,128)(2,1)S(1)}, u32[]{:S(2)}, u32[]{:S(2)}) collective-permute-start(bf16[48,1536]{1,0:T(8,128)(2,1)S(1)} %get-tuple-element.33), channel_id=1, source_target_pairs={{0,1},{1,0},{2,3},{3,2},{4,5},{5,4},{6,7},{7,6},{8,9},{9,8},{10,11... | collective-permute-start | bytes 442376 | tf_op jit(solution)/shard_map/ppermute | solution.py:23
  18.3 7.3 %collective-permute-start.6 = (bf16[48,1792]{1,0:T(8,128)(2,1)S(1)}, bf16[48,1792]{1,0:T(8,128)(2,1)S(1)}, u32[]{:S(2)}, u32[]{:S(2)}) collective-permute-start(bf16[48,1792]{1,0:T(8,128)(2,1)S(1)} %get-tuple-element.36.refs_0_), channel_id=1, source_target_pairs={{0,2},{1,3},{2,0},{3,1},{4,6},{5,7},{6,4},{7,5},{8,10},{9,11},{10,... | collective-permute-start | bytes 516104 | tf_op jit(solution)/shard_map/ppermute | solution.py:23
  20.1 7.8 %collective-permute-start.7 = (bf16[48,1536]{1,0:T(8,128)(2,1)S(1)}, bf16[48,1536]{1,0:T(8,128)(2,1)S(1)}, u32[]{:S(2)}, u32[]{:S(2)}) collective-permute-start(bf16[48,1536]{1,0:T(8,128)(2,1)S(1)} %get-tuple-element.37), channel_id=1, source_target_pairs={{0,2},{1,3},{2,0},{3,1},{4,6},{5,7},{6,4},{7,5},{8,10},{9,11},{10,... | collective-permute-start | bytes 442376 | tf_op jit(solution)/shard_map/ppermute | solution.py:23
  25.9 2.4 %collective-permute-start.9 = (bf16[48,1536]{1,0:T(8,128)(2,1)S(1)}, bf16[48,1536]{1,0:T(8,128)(2,1)S(1)}, u32[]{:S(2)}, u32[]{:S(2)}) collective-permute-start(bf16[48,1536]{1,0:T(8,128)(2,1)S(1)} %shard_map.89.kept_ref), channel_id=1, source_target_pairs={{0,1},{1,0},{2,3},{3,2},{4,5},{5,4},{6,7},{7,6},{8,9},{9,8},{10,11... | collective-permute-start | bytes 442376 | tf_op jit(solution)/shard_map/ppermute | solution.py:23
  28.2 12.9 %copy-start.4 = (s32[12]{0:T(128)S(1)}, s32[12]{0:T(128)}, u32[]{:S(2)}) copy-start(s32[12]{0:T(128)} %param.10) | copy-start | bytes 148
  28.2 16.0 %copy-start.3 = (f32[1536]{0:T(1024)S(1)}, f32[1536]{0:T(1024)}, u32[]{:S(2)}) copy-start(f32[1536]{0:T(1024)} %param.15) | copy-start | bytes 18436
  28.2 1.4 %collective-permute-start.8 = (bf16[48,1536]{1,0:T(8,128)(2,1)S(1)}, bf16[48,1536]{1,0:T(8,128)(2,1)S(1)}, u32[]{:S(2)}, u32[]{:S(2)}) collective-permute-start(bf16[48,1536]{1,0:T(8,128)(2,1)S(1)} %shard_map.88.kept_ref), channel_id=1, source_target_pairs={{0,1},{1,0},{2,3},{3,2},{4,5},{5,4},{6,7},{7,6},{8,9},{9,8},{10,11... | collective-permute-start | bytes 442376 | tf_op jit(solution)/shard_map/ppermute | solution.py:23
  30.6 6.0 %collective-permute-start.10 = (bf16[48,1536]{1,0:T(8,128)(2,1)S(1)}, bf16[48,1536]{1,0:T(8,128)(2,1)S(1)}, u32[]{:S(2)}, u32[]{:S(2)}) collective-permute-start(bf16[48,1536]{1,0:T(8,128)(2,1)S(1)} %get-tuple-element.40), channel_id=1, source_target_pairs={{0,4},{4,0},{8,12},{12,8},{16,20},{20,16},{24,28},{28,24},{1,5},{5... | collective-permute-start | bytes 442376 | tf_op jit(solution)/shard_map/ppermute | solution.py:23
  36.6 6.1 %collective-permute-start.11 = (bf16[12,1536]{1,0:T(8,128)(2,1)S(1)}, bf16[12,1536]{1,0:T(8,128)(2,1)S(1)}, u32[]{:S(2)}, u32[]{:S(2)}) collective-permute-start(bf16[12,1536]{1,0:T(8,128)(2,1)S(1)} %get-tuple-element.43), channel_id=1, source_target_pairs={{0,24},{4,28},{8,16},{12,20},{16,8},{20,12},{24,0},{28,4},{1,25},{... | collective-permute-start | bytes 110600 | tf_op jit(solution)/shard_map/ppermute | solution.py:23
  38.8 5.4 %collective-permute-start.12 = (bf16[12,1536]{1,0:T(8,128)(2,1)S(1)}, bf16[12,1536]{1,0:T(8,128)(2,1)S(1)}, u32[]{:S(2)}, u32[]{:S(2)}) collective-permute-start(bf16[12,1536]{1,0:T(8,128)(2,1)S(1)} %get-tuple-element.45), channel_id=1, source_target_pairs={{0,16},{4,20},{8,24},{12,28},{16,0},{20,4},{24,8},{28,12},{1,17},{... | collective-permute-start | bytes 110600 | tf_op jit(solution)/shard_map/ppermute | solution.py:23
  38.8 5.4 %collective-permute-start.13 = (bf16[12,1536]{1,0:T(8,128)(2,1)S(1)}, bf16[12,1536]{1,0:T(8,128)(2,1)S(1)}, u32[]{:S(2)}, u32[]{:S(2)}) collective-permute-start(bf16[12,1536]{1,0:T(8,128)(2,1)S(1)} %get-tuple-element.44), channel_id=1, source_target_pairs={{0,8},{4,12},{8,0},{12,4},{16,24},{20,28},{24,16},{28,20},{1,9},{5... | collective-permute-start | bytes 110600 | tf_op jit(solution)/shard_map/ppermute | solution.py:23

commit v5 on v4

--- a/solution.py
+++ b/solution.py
@@ -41,7 +41,7 @@
         scratch_shapes=list(scratch),
         compiler_params=pltpu.CompilerParams(vmem_limit_bytes=limit * MIB),
         cost_estimate=pl.CostEstimate(
-            flops=flops, bytes_accessed=sum(o.size * 4 for o in outs), transcendentals=0
+            flops=8 * flops, bytes_accessed=0, transcendentals=0
         ),
     )
 
@@ -97,19 +97,26 @@
 
 
 def load_last_kernel(start, gain_ref, *refs):
-    weight_ref, out_ref, row_ref, packed_ref, scratch, sem = refs[-6:]
+    weight_ref, out_ref, row_ref, packed_ref, scratch, sems = refs[-6:]
     width = out_ref.shape[1]
-    copy = pltpu.make_async_copy(weight_ref.at[:, pl.ds(start, width)], out_ref, sem)
-    copy.start()
+    tile = tile_of(width)
+    tiles = range(0, width, tile)
+    copies = [
+        pltpu.make_async_copy(
+            weight_ref.at[:, pl.ds(start + at, tile)], out_ref.at[:, pl.ds(at, tile)], sems.at[at // tile]
+        )
+        for at in tiles
+    ]
+    for copy in copies:
+        copy.start()
     gain = gain_ref[...][None, :]
     high = gain.astype(jnp.bfloat16).astype(jnp.float32)
     row = lax.broadcasted_iota(jnp.int32, (16, gain.shape[1]), 0)
     rows = jnp.where(row == 0, high, jnp.where(row == 1, gain - high, 0.0)).astype(jnp.bfloat16)
-    tile = tile_of(width)
     for part, loaded in enumerate(refs[:-6] + (out_ref,)):
-        if loaded is out_ref:
-            copy.wait()
-        for at in range(0, width, tile):
+        for at, copy in zip(tiles, copies):
+            if loaded is out_ref:
+                copy.wait()
             product = jnp.dot(rows, loaded[:, at:at + tile], preferred_element_type=jnp.float32)
             row_ref[:, part * width + at:part * width + at + tile] = product[0:1] + product[1:2]
     pack_row(lambda at: row_ref[:, at:at + LANES], row_ref.shape[1], scratch, packed_ref)
@@ -249,7 +256,7 @@
         functools.partial(load_last_kernel, starts[-1]),
         [((block_width, width), bf16), ((1, hidden_width), f32), ((half, side), bf16)],
         [in_vmem] * parts + [in_hbm],
-        [pltpu.VMEM((half, side), f32), copied],
+        [pltpu.VMEM((half, side), f32), copied((width // tile_of(width),))],
         flops=32 * up_weight.size,
         limit=40,
     )(norm_gain, *loaded, up_weight)
@@ -305,12 +312,17 @@
         )(active, swap(active, "feat", 1), down_weight, *total)
     near_sum, far_sum = total
 
-    near_sum = near_sum + swap(far_sum, "tok", 1)
-    blocks = near_sum.reshape(tok_size // 2, tok_rows, block_width)
-    summed = blocks[0]
-    sent = blocks.astype(bf16)
-    for part in [swap(sent[order.index(mask)], "tok", mask) for mask in reversed(masks)]:
-        summed = summed + part
+    def rows_of(array, masks):
+        at = [order.index(mask) * tok_rows for mask in masks]
+        return jnp.concatenate([array[start:start + tok_rows] for start in at])
+
+    first, second = order[1:1 + len(order) // 2], order[1 + len(order) // 2:] + [0]
+    summed = 0
+    for group in (first, second):
+        total = rows_of(near_sum, group) + swap(rows_of(far_sum, group), "tok", 1)
+        for at, mask in enumerate(group):
+            block = total[at * tok_rows:(at + 1) * tok_rows]
+            summed = summed + (swap(block.astype(bf16), "tok", mask) if mask else block)
 
     positions = jnp.arange(tok_rows, dtype=jnp.int32)
     valid_rows = ((positions // FRAME_TOK < frame_counts) & (patch_mask == 1)).astype(f32)

time: 45.1 us -> 44.4 us (0.984)
  Pallas kernels: 10.4 us -> 9.92 us
    pallas_call x1, Pallas kernels: 3.36 us -> 2.86 us  [per_device(): call(functools.partial(load_last_kernel, starts[-1]), [((block_width, wid...]
    ppermute x14 -> x15, waiting for transfers between devices: 16.4 us -> 16.1 us  [swap(): return lax.ppermute(block, axis, [(i, i ^ mask) for i in range(size)])]
    ppermute x14 -> x15, starting transfers between devices: 16.4 us -> 16.4 us  [swap(): return lax.ppermute(block, axis, [(i, i ^ mask) for i in range(size)])]
  transfers between devices with their start and end apart: 14 -> 15, of which waited for: 8 -> 10; matrix products, arithmetic and copies ran while one was open for 0% -> 0% of each run, Pallas kernels for 19% -> 18%
where the time goes in v5:
time: 44.4 us; the launch traced here: 44.2 us
  starting transfers between devices  16.4 us (37%)
  waiting for transfers between devices  16.1 us (36%)
  Pallas kernels  9.92 us (22%)
  between operations  0.89 us (2%)
  other arithmetic  0.83 us (2%)
    ppermute x15, starting transfers between devices, swap(): return lax.ppermute(block, axis, [(i, i ^ mask) for i in range(size)])  16.4 us
    ppermute x15, waiting for transfers between devices, swap(): return lax.ppermute(block, axis, [(i, i ^ mask) for i in range(size)])  16.1 us
    pallas_call x1, Pallas kernels, per_device(): call(functools.partial(load_last_kernel, starts[-1]), [((block_width, wid...  2.86 us
    pallas_call x1, Pallas kernels, per_device(): call(functools.partial(load_kernel, start), [((block_width, width), bf16)...  2.34 us
    pallas_call x2, Pallas kernels, per_device(): call(functools.partial(down_kernel, start, last), [((half, block_width),...  1.78 us
    pallas_call x1, Pallas kernels, per_device(): call(up_kernel, [((2 * half, block_width), bf16), ((half, LANES), bf16)]...  1.01 us
  transfers between devices with their start and end apart: 15, of which 10 were waited for; matrix products, arithmetic and copies ran while one was open for 0% of the time, Pallas kernels for 18%

profile of v5, /device:TPU:0, one launch (start us, length us, event | category | flops | bytes accessed | tf_op | source)
XLA Modules:
  0.0 44.2 jit_solution(81366128932925463)
XLA Ops:
  0.0 0.0 copy-start.2
  0.0 0.0 copy-start.1
  0.0 5.0 %collective-permute-start = (bf16[12,1536]{1,0:T(8,128)(2,1)}, bf16[12,1536]{1,0:T(8,128)(2,1)S(1)}, u32[]{:S(2)}, u32[]{:S(2)}) collective-permute-start(bf16[12,1536]{1,0:T(8,128)(2,1)} %param.8), channel_id=1, source_target_pairs={{0,24},{4,28},{8,16},{12,20},{16,8},{20,12},{24,0},{28,4},{1,25},{... | collective-permute-start | bytes 110600 | tf_op jit(solution)/shard_map/ppermute | solution.py:23
  5.1 0.0 collective-permute-start.1
  5.1 0.6 %collective-permute-start.2 = (bf16[12,1536]{1,0:T(8,128)(2,1)}, bf16[12,1536]{1,0:T(8,128)(2,1)S(1)}, u32[]{:S(2)}, u32[]{:S(2)}) collective-permute-start(bf16[12,1536]{1,0:T(8,128)(2,1)} %param.8), channel_id=1, source_target_pairs={{0,8},{4,12},{8,0},{12,4},{16,24},{20,28},{24,16},{28,20},{1,9},{5... | collective-permute-start | bytes 110600 | tf_op jit(solution)/shard_map/ppermute | solution.py:23
  5.7 2.3 %shard_map.82.refs_0_.weight_ref = bf16[1536,1536]{1,0:T(8,128)(2,1)S(1)} custom-call(bf16[1536,3072]{1,0:T(8,128)(2,1)} %refs_1_.1), custom_call_target="tpu_custom_call" | custom-call | tf_op jit(solution)/shard_map/pallas_call | solution.py:242
  8.0 0.0 collective-permute-done
  8.1 2.2 %collective-permute-done.1 = bf16[12,1536]{1,0:T(8,128)(2,1)S(1)} collective-permute-done((bf16[12,1536]{1,0:T(8,128)(2,1)}, bf16[12,1536]{1,0:T(8,128)(2,1)S(1)}, u32[]{:S(2)}, u32[]{:S(2)}) %collective-permute-start.1) | collective-permute-done | bytes 36896 | tf_op jit(solution)/shard_map/ppermute | solution.py:23
  10.3 0.0 collective-permute-done.2
  10.3 0.0 copy-done.2
  10.3 1.6 %collective-permute-start.3 = (bf16[48,1536]{1,0:T(8,128)(2,1)S(1)}, bf16[48,1536]{1,0:T(8,128)(2,1)S(1)}, u32[]{:S(2)}, u32[]{:S(2)}) collective-permute-start(bf16[48,1536]{1,0:T(8,128)(2,1)S(1)} %pad_maximum_fusion.near_ref), channel_id=1, source_target_pairs={{0,4},{4,0},{8,12},{12,8},{16,20},{20,16},{24,28},{28,24},{1,5},{5... | collective-permute-start | bytes 442376 | tf_op jit(solution)/shard_map/ppermute | solution.py:23
  11.9 0.0 copy-done.1
  11.9 2.9 %shard_map.83 = (bf16[1536,1536]{1,0:T(8,128)(2,1)S(1)}, f32[1,3072]{1,0:T(1,128)S(1)}, bf16[48,128]{1,0:T(8,128)(2,1)S(1)}) custom-call(f32[1536]{0:T(1024)S(1)} %copy-done.1, bf16[1536,1536]{1,0:T(8,128)(2,1)S(1)} %shard_map.82.refs_0_.weight_ref, bf16[1536,3072]{1,0:T(8,128)(2,1)} %refs_1_.1), custom_call_target="tpu_custom_call" | custom-call | flops 1207959552 | tf_op jit(solution)/shard_map/pallas_call | solution.py:255
  14.7 0.8 %collective-permute-done.3.far_ref = bf16[48,1536]{1,0:T(8,128)(2,1)S(1)} collective-permute-done((bf16[48,1536]{1,0:T(8,128)(2,1)S(1)}, bf16[48,1536]{1,0:T(8,128)(2,1)S(1)}, u32[]{:S(2)}, u32[]{:S(2)}) %collective-permute-start.3) | collective-permute-done | bytes 147488 | tf_op jit(solution)/shard_map/ppermute | solution.py:23
  15.5 0.0 slice-start
  15.5 0.0 slice-start.1
  15.5 1.0 %shard_map.84 = (bf16[96,1536]{1,0:T(8,128)(2,1)S(1)}, bf16[48,128]{1,0:T(8,128)(2,1)S(1)}, f32[48,1536]{1,0:T(8,128)S(1)}, bf16[48,1792]{1,0:T(8,128)(2,1)S(1)}) custom-call(bf16[48,1536]{1,0:T(8,128)(2,1)S(1)} %pad_maximum_fusion.near_ref, bf16[48,1536]{1,0:T(8,128)(2,1)S(1)} %collective-permute-done.3.far_ref, f32[1536]{0:T(1024)S(1)} %copy-done.1, ...), custom_call_target="tpu_custom_call" | custom-call | flops 3623878656 | tf_op jit(solution)/shard_map/pallas_call | solution.py:270
  16.5 0.0 copy-start
  16.6 0.1 collective-permute-start.4
  16.6 1.4 %collective-permute-done.4.packed_ref.other_ref = bf16[48,1792]{1,0:T(8,128)(2,1)S(1)} collective-permute-done((bf16[48,1792]{1,0:T(8,128)(2,1)S(1)}, bf16[48,1792]{1,0:T(8,128)(2,1)S(1)}, u32[]{:S(2)}, u32[]{:S(2)}) %collective-permute-start.4) | collective-permute-done | bytes 172064 | tf_op jit(solution)/shard_map/ppermute | solution.py:23
  18.0 0.2 shard_map.87
  18.2 1.6 %collective-permute-start.6 = (bf16[48,1792]{1,0:T(8,128)(2,1)S(1)}, bf16[48,1792]{1,0:T(8,128)(2,1)S(1)}, u32[]{:S(2)}, u32[]{:S(2)}) collective-permute-start(bf16[48,1792]{1,0:T(8,128)(2,1)S(1)} %get-tuple-element.36.refs_0_), channel_id=1, source_target_pairs={{0,2},{1,3},{2,0},{3,1},{4,6},{5,7},{6,4},{7,5},{8,10},{9,11},{10,... | collective-permute-start | bytes 516104 | tf_op jit(solution)/shard_map/ppermute | solution.py:23
  19.8 0.0 slice-start.2
  19.8 0.9 %shard_map.85 = (f32[48,1536]{1,0:T(8,128)S(1)}, bf16[48,1536]{1,0:T(8,128)(2,1)S(1)}) custom-call(bf16[96,1536]{1,0:T(8,128)(2,1)S(1)} %get-tuple-element.27.rows_ref, bf16[1536,1536]{1,0:T(8,128)(2,1)S(1)} %get-tuple-element.28.weight_ref), custom_call_target="tpu_custom_call" | custom-call | flops 3623878656 | tf_op jit(solution)/shard_map/pallas_call | solution.py:277
  20.7 0.1 collective-permute-start.5
  20.8 1.4 %collective-permute-done.5.other_ref = bf16[48,1536]{1,0:T(8,128)(2,1)S(1)} collective-permute-done((bf16[48,1536]{1,0:T(8,128)(2,1)S(1)}, bf16[48,1536]{1,0:T(8,128)(2,1)S(1)}, u32[]{:S(2)}, u32[]{:S(2)}) %collective-permute-start.5) | collective-permute-done | bytes 147488 | tf_op jit(solution)/shard_map/ppermute | solution.py:23
  22.1 0.2 shard_map.86
  22.3 0.6 %collective-permute-start.7 = (bf16[48,1536]{1,0:T(8,128)(2,1)S(1)}, bf16[48,1536]{1,0:T(8,128)(2,1)S(1)}, u32[]{:S(2)}, u32[]{:S(2)}) collective-permute-start(bf16[48,1536]{1,0:T(8,128)(2,1)S(1)} %get-tuple-element.37), channel_id=1, source_target_pairs={{0,2},{1,3},{2,0},{3,1},{4,6},{5,7},{6,4},{7,5},{8,10},{9,11},{10,... | collective-permute-start | bytes 442376 | tf_op jit(solution)/shard_map/ppermute | solution.py:23
  22.9 1.8 %collective-permute-done.6.refs_1_ = bf16[48,1792]{1,0:T(8,128)(2,1)S(1)} collective-permute-done((bf16[48,1792]{1,0:T(8,128)(2,1)S(1)}, bf16[48,1792]{1,0:T(8,128)(2,1)S(1)}, u32[]{:S(2)}, u32[]{:S(2)}) %collective-permute-start.6) | collective-permute-done | bytes 172064 | tf_op jit(solution)/shard_map/ppermute | solution.py:23
  24.7 0.0 copy-done
  24.7 0.3 shard_map.89.kept_ref
  25.1 0.1 collective-permute-start.9
  25.8 2.5 %collective-permute-done.7.refs_2_ = bf16[48,1536]{1,0:T(8,128)(2,1)S(1)} collective-permute-done((bf16[48,1536]{1,0:T(8,128)(2,1)S(1)}, bf16[48,1536]{1,0:T(8,128)(2,1)S(1)}, u32[]{:S(2)}, u32[]{:S(2)}) %collective-permute-start.7) | collective-permute-done | bytes 147488 | tf_op jit(solution)/shard_map/ppermute | solution.py:23
  28.3 0.3 shard_map.88.kept_ref
  28.6 0.1 collective-permute-start.8
  28.7 0.0 collective-permute-done.9.given_ref
  28.7 0.0 slice-done
  28.7 0.0 slice-done.1
  28.7 0.0 slice-done.2
  28.8 0.9 %shard_map.90.refs_0_ = f32[96,1536]{1,0:T(8,128)S(1)} custom-call(bf16[48,1536]{1,0:T(8,128)(2,1)S(1)} %shard_map.89.kept_ref, bf16[48,1536]{1,0:T(8,128)(2,1)S(1)} %collective-permute-done.9.given_ref, bf16[3072,1536]{1,0:T(8,128)(2,1)S(1)} %bitcast.6), custom_call_target="tpu_custom_call" | custom-call | flops 3623878656 | tf_op jit(solution)/shard_map/pallas_call | solution.py:304
  29.6 0.0 copy-start.4
  29.7 0.0 copy-start.3
  29.7 0.4 collective-permute-done.8.given_ref
  30.1 0.9 %shard_map.91 = (f32[48,1536]{1,0:T(8,128)S(1)}, bf16[48,1536]{1,0:T(8,128)(2,1)S(1)}) custom-call(bf16[48,1536]{1,0:T(8,128)(2,1)S(1)} %shard_map.88.kept_ref, bf16[48,1536]{1,0:T(8,128)(2,1)S(1)} %collective-permute-done.8.given_ref, bf16[3072,1536]{1,0:T(8,128)(2,1)S(1)} %bitcast.6, f32[96,1536]{1,0:T(8,128)S(1)} %shard_map.90.refs_0_), custom_call_target="tpu_custom_call" | custom-call | flops 3623878656 | tf_op jit(solution)/shard_map/pallas_call | solution.py:304
  31.0 1.6 %collective-permute-start.10 = (bf16[24,1536]{1,0:T(8,128)(2,1)S(1)}, bf16[24,1536]{1,0:T(8,128)(2,1)S(1)}, u32[]{:S(2)}, u32[]{:S(2)}) collective-permute-start(bf16[24,1536]{1,0:T(8,128)(2,1)S(1)} %concatenate.17), channel_id=1, source_target_pairs={{0,4},{4,0},{8,12},{12,8},{16,20},{20,16},{24,28},{28,24},{1,5},{5... | collective-permute-start | bytes 221192 | tf_op jit(solution)/shard_map/ppermute | solution.py:23
  32.6 0.6 %collective-permute-start.13 = (bf16[24,1536]{1,0:T(8,128)(2,1)S(1)}, bf16[24,1536]{1,0:T(8,128)(2,1)S(1)}, u32[]{:S(2)}, u32[]{:S(2)}) collective-permute-start(bf16[24,1536]{1,0:T(8,128)(2,1)S(1)} %pad_maximum_fusion.1), channel_id=1, source_target_pairs={{0,4},{4,0},{8,12},{12,8},{16,20},{20,16},{24,28},{28,24},{1,5},{5... | collective-permute-start | bytes 221192 | tf_op jit(solution)/shard_map/ppermute | solution.py:23
  33.2 2.6 %collective-permute-done.10 = bf16[24,1536]{1,0:T(8,128)(2,1)S(1)} collective-permute-done((bf16[24,1536]{1,0:T(8,128)(2,1)S(1)}, bf16[24,1536]{1,0:T(8,128)(2,1)S(1)}, u32[]{:S(2)}, u32[]{:S(2)}) %collective-permute-start.10) | collective-permute-done | bytes 73760 | tf_op jit(solution)/shard_map/ppermute | solution.py:23
  35.9 2.2 %collective-permute-start.11 = (bf16[12,1536]{1,0:T(8,128)(2,1)S(1)}, bf16[12,1536]{1,0:T(8,128)(2,1)S(1)}, u32[]{:S(2)}, u32[]{:S(2)}) collective-permute-start(bf16[12,1536]{1,0:T(8,128)(2,1)S(1)} %get-tuple-element.46), channel_id=1, source_target_pairs={{0,24},{4,28},{8,16},{12,20},{16,8},{20,12},{24,0},{28,4},{1,25},{... | collective-permute-start | bytes 110600 | tf_op jit(solution)/shard_map/ppermute | solution.py:23
  38.1 0.0 collective-permute-start.12
  38.1 0.0 collective-permute-done.13
  38.1 2.3 %collective-permute-start.14 = (bf16[12,1536]{1,0:T(8,128)(2,1)S(1)}, bf16[12,1536]{1,0:T(8,128)(2,1)S(1)}, u32[]{:S(2)}, u32[]{:S(2)}) collective-permute-start(bf16[12,1536]{1,0:T(8,128)(2,1)S(1)} %slice.53), channel_id=1, source_target_pairs={{0,8},{4,12},{8,0},{12,4},{16,24},{20,28},{24,16},{28,20},{1,9},{5... | collective-permute-start | bytes 110600 | tf_op jit(solution)/shard_map/ppermute | solution.py:23
  40.5 0.0 copy-done.4
  40.5 1.9 %collective-permute-done.11 = bf16[12,1536]{1,0:T(8,128)(2,1)S(1)} collective-permute-done((bf16[12,1536]{1,0:T(8,128)(2,1)S(1)}, bf16[12,1536]{1,0:T(8,128)(2,1)S(1)}, u32[]{:S(2)}, u32[]{:S(2)}) %collective-permute-start.11) | collective-permute-done | bytes 36896 | tf_op jit(solution)/shard_map/ppermute | solution.py:23
  42.3 1.2 %collective-permute-done.12 = bf16[12,1536]{1,0:T(8,128)(2,1)S(1)} collective-permute-done((bf16[12,1536]{1,0:T(8,128)(2,1)S(1)}, bf16[12,1536]{1,0:T(8,128)(2,1)S(1)}, u32[]{:S(2)}, u32[]{:S(2)}) %collective-permute-start.12) | collective-permute-done | bytes 36896 | tf_op jit(solution)/shard_map/ppermute | solution.py:23
  43.5 0.0 collective-permute-done.14
  43.5 0.0 copy-done.3
  43.5 0.7 %fusion.2 = bf16[12,1536]{1,0:T(8,128)(2,1)} fusion(f32[24,1536]{1,0:T(8,128)S(1)} %maximum_add_fusion, f32[1536]{0:T(1024)S(1)} %copy-done.3, bf16[12,1536]{1,0:T(8,128)(2,1)S(1)} %collective-permute-done.14, bf16[12,1536]{1,0:T(8,128)(2,1)S(1)} %collective-permute-done.11, bf16[12,1536]{1,0:T(8,128)(2,1)S(1)} %collective-permute-done.12, ...), kind=kLoop, calls=%fused_computation.6 | loop fusion | flops 129024 | bytes 227376 | tf_op jit(solution)/shard_map/convert_element_type | solution.py:329
  (11 shorter events, 0.2 us)
Async XLA Ops:
  0.0 10.3 %copy-start.2 = (bf16[12,1536]{1,0:T(8,128)(2,1)S(1)}, bf16[12,1536]{1,0:T(8,128)(2,1)}, u32[]{:S(2)}) copy-start(bf16[12,1536]{1,0:T(8,128)(2,1)} %param.8) | copy-start | bytes 110596
  0.0 11.9 %copy-start.1 = (f32[1536]{0:T(1024)S(1)}, f32[1536]{0:T(1024)}, u32[]{:S(2)}) copy-start(f32[1536]{0:T(1024)} %gain_ref.1) | copy-start | bytes 18436
  0.0 8.0 %collective-permute-start = (bf16[12,1536]{1,0:T(8,128)(2,1)}, bf16[12,1536]{1,0:T(8,128)(2,1)S(1)}, u32[]{:S(2)}, u32[]{:S(2)}) collective-permute-start(bf16[12,1536]{1,0:T(8,128)(2,1)} %param.8), channel_id=1, source_target_pairs={{0,24},{4,28},{8,16},{12,20},{16,8},{20,12},{24,0},{28,4},{1,25},{... | collective-permute-start | bytes 110600 | tf_op jit(solution)/shard_map/ppermute | solution.py:23
  5.1 5.2 %collective-permute-start.1 = (bf16[12,1536]{1,0:T(8,128)(2,1)}, bf16[12,1536]{1,0:T(8,128)(2,1)S(1)}, u32[]{:S(2)}, u32[]{:S(2)}) collective-permute-start(bf16[12,1536]{1,0:T(8,128)(2,1)} %param.8), channel_id=1, source_target_pairs={{0,16},{4,20},{8,24},{12,28},{16,0},{20,4},{24,8},{28,12},{1,17},{... | collective-permute-start | bytes 110600 | tf_op jit(solution)/shard_map/ppermute | solution.py:23
  5.1 5.2 %collective-permute-start.2 = (bf16[12,1536]{1,0:T(8,128)(2,1)}, bf16[12,1536]{1,0:T(8,128)(2,1)S(1)}, u32[]{:S(2)}, u32[]{:S(2)}) collective-permute-start(bf16[12,1536]{1,0:T(8,128)(2,1)} %param.8), channel_id=1, source_target_pairs={{0,8},{4,12},{8,0},{12,4},{16,24},{20,28},{24,16},{28,20},{1,9},{5... | collective-permute-start | bytes 110600 | tf_op jit(solution)/shard_map/ppermute | solution.py:23
  10.3 5.2 %collective-permute-start.3 = (bf16[48,1536]{1,0:T(8,128)(2,1)S(1)}, bf16[48,1536]{1,0:T(8,128)(2,1)S(1)}, u32[]{:S(2)}, u32[]{:S(2)}) collective-permute-start(bf16[48,1536]{1,0:T(8,128)(2,1)S(1)} %pad_maximum_fusion.near_ref), channel_id=1, source_target_pairs={{0,4},{4,0},{8,12},{12,8},{16,20},{20,16},{24,28},{28,24},{1,5},{5... | collective-permute-start | bytes 442376 | tf_op jit(solution)/shard_map/ppermute | solution.py:23
  15.5 13.2 %slice-start = ((s8[9437184]{0:T(1024)(128)(4,1)}), s8[4194304]{0:T(1024)(128)(4,1)S(1)}, s32[]{:S(2)}) async-start(s8[9437184]{0:T(1024)(128)(4,1)} %bitcast.5), calls=%async_computation | async-start | bytes 8388608
  15.5 13.2 %slice-start.1 = ((s8[9437184]{0:T(1024)(128)(4,1)}), s8[4194304]{0:T(1024)(128)(4,1)S(1)}, s32[]{:S(2)}) async-start(s8[9437184]{0:T(1024)(128)(4,1)} %bitcast.5), calls=%async_computation.1 | async-start | bytes 8388608
  16.5 8.2 %copy-start = (f32[3072]{0:T(1024)S(1)}, f32[3072]{0:T(1024)}, u32[]{:S(2)}) copy-start(f32[3072]{0:T(1024)} %param.13) | copy-start | bytes 36868
  16.6 1.5 %collective-permute-start.4 = (bf16[48,1792]{1,0:T(8,128)(2,1)S(1)}, bf16[48,1792]{1,0:T(8,128)(2,1)S(1)}, u32[]{:S(2)}, u32[]{:S(2)}) collective-permute-start(bf16[48,1792]{1,0:T(8,128)(2,1)S(1)} %get-tuple-element.32), channel_id=1, source_target_pairs={{0,1},{1,0},{2,3},{3,2},{4,5},{5,4},{6,7},{7,6},{8,9},{9,8},{10,11... | collective-permute-start | bytes 516104 | tf_op jit(solution)/shard_map/ppermute | solution.py:23
  18.2 6.5 %collective-permute-start.6 = (bf16[48,1792]{1,0:T(8,128)(2,1)S(1)}, bf16[48,1792]{1,0:T(8,128)(2,1)S(1)}, u32[]{:S(2)}, u32[]{:S(2)}) collective-permute-start(bf16[48,1792]{1,0:T(8,128)(2,1)S(1)} %get-tuple-element.36.refs_0_), channel_id=1, source_target_pairs={{0,2},{1,3},{2,0},{3,1},{4,6},{5,7},{6,4},{7,5},{8,10},{9,11},{10,... | collective-permute-start | bytes 516104 | tf_op jit(solution)/shard_map/ppermute | solution.py:23
  19.8 8.9 %slice-start.2 = ((s8[9437184]{0:T(1024)(128)(4,1)}), s8[1048576]{0:T(1024)(128)(4,1)S(1)}, s32[]{:S(2)}) async-start(s8[9437184]{0:T(1024)(128)(4,1)} %bitcast.5), calls=%async_computation.2 | async-start | bytes 2097152
  20.7 1.4 %collective-permute-start.5 = (bf16[48,1536]{1,0:T(8,128)(2,1)S(1)}, bf16[48,1536]{1,0:T(8,128)(2,1)S(1)}, u32[]{:S(2)}, u32[]{:S(2)}) collective-permute-start(bf16[48,1536]{1,0:T(8,128)(2,1)S(1)} %get-tuple-element.33), channel_id=1, source_target_pairs={{0,1},{1,0},{2,3},{3,2},{4,5},{5,4},{6,7},{7,6},{8,9},{9,8},{10,11... | collective-permute-start | bytes 442376 | tf_op jit(solution)/shard_map/ppermute | solution.py:23
  22.3 6.0 %collective-permute-start.7 = (bf16[48,1536]{1,0:T(8,128)(2,1)S(1)}, bf16[48,1536]{1,0:T(8,128)(2,1)S(1)}, u32[]{:S(2)}, u32[]{:S(2)}) collective-permute-start(bf16[48,1536]{1,0:T(8,128)(2,1)S(1)} %get-tuple-element.37), channel_id=1, source_target_pairs={{0,2},{1,3},{2,0},{3,1},{4,6},{5,7},{6,4},{7,5},{8,10},{9,11},{10,... | collective-permute-start | bytes 442376 | tf_op jit(solution)/shard_map/ppermute | solution.py:23
  25.1 3.6 %collective-permute-start.9 = (bf16[48,1536]{1,0:T(8,128)(2,1)S(1)}, bf16[48,1536]{1,0:T(8,128)(2,1)S(1)}, u32[]{:S(2)}, u32[]{:S(2)}) collective-permute-start(bf16[48,1536]{1,0:T(8,128)(2,1)S(1)} %shard_map.89.kept_ref), channel_id=1, source_target_pairs={{0,1},{1,0},{2,3},{3,2},{4,5},{5,4},{6,7},{7,6},{8,9},{9,8},{10,11... | collective-permute-start | bytes 442376 | tf_op jit(solution)/shard_map/ppermute | solution.py:23
  28.6 1.4 %collective-permute-start.8 = (bf16[48,1536]{1,0:T(8,128)(2,1)S(1)}, bf16[48,1536]{1,0:T(8,128)(2,1)S(1)}, u32[]{:S(2)}, u32[]{:S(2)}) collective-permute-start(bf16[48,1536]{1,0:T(8,128)(2,1)S(1)} %shard_map.88.kept_ref), channel_id=1, source_target_pairs={{0,1},{1,0},{2,3},{3,2},{4,5},{5,4},{6,7},{7,6},{8,9},{9,8},{10,11... | collective-permute-start | bytes 442376 | tf_op jit(solution)/shard_map/ppermute | solution.py:23
  29.6 10.8 %copy-start.4 = (s32[12]{0:T(128)S(1)}, s32[12]{0:T(128)}, u32[]{:S(2)}) copy-start(s32[12]{0:T(128)} %param.10) | copy-start | bytes 148
  29.7 13.9 %copy-start.3 = (f32[1536]{0:T(1024)S(1)}, f32[1536]{0:T(1024)}, u32[]{:S(2)}) copy-start(f32[1536]{0:T(1024)} %param.15) | copy-start | bytes 18436
  31.0 4.8 %collective-permute-start.10 = (bf16[24,1536]{1,0:T(8,128)(2,1)S(1)}, bf16[24,1536]{1,0:T(8,128)(2,1)S(1)}, u32[]{:S(2)}, u32[]{:S(2)}) collective-permute-start(bf16[24,1536]{1,0:T(8,128)(2,1)S(1)} %concatenate.17), channel_id=1, source_target_pairs={{0,4},{4,0},{8,12},{12,8},{16,20},{20,16},{24,28},{28,24},{1,5},{5... | collective-permute-start | bytes 221192 | tf_op jit(solution)/shard_map/ppermute | solution.py:23
  32.6 5.5 %collective-permute-start.13 = (bf16[24,1536]{1,0:T(8,128)(2,1)S(1)}, bf16[24,1536]{1,0:T(8,128)(2,1)S(1)}, u32[]{:S(2)}, u32[]{:S(2)}) collective-permute-start(bf16[24,1536]{1,0:T(8,128)(2,1)S(1)} %pad_maximum_fusion.1), channel_id=1, source_target_pairs={{0,4},{4,0},{8,12},{12,8},{16,20},{20,16},{24,28},{28,24},{1,5},{5... | collective-permute-start | bytes 221192 | tf_op jit(solution)/shard_map/ppermute | solution.py:23
  35.9 6.4 %collective-permute-start.11 = (bf16[12,1536]{1,0:T(8,128)(2,1)S(1)}, bf16[12,1536]{1,0:T(8,128)(2,1)S(1)}, u32[]{:S(2)}, u32[]{:S(2)}) collective-permute-start(bf16[12,1536]{1,0:T(8,128)(2,1)S(1)} %get-tuple-element.46), channel_id=1, source_target_pairs={{0,24},{4,28},{8,16},{12,20},{16,8},{20,12},{24,0},{28,4},{1,25},{... | collective-permute-start | bytes 110600 | tf_op jit(solution)/shard_map/ppermute | solution.py:23
  38.1 5.4 %collective-permute-start.12 = (bf16[12,1536]{1,0:T(8,128)(2,1)S(1)}, bf16[12,1536]{1,0:T(8,128)(2,1)S(1)}, u32[]{:S(2)}, u32[]{:S(2)}) collective-permute-start(bf16[12,1536]{1,0:T(8,128)(2,1)S(1)} %get-tuple-element.45), channel_id=1, source_target_pairs={{0,16},{4,20},{8,24},{12,28},{16,0},{20,4},{24,8},{28,12},{1,17},{... | collective-permute-start | bytes 110600 | tf_op jit(solution)/shard_map/ppermute | solution.py:23
  38.1 5.4 %collective-permute-start.14 = (bf16[12,1536]{1,0:T(8,128)(2,1)S(1)}, bf16[12,1536]{1,0:T(8,128)(2,1)S(1)}, u32[]{:S(2)}, u32[]{:S(2)}) collective-permute-start(bf16[12,1536]{1,0:T(8,128)(2,1)S(1)} %slice.53), channel_id=1, source_target_pairs={{0,8},{4,12},{8,0},{12,4},{16,24},{20,28},{24,16},{28,20},{1,9},{5... | collective-permute-start | bytes 110600 | tf_op jit(solution)/shard_map/ppermute | solution.py:23

commit v6 on v5

--- a/solution.py
+++ b/solution.py
@@ -10,7 +10,7 @@
 FRAME_TOK = 4
 LANES = 128
 MIB = 2**20
-PARTS = 2
+PARTS = 3
 
 epsilon = 1e-06
 
@@ -96,27 +96,29 @@
     copy.wait()
 
 
-def load_last_kernel(start, gain_ref, *refs):
-    weight_ref, out_ref, row_ref, packed_ref, scratch, sems = refs[-6:]
-    width = out_ref.shape[1]
+def load_rest_kernel(gain_ref, first_ref, weight_ref, *refs):
+    outs, (row_ref, packed_ref, scratch, sems) = refs[:-4], refs[-4:]
+    width = first_ref.shape[1]
     tile = tile_of(width)
     tiles = range(0, width, tile)
-    copies = [
-        pltpu.make_async_copy(
-            weight_ref.at[:, pl.ds(start + at, tile)], out_ref.at[:, pl.ds(at, tile)], sems.at[at // tile]
-        )
-        for at in tiles
-    ]
-    for copy in copies:
-        copy.start()
+    copies = {}
+    for part, out_ref in enumerate(outs, 1):
+        for at in tiles:
+            copy = pltpu.make_async_copy(
+                weight_ref.at[:, pl.ds(part * width + at, tile)],
+                out_ref.at[:, pl.ds(at, tile)],
+                sems.at[len(copies)],
+            )
+            copy.start()
+            copies[part, at] = copy
     gain = gain_ref[...][None, :]
     high = gain.astype(jnp.bfloat16).astype(jnp.float32)
     row = lax.broadcasted_iota(jnp.int32, (16, gain.shape[1]), 0)
     rows = jnp.where(row == 0, high, jnp.where(row == 1, gain - high, 0.0)).astype(jnp.bfloat16)
-    for part, loaded in enumerate(refs[:-6] + (out_ref,)):
-        for at, copy in zip(tiles, copies):
-            if loaded is out_ref:
-                copy.wait()
+    for part, loaded in enumerate((first_ref,) + outs):
+        for at in tiles:
+            if part:
+                copies[part, at].wait()
             product = jnp.dot(rows, loaded[:, at:at + tile], preferred_element_type=jnp.float32)
             row_ref[:, part * width + at:part * width + at + tile] = product[0:1] + product[1:2]
     pack_row(lambda at: row_ref[:, at:at + LANES], row_ref.shape[1], scratch, packed_ref)
@@ -238,29 +240,30 @@
     side = LANES * -(-2 * hidden_width // (LANES * half))
     extra = [LANES + side if start == 0 else 0 for start in starts]
     copied = pltpu.SemaphoreType.DMA
-    loaded = [
-        call(
-            functools.partial(load_kernel, start),
-            [((block_width, width), bf16)],
-            [in_hbm],
-            [copied],
-            limit=46,
-        )(up_weight)[0]
-        for start in starts[:-1]
-    ]
+    (loaded,) = call(
+        functools.partial(load_kernel, 0),
+        [((block_width, width), bf16)],
+        [in_hbm],
+        [copied],
+        limit=46,
+    )(up_weight)
     order = [0] + list(reversed(masks))
     near = jnp.concatenate([patches] + [swap(patches, "tok", mask) for mask in order[1:]])
     near, loaded, norm_gain = lax.optimization_barrier((near, loaded, norm_gain))
     far = swap(near, "tok", 1)
-    last, gain_row, gain_packed = call(
-        functools.partial(load_last_kernel, starts[-1]),
-        [((block_width, width), bf16), ((1, hidden_width), f32), ((half, side), bf16)],
-        [in_vmem] * parts + [in_hbm],
-        [pltpu.VMEM((half, side), f32), copied((width // tile_of(width),))],
+    *rest, gain_row, gain_packed = call(
+        load_rest_kernel,
+        [((block_width, width), bf16)] * (parts - 1)
+        + [((1, hidden_width), f32), ((half, side), bf16)],
+        [in_vmem] * 2 + [in_hbm],
+        [
+            pltpu.VMEM((half, side), f32),
+            copied(((parts - 1) * (width // tile_of(width)) or 1,)),
+        ],
         flops=32 * up_weight.size,
         limit=40,
-    )(norm_gain, *loaded, up_weight)
-    loaded = loaded + [last]
+    )(norm_gain, loaded, up_weight)
+    loaded = [loaded, *rest]
 
     kepts, givens = [], []
     for start, more, weight in zip(starts, extra, loaded):

time: 44.4 us -> 43.8 us (0.986)
  waiting for transfers between devices: 16.1 us -> 13.1 us
  starting transfers between devices: 16.4 us -> 18 us
  Pallas kernels: 9.92 us -> 10.6 us
    ppermute x15 -> x18, waiting for transfers between devices: 16.1 us -> 13.1 us  [swap(): return lax.ppermute(block, axis, [(i, i ^ mask) for i in range(size)])]
    ppermute x15 -> x18, starting transfers between devices: 16.4 us -> 18 us  [swap(): return lax.ppermute(block, axis, [(i, i ^ mask) for i in range(size)])]
    pallas_call x1 -> x2, Pallas kernels: 0.87 us -> 1.33 us  [per_device(): call(up_products, outs, [in_vmem] * 2, flops=flops)(rows, weight)]
    pallas_call x2 -> x3, Pallas kernels: 0.69 us -> 0.92 us  [per_device(): call(functools.partial(gelu_kernel, start, hidden_width, block_width, ful...]
    pallas_call x2 -> x3, Pallas kernels: 1.78 us -> 1.92 us  [per_device(): call(functools.partial(down_kernel, start, last), [((half, block_width),...]
  transfers between devices with their start and end apart: 15 -> 18, of which waited for: 10 -> 10; matrix products, arithmetic and copies ran while one was open for 0% -> 0% of each run, Pallas kernels for 18% -> 21%
where the time goes in v6:
time: 43.8 us; the launch traced here: 43.6 us
  starting transfers between devices  18 us (41%)
  waiting for transfers between devices  13.1 us (30%)
  Pallas kernels  10.6 us (24%)
  between operations  0.93 us (2%)
  other arithmetic  0.83 us (2%)
    ppermute x18, starting transfers between devices, swap(): return lax.ppermute(block, axis, [(i, i ^ mask) for i in range(size)])  18 us
    ppermute x18, waiting for transfers between devices, swap(): return lax.ppermute(block, axis, [(i, i ^ mask) for i in range(size)])  13.1 us
    pallas_call x1, Pallas kernels, per_device(): call(load_rest_kernel, [((block_width, width), bf16)] * (parts - 1) + [((...  3.27 us
    pallas_call x3, Pallas kernels, per_device(): call(functools.partial(down_kernel, start, last), [((half, block_width),...  1.92 us
    pallas_call x1, Pallas kernels, per_device(): call(functools.partial(load_kernel, 0), [((block_width, width), bf16)], [...  1.9 us
    pallas_call x2, Pallas kernels, per_device(): call(up_products, outs, [in_vmem] * 2, flops=flops)(rows, weight)  1.33 us
    pallas_call x3, Pallas kernels, per_device(): call(functools.partial(gelu_kernel, start, hidden_width, block_width, ful...  0.92 us
  transfers between devices with their start and end apart: 18, of which 10 were waited for; matrix products, arithmetic and copies ran while one was open for 0% of the time, Pallas kernels for 21%

profile of v6, /device:TPU:0, one launch (start us, length us, event | category | flops | bytes accessed | tf_op | source)
XLA Modules:
  0.0 43.6 jit_solution(4046559618086960300)
XLA Ops:
  0.0 0.0 copy-start.2
  0.0 5.0 %collective-permute-start = (bf16[12,1536]{1,0:T(8,128)(2,1)}, bf16[12,1536]{1,0:T(8,128)(2,1)S(1)}, u32[]{:S(2)}, u32[]{:S(2)}) collective-permute-start(bf16[12,1536]{1,0:T(8,128)(2,1)} %param.8), channel_id=1, source_target_pairs={{0,24},{4,28},{8,16},{12,20},{16,8},{20,12},{24,0},{28,4},{1,25},{... | collective-permute-start | bytes 110600 | tf_op jit(solution)/shard_map/ppermute | solution.py:23
  5.1 0.0 collective-permute-start.1
  5.1 0.6 %collective-permute-start.2 = (bf16[12,1536]{1,0:T(8,128)(2,1)}, bf16[12,1536]{1,0:T(8,128)(2,1)S(1)}, u32[]{:S(2)}, u32[]{:S(2)}) collective-permute-start(bf16[12,1536]{1,0:T(8,128)(2,1)} %param.8), channel_id=1, source_target_pairs={{0,8},{4,12},{8,0},{12,4},{16,24},{20,28},{24,16},{28,20},{1,9},{5... | collective-permute-start | bytes 110600 | tf_op jit(solution)/shard_map/ppermute | solution.py:23
  5.7 1.9 %shard_map.82.first_ref.weight_ref = bf16[1536,1024]{1,0:T(8,128)(2,1)S(1)} custom-call(bf16[1536,3072]{1,0:T(8,128)(2,1)} %weight_ref.6), custom_call_target="tpu_custom_call" | custom-call | tf_op jit(solution)/shard_map/pallas_call | solution.py:243
  7.6 0.0 collective-permute-done
  7.6 2.6 %collective-permute-done.1 = bf16[12,1536]{1,0:T(8,128)(2,1)S(1)} collective-permute-done((bf16[12,1536]{1,0:T(8,128)(2,1)}, bf16[12,1536]{1,0:T(8,128)(2,1)S(1)}, u32[]{:S(2)}, u32[]{:S(2)}) %collective-permute-start.1) | collective-permute-done | bytes 36896 | tf_op jit(solution)/shard_map/ppermute | solution.py:23
  10.3 0.0 collective-permute-done.2
  10.3 0.0 copy-done.2
  10.3 1.6 %collective-permute-start.3 = (bf16[48,1536]{1,0:T(8,128)(2,1)S(1)}, bf16[48,1536]{1,0:T(8,128)(2,1)S(1)}, u32[]{:S(2)}, u32[]{:S(2)}) collective-permute-start(bf16[48,1536]{1,0:T(8,128)(2,1)S(1)} %pad_maximum_fusion.near_ref), channel_id=1, source_target_pairs={{0,4},{4,0},{8,12},{12,8},{16,20},{20,16},{24,28},{28,24},{1,5},{5... | collective-permute-start | bytes 442376 | tf_op jit(solution)/shard_map/ppermute | solution.py:23
  11.9 0.0 copy-done.1
  11.9 3.3 %shard_map.83 = (bf16[1536,1024]{1,0:T(8,128)(2,1)S(1)}, bf16[1536,1024]{1,0:T(8,128)(2,1)S(1)}, f32[1,3072]{1,0:T(1,128)S(1)}, bf16[48,128]{1,0:T(8,128)(2,1)S(1)}) custom-call(f32[1536]{0:T(1024)S(1)} %copy-done.1, bf16[1536,1024]{1,0:T(8,128)(2,1)S(1)} %shard_map.82.first_ref.weight_ref, bf16[1536,3072]{1,0:T(8,128)(2,1)} %weight_ref.6), custom_call_target="tpu_custom_call" | custom-call | flops 1207959552 | tf_op jit(solution)/shard_map/pallas_call | solution.py:254
  15.1 0.4 collective-permute-done.3.far_ref
  15.5 0.8 %shard_map.84 = (bf16[96,1536]{1,0:T(8,128)(2,1)S(1)}, bf16[48,128]{1,0:T(8,128)(2,1)S(1)}, f32[48,1024]{1,0:T(8,128)S(1)}, bf16[48,1280]{1,0:T(8,128)(2,1)S(1)}) custom-call(bf16[48,1536]{1,0:T(8,128)(2,1)S(1)} %pad_maximum_fusion.near_ref, bf16[48,1536]{1,0:T(8,128)(2,1)S(1)} %collective-permute-done.3.far_ref, f32[1536]{0:T(1024)S(1)} %copy-done.1, ...), custom_call_target="tpu_custom_call" | custom-call | flops 2415919104 | tf_op jit(solution)/shard_map/pallas_call | solution.py:273
  16.3 0.1 collective-permute-start.4
  16.4 0.0 slice-start
  16.4 0.0 slice-start.1
  16.4 0.7 %shard_map.89 = (f32[48,1024]{1,0:T(8,128)S(1)}, bf16[48,1024]{1,0:T(8,128)(2,1)S(1)}) custom-call(bf16[96,1536]{1,0:T(8,128)(2,1)S(1)} %get-tuple-element.32.rows_ref, bf16[1536,1024]{1,0:T(8,128)(2,1)S(1)} %get-tuple-element.43.weight_ref), custom_call_target="tpu_custom_call" | custom-call | flops 2415919104 | tf_op jit(solution)/shard_map/pallas_call | solution.py:280
  17.1 0.5 %collective-permute-start.9 = (bf16[48,1024]{1,0:T(8,128)(2,1)S(1)}, bf16[48,1024]{1,0:T(8,128)(2,1)S(1)}, u32[]{:S(2)}, u32[]{:S(2)}) collective-permute-start(bf16[48,1024]{1,0:T(8,128)(2,1)S(1)} %get-tuple-element.45), channel_id=1, source_target_pairs={{0,1},{1,0},{2,3},{3,2},{4,5},{5,4},{6,7},{7,6},{8,9},{9,8},{10,11... | collective-permute-start | bytes 294920 | tf_op jit(solution)/shard_map/ppermute | solution.py:23
  17.6 0.1 collective-permute-done.4.packed_ref.other_ref
  17.7 0.2 shard_map.87
  17.9 1.6 %collective-permute-start.6 = (bf16[48,1280]{1,0:T(8,128)(2,1)S(1)}, bf16[48,1280]{1,0:T(8,128)(2,1)S(1)}, u32[]{:S(2)}, u32[]{:S(2)}) collective-permute-start(bf16[48,1280]{1,0:T(8,128)(2,1)S(1)} %get-tuple-element.41.refs_0_), channel_id=1, source_target_pairs={{0,2},{1,3},{2,0},{3,1},{4,6},{5,7},{6,4},{7,5},{8,10},{9,11},{10,... | collective-permute-start | bytes 368648 | tf_op jit(solution)/shard_map/ppermute | solution.py:23
  19.5 0.7 %shard_map.85 = (f32[48,1024]{1,0:T(8,128)S(1)}, bf16[48,1024]{1,0:T(8,128)(2,1)S(1)}) custom-call(bf16[96,1536]{1,0:T(8,128)(2,1)S(1)} %get-tuple-element.32.rows_ref, bf16[1536,1024]{1,0:T(8,128)(2,1)S(1)} %get-tuple-element.33.weight_ref), custom_call_target="tpu_custom_call" | custom-call | flops 2415919104 | tf_op jit(solution)/shard_map/pallas_call | solution.py:280
  20.2 0.1 collective-permute-start.5
  20.2 0.0 collective-permute-done.9.other_ref
  20.2 0.2 shard_map.90
  20.4 0.6 %collective-permute-start.10 = (bf16[48,1024]{1,0:T(8,128)(2,1)S(1)}, bf16[48,1024]{1,0:T(8,128)(2,1)S(1)}, u32[]{:S(2)}, u32[]{:S(2)}) collective-permute-start(bf16[48,1024]{1,0:T(8,128)(2,1)S(1)} %get-tuple-element.47), channel_id=1, source_target_pairs={{0,2},{1,3},{2,0},{3,1},{4,6},{5,7},{6,4},{7,5},{8,10},{9,11},{10,... | collective-permute-start | bytes 294920 | tf_op jit(solution)/shard_map/ppermute | solution.py:23
  21.0 0.5 %collective-permute-done.5.other_ref = bf16[48,1024]{1,0:T(8,128)(2,1)S(1)} collective-permute-done((bf16[48,1024]{1,0:T(8,128)(2,1)S(1)}, bf16[48,1024]{1,0:T(8,128)(2,1)S(1)}, u32[]{:S(2)}, u32[]{:S(2)}) %collective-permute-start.5) | collective-permute-done | bytes 98336 | tf_op jit(solution)/shard_map/ppermute | solution.py:23
  21.5 0.2 shard_map.86
  21.7 1.1 %collective-permute-start.7 = (bf16[48,1024]{1,0:T(8,128)(2,1)S(1)}, bf16[48,1024]{1,0:T(8,128)(2,1)S(1)}, u32[]{:S(2)}, u32[]{:S(2)}) collective-permute-start(bf16[48,1024]{1,0:T(8,128)(2,1)S(1)} %get-tuple-element.42), channel_id=1, source_target_pairs={{0,2},{1,3},{2,0},{3,1},{4,6},{5,7},{6,4},{7,5},{8,10},{9,11},{10,... | collective-permute-start | bytes 294920 | tf_op jit(solution)/shard_map/ppermute | solution.py:23
  22.8 0.6 %collective-permute-done.6.refs_1_ = bf16[48,1280]{1,0:T(8,128)(2,1)S(1)} collective-permute-done((bf16[48,1280]{1,0:T(8,128)(2,1)S(1)}, bf16[48,1280]{1,0:T(8,128)(2,1)S(1)}, u32[]{:S(2)}, u32[]{:S(2)}) %collective-permute-start.6) | collective-permute-done | bytes 122912 | tf_op jit(solution)/shard_map/ppermute | solution.py:23
  23.3 0.0 copy-done
  23.3 0.3 shard_map.92.kept_ref
  23.7 0.1 collective-permute-start.12
  24.4 1.7 %collective-permute-done.10.refs_2_ = bf16[48,1024]{1,0:T(8,128)(2,1)S(1)} collective-permute-done((bf16[48,1024]{1,0:T(8,128)(2,1)S(1)}, bf16[48,1024]{1,0:T(8,128)(2,1)S(1)}, u32[]{:S(2)}, u32[]{:S(2)}) %collective-permute-start.10) | collective-permute-done | bytes 98336 | tf_op jit(solution)/shard_map/ppermute | solution.py:23
  26.1 0.3 shard_map.91.kept_ref
  26.4 0.1 collective-permute-start.11
  26.5 1.3 %collective-permute-done.7.refs_2_ = bf16[48,1024]{1,0:T(8,128)(2,1)S(1)} collective-permute-done((bf16[48,1024]{1,0:T(8,128)(2,1)S(1)}, bf16[48,1024]{1,0:T(8,128)(2,1)S(1)}, u32[]{:S(2)}, u32[]{:S(2)}) %collective-permute-start.7) | collective-permute-done | bytes 98336 | tf_op jit(solution)/shard_map/ppermute | solution.py:23
  27.8 0.3 shard_map.88.kept_ref
  28.1 0.1 collective-permute-start.8
  28.2 0.0 collective-permute-done.12.given_ref
  28.2 0.0 slice-done
  28.2 0.0 slice-done.1
  28.2 0.0 slice-done.2
  28.2 0.6 %shard_map.93.refs_0_ = f32[96,1536]{1,0:T(8,128)S(1)} custom-call(bf16[48,1024]{1,0:T(8,128)(2,1)S(1)} %shard_map.92.kept_ref, bf16[48,1024]{1,0:T(8,128)(2,1)S(1)} %collective-permute-done.12.given_ref, bf16[3072,1536]{1,0:T(8,128)(2,1)S(1)} %bitcast.4), custom_call_target="tpu_custom_call" | custom-call | flops 2415919104 | tf_op jit(solution)/shard_map/pallas_call | solution.py:307
  28.9 0.0 collective-permute-done.11.given_ref
  28.9 0.6 %shard_map.94.refs_0_ = f32[96,1536]{1,0:T(8,128)S(1)} custom-call(bf16[48,1024]{1,0:T(8,128)(2,1)S(1)} %shard_map.91.kept_ref, bf16[48,1024]{1,0:T(8,128)(2,1)S(1)} %collective-permute-done.11.given_ref, bf16[3072,1536]{1,0:T(8,128)(2,1)S(1)} %bitcast.4, f32[96,1536]{1,0:T(8,128)S(1)} %shard_map.93.refs_0_), custom_call_target="tpu_custom_call" | custom-call | flops 2415919104 | tf_op jit(solution)/shard_map/pallas_call | solution.py:307
  29.5 0.0 copy-start.4
  29.5 0.0 copy-start.3
  29.5 0.0 collective-permute-done.8.given_ref
  29.6 0.7 %shard_map.95 = (f32[48,1536]{1,0:T(8,128)S(1)}, bf16[48,1536]{1,0:T(8,128)(2,1)S(1)}) custom-call(bf16[48,1024]{1,0:T(8,128)(2,1)S(1)} %shard_map.88.kept_ref, bf16[48,1024]{1,0:T(8,128)(2,1)S(1)} %collective-permute-done.8.given_ref, bf16[3072,1536]{1,0:T(8,128)(2,1)S(1)} %bitcast.4, f32[96,1536]{1,0:T(8,128)S(1)} %shard_map.94.refs_0_), custom_call_target="tpu_custom_call" | custom-call | flops 2415919104 | tf_op jit(solution)/shard_map/pallas_call | solution.py:307
  30.3 1.6 %collective-permute-start.13 = (bf16[24,1536]{1,0:T(8,128)(2,1)S(1)}, bf16[24,1536]{1,0:T(8,128)(2,1)S(1)}, u32[]{:S(2)}, u32[]{:S(2)}) collective-permute-start(bf16[24,1536]{1,0:T(8,128)(2,1)S(1)} %concatenate.17), channel_id=1, source_target_pairs={{0,4},{4,0},{8,12},{12,8},{16,20},{20,16},{24,28},{28,24},{1,5},{5... | collective-permute-start | bytes 221192 | tf_op jit(solution)/shard_map/ppermute | solution.py:23
  31.9 0.6 %collective-permute-start.16 = (bf16[24,1536]{1,0:T(8,128)(2,1)S(1)}, bf16[24,1536]{1,0:T(8,128)(2,1)S(1)}, u32[]{:S(2)}, u32[]{:S(2)}) collective-permute-start(bf16[24,1536]{1,0:T(8,128)(2,1)S(1)} %pad_maximum_fusion.1), channel_id=1, source_target_pairs={{0,4},{4,0},{8,12},{12,8},{16,20},{20,16},{24,28},{28,24},{1,5},{5... | collective-permute-start | bytes 221192 | tf_op jit(solution)/shard_map/ppermute | solution.py:23
  32.5 2.8 %collective-permute-done.13 = bf16[24,1536]{1,0:T(8,128)(2,1)S(1)} collective-permute-done((bf16[24,1536]{1,0:T(8,128)(2,1)S(1)}, bf16[24,1536]{1,0:T(8,128)(2,1)S(1)}, u32[]{:S(2)}, u32[]{:S(2)}) %collective-permute-start.13) | collective-permute-done | bytes 73760 | tf_op jit(solution)/shard_map/ppermute | solution.py:23
  35.3 2.2 %collective-permute-start.14 = (bf16[12,1536]{1,0:T(8,128)(2,1)S(1)}, bf16[12,1536]{1,0:T(8,128)(2,1)S(1)}, u32[]{:S(2)}, u32[]{:S(2)}) collective-permute-start(bf16[12,1536]{1,0:T(8,128)(2,1)S(1)} %get-tuple-element.56), channel_id=1, source_target_pairs={{0,24},{4,28},{8,16},{12,20},{16,8},{20,12},{24,0},{28,4},{1,25},{... | collective-permute-start | bytes 110600 | tf_op jit(solution)/shard_map/ppermute | solution.py:23
  37.5 0.0 collective-permute-start.15
  37.5 0.0 collective-permute-done.16
  37.6 2.3 %collective-permute-start.17 = (bf16[12,1536]{1,0:T(8,128)(2,1)S(1)}, bf16[12,1536]{1,0:T(8,128)(2,1)S(1)}, u32[]{:S(2)}, u32[]{:S(2)}) collective-permute-start(bf16[12,1536]{1,0:T(8,128)(2,1)S(1)} %slice.53), channel_id=1, source_target_pairs={{0,8},{4,12},{8,0},{12,4},{16,24},{20,28},{24,16},{28,20},{1,9},{5... | collective-permute-start | bytes 110600 | tf_op jit(solution)/shard_map/ppermute | solution.py:23
  39.9 0.0 copy-done.4
  39.9 1.4 %collective-permute-done.14 = bf16[12,1536]{1,0:T(8,128)(2,1)S(1)} collective-permute-done((bf16[12,1536]{1,0:T(8,128)(2,1)S(1)}, bf16[12,1536]{1,0:T(8,128)(2,1)S(1)}, u32[]{:S(2)}, u32[]{:S(2)}) %collective-permute-start.14) | collective-permute-done | bytes 36896 | tf_op jit(solution)/shard_map/ppermute | solution.py:23
  41.3 1.7 %collective-permute-done.15 = bf16[12,1536]{1,0:T(8,128)(2,1)S(1)} collective-permute-done((bf16[12,1536]{1,0:T(8,128)(2,1)S(1)}, bf16[12,1536]{1,0:T(8,128)(2,1)S(1)}, u32[]{:S(2)}, u32[]{:S(2)}) %collective-permute-start.15) | collective-permute-done | bytes 36896 | tf_op jit(solution)/shard_map/ppermute | solution.py:23
  42.9 0.0 collective-permute-done.17
  42.9 0.0 copy-done.3
  42.9 0.7 %fusion.2 = bf16[12,1536]{1,0:T(8,128)(2,1)} fusion(f32[24,1536]{1,0:T(8,128)S(1)} %maximum_add_fusion, f32[1536]{0:T(1024)S(1)} %copy-done.3, bf16[12,1536]{1,0:T(8,128)(2,1)S(1)} %collective-permute-done.17, bf16[12,1536]{1,0:T(8,128)(2,1)S(1)} %collective-permute-done.14, bf16[12,1536]{1,0:T(8,128)(2,1)S(1)} %collective-permute-done.15, ...), kind=kLoop, calls=%fused_computation.6 | loop fusion | flops 129024 | bytes 227376 | tf_op jit(solution)/shard_map/convert_element_type | solution.py:332
  (14 shorter events, 0.2 us)
Async XLA Ops:
  0.0 10.3 %copy-start.2 = (bf16[12,1536]{1,0:T(8,128)(2,1)S(1)}, bf16[12,1536]{1,0:T(8,128)(2,1)}, u32[]{:S(2)}) copy-start(bf16[12,1536]{1,0:T(8,128)(2,1)} %param.8) | copy-start | bytes 110596
  0.0 11.9 %copy-start.1 = (f32[1536]{0:T(1024)S(1)}, f32[1536]{0:T(1024)}, u32[]{:S(2)}) copy-start(f32[1536]{0:T(1024)} %gain_ref.1) | copy-start | bytes 18436
  0.0 7.6 %collective-permute-start = (bf16[12,1536]{1,0:T(8,128)(2,1)}, bf16[12,1536]{1,0:T(8,128)(2,1)S(1)}, u32[]{:S(2)}, u32[]{:S(2)}) collective-permute-start(bf16[12,1536]{1,0:T(8,128)(2,1)} %param.8), channel_id=1, source_target_pairs={{0,24},{4,28},{8,16},{12,20},{16,8},{20,12},{24,0},{28,4},{1,25},{... | collective-permute-start | bytes 110600 | tf_op jit(solution)/shard_map/ppermute | solution.py:23
  5.1 5.2 %collective-permute-start.1 = (bf16[12,1536]{1,0:T(8,128)(2,1)}, bf16[12,1536]{1,0:T(8,128)(2,1)S(1)}, u32[]{:S(2)}, u32[]{:S(2)}) collective-permute-start(bf16[12,1536]{1,0:T(8,128)(2,1)} %param.8), channel_id=1, source_target_pairs={{0,16},{4,20},{8,24},{12,28},{16,0},{20,4},{24,8},{28,12},{1,17},{... | collective-permute-start | bytes 110600 | tf_op jit(solution)/shard_map/ppermute | solution.py:23
  5.1 5.2 %collective-permute-start.2 = (bf16[12,1536]{1,0:T(8,128)(2,1)}, bf16[12,1536]{1,0:T(8,128)(2,1)S(1)}, u32[]{:S(2)}, u32[]{:S(2)}) collective-permute-start(bf16[12,1536]{1,0:T(8,128)(2,1)} %param.8), channel_id=1, source_target_pairs={{0,8},{4,12},{8,0},{12,4},{16,24},{20,28},{24,16},{28,20},{1,9},{5... | collective-permute-start | bytes 110600 | tf_op jit(solution)/shard_map/ppermute | solution.py:23
  10.3 5.2 %collective-permute-start.3 = (bf16[48,1536]{1,0:T(8,128)(2,1)S(1)}, bf16[48,1536]{1,0:T(8,128)(2,1)S(1)}, u32[]{:S(2)}, u32[]{:S(2)}) collective-permute-start(bf16[48,1536]{1,0:T(8,128)(2,1)S(1)} %pad_maximum_fusion.near_ref), channel_id=1, source_target_pairs={{0,4},{4,0},{8,12},{12,8},{16,20},{20,16},{24,28},{28,24},{1,5},{5... | collective-permute-start | bytes 442376 | tf_op jit(solution)/shard_map/ppermute | solution.py:23
  16.3 1.4 %collective-permute-start.4 = (bf16[48,1280]{1,0:T(8,128)(2,1)S(1)}, bf16[48,1280]{1,0:T(8,128)(2,1)S(1)}, u32[]{:S(2)}, u32[]{:S(2)}) collective-permute-start(bf16[48,1280]{1,0:T(8,128)(2,1)S(1)} %get-tuple-element.37), channel_id=1, source_target_pairs={{0,1},{1,0},{2,3},{3,2},{4,5},{5,4},{6,7},{7,6},{8,9},{9,8},{10,11... | collective-permute-start | bytes 368648 | tf_op jit(solution)/shard_map/ppermute | solution.py:23
  16.4 11.8 %slice-start = ((s8[9437184]{0:T(1024)(128)(4,1)}), s8[4194304]{0:T(1024)(128)(4,1)S(1)}, s32[]{:S(2)}) async-start(s8[9437184]{0:T(1024)(128)(4,1)} %bitcast.3), calls=%async_computation | async-start | bytes 8388608
  16.4 11.8 %slice-start.1 = ((s8[9437184]{0:T(1024)(128)(4,1)}), s8[4194304]{0:T(1024)(128)(4,1)S(1)}, s32[]{:S(2)}) async-start(s8[9437184]{0:T(1024)(128)(4,1)} %bitcast.3), calls=%async_computation.1 | async-start | bytes 8388608
  17.1 3.2 %collective-permute-start.9 = (bf16[48,1024]{1,0:T(8,128)(2,1)S(1)}, bf16[48,1024]{1,0:T(8,128)(2,1)S(1)}, u32[]{:S(2)}, u32[]{:S(2)}) collective-permute-start(bf16[48,1024]{1,0:T(8,128)(2,1)S(1)} %get-tuple-element.45), channel_id=1, source_target_pairs={{0,1},{1,0},{2,3},{3,2},{4,5},{5,4},{6,7},{7,6},{8,9},{9,8},{10,11... | collective-permute-start | bytes 294920 | tf_op jit(solution)/shard_map/ppermute | solution.py:23
  17.9 5.4 %collective-permute-start.6 = (bf16[48,1280]{1,0:T(8,128)(2,1)S(1)}, bf16[48,1280]{1,0:T(8,128)(2,1)S(1)}, u32[]{:S(2)}, u32[]{:S(2)}) collective-permute-start(bf16[48,1280]{1,0:T(8,128)(2,1)S(1)} %get-tuple-element.41.refs_0_), channel_id=1, source_target_pairs={{0,2},{1,3},{2,0},{3,1},{4,6},{5,7},{6,4},{7,5},{8,10},{9,11},{10,... | collective-permute-start | bytes 368648 | tf_op jit(solution)/shard_map/ppermute | solution.py:23
  19.5 3.9 %copy-start = (f32[3072]{0:T(1024)S(1)}, f32[3072]{0:T(1024)}, u32[]{:S(2)}) copy-start(f32[3072]{0:T(1024)} %param.13) | copy-start | bytes 36868
  19.5 8.7 %slice-start.2 = ((s8[9437184]{0:T(1024)(128)(4,1)}), s8[1048576]{0:T(1024)(128)(4,1)S(1)}, s32[]{:S(2)}) async-start(s8[9437184]{0:T(1024)(128)(4,1)} %bitcast.3), calls=%async_computation.2 | async-start | bytes 2097152
  20.2 1.4 %collective-permute-start.5 = (bf16[48,1024]{1,0:T(8,128)(2,1)S(1)}, bf16[48,1024]{1,0:T(8,128)(2,1)S(1)}, u32[]{:S(2)}, u32[]{:S(2)}) collective-permute-start(bf16[48,1024]{1,0:T(8,128)(2,1)S(1)} %get-tuple-element.38), channel_id=1, source_target_pairs={{0,1},{1,0},{2,3},{3,2},{4,5},{5,4},{6,7},{7,6},{8,9},{9,8},{10,11... | collective-permute-start | bytes 294920 | tf_op jit(solution)/shard_map/ppermute | solution.py:23
  20.4 5.7 %collective-permute-start.10 = (bf16[48,1024]{1,0:T(8,128)(2,1)S(1)}, bf16[48,1024]{1,0:T(8,128)(2,1)S(1)}, u32[]{:S(2)}, u32[]{:S(2)}) collective-permute-start(bf16[48,1024]{1,0:T(8,128)(2,1)S(1)} %get-tuple-element.47), channel_id=1, source_target_pairs={{0,2},{1,3},{2,0},{3,1},{4,6},{5,7},{6,4},{7,5},{8,10},{9,11},{10,... | collective-permute-start | bytes 294920 | tf_op jit(solution)/shard_map/ppermute | solution.py:23
  21.7 6.1 %collective-permute-start.7 = (bf16[48,1024]{1,0:T(8,128)(2,1)S(1)}, bf16[48,1024]{1,0:T(8,128)(2,1)S(1)}, u32[]{:S(2)}, u32[]{:S(2)}) collective-permute-start(bf16[48,1024]{1,0:T(8,128)(2,1)S(1)} %get-tuple-element.42), channel_id=1, source_target_pairs={{0,2},{1,3},{2,0},{3,1},{4,6},{5,7},{6,4},{7,5},{8,10},{9,11},{10,... | collective-permute-start | bytes 294920 | tf_op jit(solution)/shard_map/ppermute | solution.py:23
  23.7 4.5 %collective-permute-start.12 = (bf16[48,1024]{1,0:T(8,128)(2,1)S(1)}, bf16[48,1024]{1,0:T(8,128)(2,1)S(1)}, u32[]{:S(2)}, u32[]{:S(2)}) collective-permute-start(bf16[48,1024]{1,0:T(8,128)(2,1)S(1)} %shard_map.92.kept_ref), channel_id=1, source_target_pairs={{0,1},{1,0},{2,3},{3,2},{4,5},{5,4},{6,7},{7,6},{8,9},{9,8},{10,11... | collective-permute-start | bytes 294920 | tf_op jit(solution)/shard_map/ppermute | solution.py:23
  26.4 2.5 %collective-permute-start.11 = (bf16[48,1024]{1,0:T(8,128)(2,1)S(1)}, bf16[48,1024]{1,0:T(8,128)(2,1)S(1)}, u32[]{:S(2)}, u32[]{:S(2)}) collective-permute-start(bf16[48,1024]{1,0:T(8,128)(2,1)S(1)} %shard_map.91.kept_ref), channel_id=1, source_target_pairs={{0,1},{1,0},{2,3},{3,2},{4,5},{5,4},{6,7},{7,6},{8,9},{9,8},{10,11... | collective-permute-start | bytes 294920 | tf_op jit(solution)/shard_map/ppermute | solution.py:23
  28.1 1.4 %collective-permute-start.8 = (bf16[48,1024]{1,0:T(8,128)(2,1)S(1)}, bf16[48,1024]{1,0:T(8,128)(2,1)S(1)}, u32[]{:S(2)}, u32[]{:S(2)}) collective-permute-start(bf16[48,1024]{1,0:T(8,128)(2,1)S(1)} %shard_map.88.kept_ref), channel_id=1, source_target_pairs={{0,1},{1,0},{2,3},{3,2},{4,5},{5,4},{6,7},{7,6},{8,9},{9,8},{10,11... | collective-permute-start | bytes 294920 | tf_op jit(solution)/shard_map/ppermute | solution.py:23
  29.5 10.4 %copy-start.4 = (s32[12]{0:T(128)S(1)}, s32[12]{0:T(128)}, u32[]{:S(2)}) copy-start(s32[12]{0:T(128)} %param.10) | copy-start | bytes 148
  29.5 13.4 %copy-start.3 = (f32[1536]{0:T(1024)S(1)}, f32[1536]{0:T(1024)}, u32[]{:S(2)}) copy-start(f32[1536]{0:T(1024)} %param.15) | copy-start | bytes 18436
  30.3 5.0 %collective-permute-start.13 = (bf16[24,1536]{1,0:T(8,128)(2,1)S(1)}, bf16[24,1536]{1,0:T(8,128)(2,1)S(1)}, u32[]{:S(2)}, u32[]{:S(2)}) collective-permute-start(bf16[24,1536]{1,0:T(8,128)(2,1)S(1)} %concatenate.17), channel_id=1, source_target_pairs={{0,4},{4,0},{8,12},{12,8},{16,20},{20,16},{24,28},{28,24},{1,5},{5... | collective-permute-start | bytes 221192 | tf_op jit(solution)/shard_map/ppermute | solution.py:23
  31.9 5.7 %collective-permute-start.16 = (bf16[24,1536]{1,0:T(8,128)(2,1)S(1)}, bf16[24,1536]{1,0:T(8,128)(2,1)S(1)}, u32[]{:S(2)}, u32[]{:S(2)}) collective-permute-start(bf16[24,1536]{1,0:T(8,128)(2,1)S(1)} %pad_maximum_fusion.1), channel_id=1, source_target_pairs={{0,4},{4,0},{8,12},{12,8},{16,20},{20,16},{24,28},{28,24},{1,5},{5... | collective-permute-start | bytes 221192 | tf_op jit(solution)/shard_map/ppermute | solution.py:23
  35.3 6.0 %collective-permute-start.14 = (bf16[12,1536]{1,0:T(8,128)(2,1)S(1)}, bf16[12,1536]{1,0:T(8,128)(2,1)S(1)}, u32[]{:S(2)}, u32[]{:S(2)}) collective-permute-start(bf16[12,1536]{1,0:T(8,128)(2,1)S(1)} %get-tuple-element.56), channel_id=1, source_target_pairs={{0,24},{4,28},{8,16},{12,20},{16,8},{20,12},{24,0},{28,4},{1,25},{... | collective-permute-start | bytes 110600 | tf_op jit(solution)/shard_map/ppermute | solution.py:23
  37.5 5.5 %collective-permute-start.15 = (bf16[12,1536]{1,0:T(8,128)(2,1)S(1)}, bf16[12,1536]{1,0:T(8,128)(2,1)S(1)}, u32[]{:S(2)}, u32[]{:S(2)}) collective-permute-start(bf16[12,1536]{1,0:T(8,128)(2,1)S(1)} %get-tuple-element.55), channel_id=1, source_target_pairs={{0,16},{4,20},{8,24},{12,28},{16,0},{20,4},{24,8},{28,12},{1,17},{... | collective-permute-start | bytes 110600 | tf_op jit(solution)/shard_map/ppermute | solution.py:23
  37.6 5.4 %collective-permute-start.17 = (bf16[12,1536]{1,0:T(8,128)(2,1)S(1)}, bf16[12,1536]{1,0:T(8,128)(2,1)S(1)}, u32[]{:S(2)}, u32[]{:S(2)}) collective-permute-start(bf16[12,1536]{1,0:T(8,128)(2,1)S(1)} %slice.53), channel_id=1, source_target_pairs={{0,8},{4,12},{8,0},{12,4},{16,24},{20,28},{24,16},{28,20},{1,9},{5... | collective-permute-start | bytes 110600 | tf_op jit(solution)/shard_map/ppermute | solution.py:23

commit v7 on v6

--- a/solution.py
+++ b/solution.py
@@ -247,7 +247,8 @@
         [copied],
         limit=46,
     )(up_weight)
-    order = [0] + list(reversed(masks))
+    far_first = list(reversed(masks))
+    order = [0] + far_first[1:2] + far_first[:1] + far_first[2:]
     near = jnp.concatenate([patches] + [swap(patches, "tok", mask) for mask in order[1:]])
     near, loaded, norm_gain = lax.optimization_barrier((near, loaded, norm_gain))
     far = swap(near, "tok", 1)
@@ -319,7 +320,7 @@
         at = [order.index(mask) * tok_rows for mask in masks]
         return jnp.concatenate([array[start:start + tok_rows] for start in at])
 
-    first, second = order[1:1 + len(order) // 2], order[1 + len(order) // 2:] + [0]
+    first, second = far_first[:len(order) // 2], far_first[len(order) // 2:] + [0]
     summed = 0
     for group in (first, second):
         total = rows_of(near_sum, group) + swap(rows_of(far_sum, group), "tok", 1)

time: 43.8 us -> 43.6 us (level)
  no operation moved by 1% of the time
where the time goes in v7:
time: 43.6 us; the launch traced here: 43.5 us
  starting transfers between devices  18 us (41%)
  waiting for transfers between devices  12.9 us (30%)
  Pallas kernels  10.7 us (25%)
  between operations  0.95 us (2%)
  other arithmetic  0.85 us (2%)
    ppermute x18, starting transfers between devices, swap(): return lax.ppermute(block, axis, [(i, i ^ mask) for i in range(size)])  18 us
    ppermute x18, waiting for transfers between devices, swap(): return lax.ppermute(block, axis, [(i, i ^ mask) for i in range(size)])  12.9 us
    pallas_call x1, Pallas kernels, per_device(): call(load_rest_kernel, [((block_width, width), bf16)] * (parts - 1) + [((...  3.27 us
    pallas_call x3, Pallas kernels, per_device(): call(functools.partial(down_kernel, start, last), [((half, block_width),...  1.93 us
    pallas_call x1, Pallas kernels, per_device(): call(functools.partial(load_kernel, 0), [((block_width, width), bf16)], [...  1.9 us
    pallas_call x2, Pallas kernels, per_device(): call(up_products, outs, [in_vmem] * 2, flops=flops)(rows, weight)  1.33 us
    pallas_call x3, Pallas kernels, per_device(): call(functools.partial(gelu_kernel, start, hidden_width, block_width, ful...  0.92 us
  transfers between devices with their start and end apart: 18, of which 10 were waited for; matrix products, arithmetic and copies ran while one was open for 0% of the time, Pallas kernels for 21%

profile of v7, /device:TPU:0, one launch (start us, length us, event | category | flops | bytes accessed | tf_op | source)
XLA Modules:
  0.0 43.5 jit_solution(3948256161955120533)
XLA Ops:
  0.0 0.0 copy-start.2
  0.0 4.0 %collective-permute-start = (bf16[12,1536]{1,0:T(8,128)(2,1)}, bf16[12,1536]{1,0:T(8,128)(2,1)S(1)}, u32[]{:S(2)}, u32[]{:S(2)}) collective-permute-start(bf16[12,1536]{1,0:T(8,128)(2,1)} %param.8), channel_id=1, source_target_pairs={{0,16},{4,20},{8,24},{12,28},{16,0},{20,4},{24,8},{28,12},{1,17},{... | collective-permute-start | bytes 110600 | tf_op jit(solution)/shard_map/ppermute | solution.py:23
  4.0 1.3 %collective-permute-start.1 = (bf16[12,1536]{1,0:T(8,128)(2,1)}, bf16[12,1536]{1,0:T(8,128)(2,1)S(1)}, u32[]{:S(2)}, u32[]{:S(2)}) collective-permute-start(bf16[12,1536]{1,0:T(8,128)(2,1)} %param.8), channel_id=1, source_target_pairs={{0,24},{4,28},{8,16},{12,20},{16,8},{20,12},{24,0},{28,4},{1,25},{... | collective-permute-start | bytes 110600 | tf_op jit(solution)/shard_map/ppermute | solution.py:23
  5.4 0.2 collective-permute-start.2
  5.6 1.9 %shard_map.82.first_ref.weight_ref = bf16[1536,1024]{1,0:T(8,128)(2,1)S(1)} custom-call(bf16[1536,3072]{1,0:T(8,128)(2,1)} %weight_ref.6), custom_call_target="tpu_custom_call" | custom-call | tf_op jit(solution)/shard_map/pallas_call | solution.py:243
  7.5 0.0 collective-permute-done
  7.5 2.7 %collective-permute-done.1 = bf16[12,1536]{1,0:T(8,128)(2,1)S(1)} collective-permute-done((bf16[12,1536]{1,0:T(8,128)(2,1)}, bf16[12,1536]{1,0:T(8,128)(2,1)S(1)}, u32[]{:S(2)}, u32[]{:S(2)}) %collective-permute-start.1) | collective-permute-done | bytes 36896 | tf_op jit(solution)/shard_map/ppermute | solution.py:23
  10.2 0.0 collective-permute-done.2
  10.2 0.0 copy-done.2
  10.3 1.6 %collective-permute-start.3 = (bf16[48,1536]{1,0:T(8,128)(2,1)S(1)}, bf16[48,1536]{1,0:T(8,128)(2,1)S(1)}, u32[]{:S(2)}, u32[]{:S(2)}) collective-permute-start(bf16[48,1536]{1,0:T(8,128)(2,1)S(1)} %pad_maximum_fusion.near_ref), channel_id=1, source_target_pairs={{0,4},{4,0},{8,12},{12,8},{16,20},{20,16},{24,28},{28,24},{1,5},{5... | collective-permute-start | bytes 442376 | tf_op jit(solution)/shard_map/ppermute | solution.py:23
  11.8 0.0 copy-done.1
  11.8 3.3 %shard_map.83 = (bf16[1536,1024]{1,0:T(8,128)(2,1)S(1)}, bf16[1536,1024]{1,0:T(8,128)(2,1)S(1)}, f32[1,3072]{1,0:T(1,128)S(1)}, bf16[48,128]{1,0:T(8,128)(2,1)S(1)}) custom-call(f32[1536]{0:T(1024)S(1)} %copy-done.1, bf16[1536,1024]{1,0:T(8,128)(2,1)S(1)} %shard_map.82.first_ref.weight_ref, bf16[1536,3072]{1,0:T(8,128)(2,1)} %weight_ref.6), custom_call_target="tpu_custom_call" | custom-call | flops 1207959552 | tf_op jit(solution)/shard_map/pallas_call | solution.py:255
  15.1 0.4 collective-permute-done.3.far_ref
  15.5 0.8 %shard_map.84 = (bf16[96,1536]{1,0:T(8,128)(2,1)S(1)}, bf16[48,128]{1,0:T(8,128)(2,1)S(1)}, f32[48,1024]{1,0:T(8,128)S(1)}, bf16[48,1280]{1,0:T(8,128)(2,1)S(1)}) custom-call(bf16[48,1536]{1,0:T(8,128)(2,1)S(1)} %pad_maximum_fusion.near_ref, bf16[48,1536]{1,0:T(8,128)(2,1)S(1)} %collective-permute-done.3.far_ref, f32[1536]{0:T(1024)S(1)} %copy-done.1, ...), custom_call_target="tpu_custom_call" | custom-call | flops 2415919104 | tf_op jit(solution)/shard_map/pallas_call | solution.py:274
  16.3 0.1 collective-permute-start.4
  16.3 0.0 slice-start
  16.4 0.0 slice-start.1
  16.4 0.7 %shard_map.89 = (f32[48,1024]{1,0:T(8,128)S(1)}, bf16[48,1024]{1,0:T(8,128)(2,1)S(1)}) custom-call(bf16[96,1536]{1,0:T(8,128)(2,1)S(1)} %get-tuple-element.32.rows_ref, bf16[1536,1024]{1,0:T(8,128)(2,1)S(1)} %get-tuple-element.43.weight_ref), custom_call_target="tpu_custom_call" | custom-call | flops 2415919104 | tf_op jit(solution)/shard_map/pallas_call | solution.py:281
  17.0 0.5 %collective-permute-start.9 = (bf16[48,1024]{1,0:T(8,128)(2,1)S(1)}, bf16[48,1024]{1,0:T(8,128)(2,1)S(1)}, u32[]{:S(2)}, u32[]{:S(2)}) collective-permute-start(bf16[48,1024]{1,0:T(8,128)(2,1)S(1)} %get-tuple-element.45), channel_id=1, source_target_pairs={{0,1},{1,0},{2,3},{3,2},{4,5},{5,4},{6,7},{7,6},{8,9},{9,8},{10,11... | collective-permute-start | bytes 294920 | tf_op jit(solution)/shard_map/ppermute | solution.py:23
  17.6 0.1 collective-permute-done.4.packed_ref.other_ref
  17.7 0.2 shard_map.87
  17.9 1.6 %collective-permute-start.6 = (bf16[48,1280]{1,0:T(8,128)(2,1)S(1)}, bf16[48,1280]{1,0:T(8,128)(2,1)S(1)}, u32[]{:S(2)}, u32[]{:S(2)}) collective-permute-start(bf16[48,1280]{1,0:T(8,128)(2,1)S(1)} %get-tuple-element.41.refs_0_), channel_id=1, source_target_pairs={{0,2},{1,3},{2,0},{3,1},{4,6},{5,7},{6,4},{7,5},{8,10},{9,11},{10,... | collective-permute-start | bytes 368648 | tf_op jit(solution)/shard_map/ppermute | solution.py:23
  19.5 0.7 %shard_map.85 = (f32[48,1024]{1,0:T(8,128)S(1)}, bf16[48,1024]{1,0:T(8,128)(2,1)S(1)}) custom-call(bf16[96,1536]{1,0:T(8,128)(2,1)S(1)} %get-tuple-element.32.rows_ref, bf16[1536,1024]{1,0:T(8,128)(2,1)S(1)} %get-tuple-element.33.weight_ref), custom_call_target="tpu_custom_call" | custom-call | flops 2415919104 | tf_op jit(solution)/shard_map/pallas_call | solution.py:281
  20.1 0.1 collective-permute-start.5
  20.2 0.0 collective-permute-done.9.other_ref
  20.2 0.2 shard_map.90
  20.4 0.6 %collective-permute-start.10 = (bf16[48,1024]{1,0:T(8,128)(2,1)S(1)}, bf16[48,1024]{1,0:T(8,128)(2,1)S(1)}, u32[]{:S(2)}, u32[]{:S(2)}) collective-permute-start(bf16[48,1024]{1,0:T(8,128)(2,1)S(1)} %get-tuple-element.47), channel_id=1, source_target_pairs={{0,2},{1,3},{2,0},{3,1},{4,6},{5,7},{6,4},{7,5},{8,10},{9,11},{10,... | collective-permute-start | bytes 294920 | tf_op jit(solution)/shard_map/ppermute | solution.py:23
  21.0 0.5 %collective-permute-done.5.other_ref = bf16[48,1024]{1,0:T(8,128)(2,1)S(1)} collective-permute-done((bf16[48,1024]{1,0:T(8,128)(2,1)S(1)}, bf16[48,1024]{1,0:T(8,128)(2,1)S(1)}, u32[]{:S(2)}, u32[]{:S(2)}) %collective-permute-start.5) | collective-permute-done | bytes 98336 | tf_op jit(solution)/shard_map/ppermute | solution.py:23
  21.5 0.2 shard_map.86
  21.7 1.1 %collective-permute-start.7 = (bf16[48,1024]{1,0:T(8,128)(2,1)S(1)}, bf16[48,1024]{1,0:T(8,128)(2,1)S(1)}, u32[]{:S(2)}, u32[]{:S(2)}) collective-permute-start(bf16[48,1024]{1,0:T(8,128)(2,1)S(1)} %get-tuple-element.42), channel_id=1, source_target_pairs={{0,2},{1,3},{2,0},{3,1},{4,6},{5,7},{6,4},{7,5},{8,10},{9,11},{10,... | collective-permute-start | bytes 294920 | tf_op jit(solution)/shard_map/ppermute | solution.py:23
  22.7 0.6 %collective-permute-done.6.refs_1_ = bf16[48,1280]{1,0:T(8,128)(2,1)S(1)} collective-permute-done((bf16[48,1280]{1,0:T(8,128)(2,1)S(1)}, bf16[48,1280]{1,0:T(8,128)(2,1)S(1)}, u32[]{:S(2)}, u32[]{:S(2)}) %collective-permute-start.6) | collective-permute-done | bytes 122912 | tf_op jit(solution)/shard_map/ppermute | solution.py:23
  23.3 0.0 copy-done
  23.3 0.3 shard_map.92.kept_ref
  23.6 0.1 collective-permute-start.12
  24.3 1.7 %collective-permute-done.10.refs_2_ = bf16[48,1024]{1,0:T(8,128)(2,1)S(1)} collective-permute-done((bf16[48,1024]{1,0:T(8,128)(2,1)S(1)}, bf16[48,1024]{1,0:T(8,128)(2,1)S(1)}, u32[]{:S(2)}, u32[]{:S(2)}) %collective-permute-start.10) | collective-permute-done | bytes 98336 | tf_op jit(solution)/shard_map/ppermute | solution.py:23
  26.0 0.3 shard_map.91.kept_ref
  26.4 0.1 collective-permute-start.11
  26.4 1.3 %collective-permute-done.7.refs_2_ = bf16[48,1024]{1,0:T(8,128)(2,1)S(1)} collective-permute-done((bf16[48,1024]{1,0:T(8,128)(2,1)S(1)}, bf16[48,1024]{1,0:T(8,128)(2,1)S(1)}, u32[]{:S(2)}, u32[]{:S(2)}) %collective-permute-start.7) | collective-permute-done | bytes 98336 | tf_op jit(solution)/shard_map/ppermute | solution.py:23
  27.8 0.3 shard_map.88.kept_ref
  28.1 0.1 collective-permute-start.8
  28.1 0.0 collective-permute-done.12.given_ref
  28.2 0.0 slice-done
  28.2 0.0 slice-done.1
  28.2 0.0 slice-done.2
  28.2 0.6 %shard_map.93.refs_0_ = f32[96,1536]{1,0:T(8,128)S(1)} custom-call(bf16[48,1024]{1,0:T(8,128)(2,1)S(1)} %shard_map.92.kept_ref, bf16[48,1024]{1,0:T(8,128)(2,1)S(1)} %collective-permute-done.12.given_ref, bf16[3072,1536]{1,0:T(8,128)(2,1)S(1)} %bitcast.4), custom_call_target="tpu_custom_call" | custom-call | flops 2415919104 | tf_op jit(solution)/shard_map/pallas_call | solution.py:308
  28.8 0.0 collective-permute-done.11.given_ref
  28.8 0.6 %shard_map.94.refs_0_ = f32[96,1536]{1,0:T(8,128)S(1)} custom-call(bf16[48,1024]{1,0:T(8,128)(2,1)S(1)} %shard_map.91.kept_ref, bf16[48,1024]{1,0:T(8,128)(2,1)S(1)} %collective-permute-done.11.given_ref, bf16[3072,1536]{1,0:T(8,128)(2,1)S(1)} %bitcast.4, f32[96,1536]{1,0:T(8,128)S(1)} %shard_map.93.refs_0_), custom_call_target="tpu_custom_call" | custom-call | flops 2415919104 | tf_op jit(solution)/shard_map/pallas_call | solution.py:308
  29.5 0.0 copy-start.4
  29.5 0.0 copy-start.3
  29.5 0.0 collective-permute-done.8.given_ref
  29.5 0.7 %shard_map.95 = (f32[48,1536]{1,0:T(8,128)S(1)}, bf16[48,1536]{1,0:T(8,128)(2,1)S(1)}) custom-call(bf16[48,1024]{1,0:T(8,128)(2,1)S(1)} %shard_map.88.kept_ref, bf16[48,1024]{1,0:T(8,128)(2,1)S(1)} %collective-permute-done.8.given_ref, bf16[3072,1536]{1,0:T(8,128)(2,1)S(1)} %bitcast.4, f32[96,1536]{1,0:T(8,128)S(1)} %shard_map.94.refs_0_), custom_call_target="tpu_custom_call" | custom-call | flops 2415919104 | tf_op jit(solution)/shard_map/pallas_call | solution.py:308
  30.2 1.6 %collective-permute-start.13 = (bf16[24,1536]{1,0:T(8,128)(2,1)S(1)}, bf16[24,1536]{1,0:T(8,128)(2,1)S(1)}, u32[]{:S(2)}, u32[]{:S(2)}) collective-permute-start(bf16[24,1536]{1,0:T(8,128)(2,1)S(1)} %pad_maximum_fusion.1), channel_id=1, source_target_pairs={{0,4},{4,0},{8,12},{12,8},{16,20},{20,16},{24,28},{28,24},{1,5},{5... | collective-permute-start | bytes 221192 | tf_op jit(solution)/shard_map/ppermute | solution.py:23
  31.9 0.6 %collective-permute-start.16 = (bf16[24,1536]{1,0:T(8,128)(2,1)S(1)}, bf16[24,1536]{1,0:T(8,128)(2,1)S(1)}, u32[]{:S(2)}, u32[]{:S(2)}) collective-permute-start(bf16[24,1536]{1,0:T(8,128)(2,1)S(1)} %pad_maximum_fusion.2), channel_id=1, source_target_pairs={{0,4},{4,0},{8,12},{12,8},{16,20},{20,16},{24,28},{28,24},{1,5},{5... | collective-permute-start | bytes 221192 | tf_op jit(solution)/shard_map/ppermute | solution.py:23
  32.5 2.8 %collective-permute-done.13 = bf16[24,1536]{1,0:T(8,128)(2,1)S(1)} collective-permute-done((bf16[24,1536]{1,0:T(8,128)(2,1)S(1)}, bf16[24,1536]{1,0:T(8,128)(2,1)S(1)}, u32[]{:S(2)}, u32[]{:S(2)}) %collective-permute-start.13) | collective-permute-done | bytes 73760 | tf_op jit(solution)/shard_map/ppermute | solution.py:23
  35.3 2.4 %collective-permute-start.14 = (bf16[12,1536]{1,0:T(8,128)(2,1)S(1)}, bf16[12,1536]{1,0:T(8,128)(2,1)S(1)}, u32[]{:S(2)}, u32[]{:S(2)}) collective-permute-start(bf16[12,1536]{1,0:T(8,128)(2,1)S(1)} %get-tuple-element.60), channel_id=1, source_target_pairs={{0,24},{4,28},{8,16},{12,20},{16,8},{20,12},{24,0},{28,4},{1,25},{... | collective-permute-start | bytes 110600 | tf_op jit(solution)/shard_map/ppermute | solution.py:23
  37.7 0.0 collective-permute-start.15
  37.7 0.0 collective-permute-done.16
  37.7 2.1 %collective-permute-start.17 = (bf16[12,1536]{1,0:T(8,128)(2,1)S(1)}, bf16[12,1536]{1,0:T(8,128)(2,1)S(1)}, u32[]{:S(2)}, u32[]{:S(2)}) collective-permute-start(bf16[12,1536]{1,0:T(8,128)(2,1)S(1)} %slice.63), channel_id=1, source_target_pairs={{0,8},{4,12},{8,0},{12,4},{16,24},{20,28},{24,16},{28,20},{1,9},{5... | collective-permute-start | bytes 110600 | tf_op jit(solution)/shard_map/ppermute | solution.py:23
  39.9 0.0 copy-done.4
  39.9 1.5 %collective-permute-done.14 = bf16[12,1536]{1,0:T(8,128)(2,1)S(1)} collective-permute-done((bf16[12,1536]{1,0:T(8,128)(2,1)S(1)}, bf16[12,1536]{1,0:T(8,128)(2,1)S(1)}, u32[]{:S(2)}, u32[]{:S(2)}) %collective-permute-start.14) | collective-permute-done | bytes 36896 | tf_op jit(solution)/shard_map/ppermute | solution.py:23
  41.3 1.4 %collective-permute-done.15 = bf16[12,1536]{1,0:T(8,128)(2,1)S(1)} collective-permute-done((bf16[12,1536]{1,0:T(8,128)(2,1)S(1)}, bf16[12,1536]{1,0:T(8,128)(2,1)S(1)}, u32[]{:S(2)}, u32[]{:S(2)}) %collective-permute-start.15) | collective-permute-done | bytes 36896 | tf_op jit(solution)/shard_map/ppermute | solution.py:23
  42.8 0.0 collective-permute-done.17
  42.8 0.0 copy-done.3
  42.8 0.7 %fusion.3 = bf16[12,1536]{1,0:T(8,128)(2,1)} fusion(f32[24,1536]{1,0:T(8,128)S(1)} %maximum_add_fusion.1, f32[1536]{0:T(1024)S(1)} %copy-done.3, bf16[12,1536]{1,0:T(8,128)(2,1)S(1)} %collective-permute-done.17, bf16[12,1536]{1,0:T(8,128)(2,1)S(1)} %collective-permute-done.14, bf16[12,1536]{1,0:T(8,128)(2,1)S(1)} %collective-permute-done.15, ...), kind=kLoop, calls=%fused_computation.7 | loop fusion | flops 129024 | bytes 227376 | tf_op jit(solution)/shard_map/convert_element_type | solution.py:333
  (14 shorter events, 0.2 us)
Async XLA Ops:
  0.0 10.2 %copy-start.2 = (bf16[12,1536]{1,0:T(8,128)(2,1)S(1)}, bf16[12,1536]{1,0:T(8,128)(2,1)}, u32[]{:S(2)}) copy-start(bf16[12,1536]{1,0:T(8,128)(2,1)} %param.8) | copy-start | bytes 110596
  0.0 11.8 %copy-start.1 = (f32[1536]{0:T(1024)S(1)}, f32[1536]{0:T(1024)}, u32[]{:S(2)}) copy-start(f32[1536]{0:T(1024)} %gain_ref.1) | copy-start | bytes 18436
  0.0 7.5 %collective-permute-start = (bf16[12,1536]{1,0:T(8,128)(2,1)}, bf16[12,1536]{1,0:T(8,128)(2,1)S(1)}, u32[]{:S(2)}, u32[]{:S(2)}) collective-permute-start(bf16[12,1536]{1,0:T(8,128)(2,1)} %param.8), channel_id=1, source_target_pairs={{0,16},{4,20},{8,24},{12,28},{16,0},{20,4},{24,8},{28,12},{1,17},{... | collective-permute-start | bytes 110600 | tf_op jit(solution)/shard_map/ppermute | solution.py:23
  4.0 6.2 %collective-permute-start.1 = (bf16[12,1536]{1,0:T(8,128)(2,1)}, bf16[12,1536]{1,0:T(8,128)(2,1)S(1)}, u32[]{:S(2)}, u32[]{:S(2)}) collective-permute-start(bf16[12,1536]{1,0:T(8,128)(2,1)} %param.8), channel_id=1, source_target_pairs={{0,24},{4,28},{8,16},{12,20},{16,8},{20,12},{24,0},{28,4},{1,25},{... | collective-permute-start | bytes 110600 | tf_op jit(solution)/shard_map/ppermute | solution.py:23
  5.4 4.8 %collective-permute-start.2 = (bf16[12,1536]{1,0:T(8,128)(2,1)}, bf16[12,1536]{1,0:T(8,128)(2,1)S(1)}, u32[]{:S(2)}, u32[]{:S(2)}) collective-permute-start(bf16[12,1536]{1,0:T(8,128)(2,1)} %param.8), channel_id=1, source_target_pairs={{0,8},{4,12},{8,0},{12,4},{16,24},{20,28},{24,16},{28,20},{1,9},{5... | collective-permute-start | bytes 110600 | tf_op jit(solution)/shard_map/ppermute | solution.py:23
  10.3 5.2 %collective-permute-start.3 = (bf16[48,1536]{1,0:T(8,128)(2,1)S(1)}, bf16[48,1536]{1,0:T(8,128)(2,1)S(1)}, u32[]{:S(2)}, u32[]{:S(2)}) collective-permute-start(bf16[48,1536]{1,0:T(8,128)(2,1)S(1)} %pad_maximum_fusion.near_ref), channel_id=1, source_target_pairs={{0,4},{4,0},{8,12},{12,8},{16,20},{20,16},{24,28},{28,24},{1,5},{5... | collective-permute-start | bytes 442376 | tf_op jit(solution)/shard_map/ppermute | solution.py:23
  16.3 1.4 %collective-permute-start.4 = (bf16[48,1280]{1,0:T(8,128)(2,1)S(1)}, bf16[48,1280]{1,0:T(8,128)(2,1)S(1)}, u32[]{:S(2)}, u32[]{:S(2)}) collective-permute-start(bf16[48,1280]{1,0:T(8,128)(2,1)S(1)} %get-tuple-element.37), channel_id=1, source_target_pairs={{0,1},{1,0},{2,3},{3,2},{4,5},{5,4},{6,7},{7,6},{8,9},{9,8},{10,11... | collective-permute-start | bytes 368648 | tf_op jit(solution)/shard_map/ppermute | solution.py:23
  16.3 11.8 %slice-start = ((s8[9437184]{0:T(1024)(128)(4,1)}), s8[4194304]{0:T(1024)(128)(4,1)S(1)}, s32[]{:S(2)}) async-start(s8[9437184]{0:T(1024)(128)(4,1)} %bitcast.3), calls=%async_computation | async-start | bytes 8388608
  16.4 11.8 %slice-start.1 = ((s8[9437184]{0:T(1024)(128)(4,1)}), s8[4194304]{0:T(1024)(128)(4,1)S(1)}, s32[]{:S(2)}) async-start(s8[9437184]{0:T(1024)(128)(4,1)} %bitcast.3), calls=%async_computation.1 | async-start | bytes 8388608
  17.0 3.2 %collective-permute-start.9 = (bf16[48,1024]{1,0:T(8,128)(2,1)S(1)}, bf16[48,1024]{1,0:T(8,128)(2,1)S(1)}, u32[]{:S(2)}, u32[]{:S(2)}) collective-permute-start(bf16[48,1024]{1,0:T(8,128)(2,1)S(1)} %get-tuple-element.45), channel_id=1, source_target_pairs={{0,1},{1,0},{2,3},{3,2},{4,5},{5,4},{6,7},{7,6},{8,9},{9,8},{10,11... | collective-permute-start | bytes 294920 | tf_op jit(solution)/shard_map/ppermute | solution.py:23
  17.9 5.4 %collective-permute-start.6 = (bf16[48,1280]{1,0:T(8,128)(2,1)S(1)}, bf16[48,1280]{1,0:T(8,128)(2,1)S(1)}, u32[]{:S(2)}, u32[]{:S(2)}) collective-permute-start(bf16[48,1280]{1,0:T(8,128)(2,1)S(1)} %get-tuple-element.41.refs_0_), channel_id=1, source_target_pairs={{0,2},{1,3},{2,0},{3,1},{4,6},{5,7},{6,4},{7,5},{8,10},{9,11},{10,... | collective-permute-start | bytes 368648 | tf_op jit(solution)/shard_map/ppermute | solution.py:23
  19.4 3.9 %copy-start = (f32[3072]{0:T(1024)S(1)}, f32[3072]{0:T(1024)}, u32[]{:S(2)}) copy-start(f32[3072]{0:T(1024)} %param.13) | copy-start | bytes 36868
  19.4 8.7 %slice-start.2 = ((s8[9437184]{0:T(1024)(128)(4,1)}), s8[1048576]{0:T(1024)(128)(4,1)S(1)}, s32[]{:S(2)}) async-start(s8[9437184]{0:T(1024)(128)(4,1)} %bitcast.3), calls=%async_computation.2 | async-start | bytes 2097152
  20.1 1.4 %collective-permute-start.5 = (bf16[48,1024]{1,0:T(8,128)(2,1)S(1)}, bf16[48,1024]{1,0:T(8,128)(2,1)S(1)}, u32[]{:S(2)}, u32[]{:S(2)}) collective-permute-start(bf16[48,1024]{1,0:T(8,128)(2,1)S(1)} %get-tuple-element.38), channel_id=1, source_target_pairs={{0,1},{1,0},{2,3},{3,2},{4,5},{5,4},{6,7},{7,6},{8,9},{9,8},{10,11... | collective-permute-start | bytes 294920 | tf_op jit(solution)/shard_map/ppermute | solution.py:23
  20.4 5.7 %collective-permute-start.10 = (bf16[48,1024]{1,0:T(8,128)(2,1)S(1)}, bf16[48,1024]{1,0:T(8,128)(2,1)S(1)}, u32[]{:S(2)}, u32[]{:S(2)}) collective-permute-start(bf16[48,1024]{1,0:T(8,128)(2,1)S(1)} %get-tuple-element.47), channel_id=1, source_target_pairs={{0,2},{1,3},{2,0},{3,1},{4,6},{5,7},{6,4},{7,5},{8,10},{9,11},{10,... | collective-permute-start | bytes 294920 | tf_op jit(solution)/shard_map/ppermute | solution.py:23
  21.7 6.1 %collective-permute-start.7 = (bf16[48,1024]{1,0:T(8,128)(2,1)S(1)}, bf16[48,1024]{1,0:T(8,128)(2,1)S(1)}, u32[]{:S(2)}, u32[]{:S(2)}) collective-permute-start(bf16[48,1024]{1,0:T(8,128)(2,1)S(1)} %get-tuple-element.42), channel_id=1, source_target_pairs={{0,2},{1,3},{2,0},{3,1},{4,6},{5,7},{6,4},{7,5},{8,10},{9,11},{10,... | collective-permute-start | bytes 294920 | tf_op jit(solution)/shard_map/ppermute | solution.py:23
  23.6 4.5 %collective-permute-start.12 = (bf16[48,1024]{1,0:T(8,128)(2,1)S(1)}, bf16[48,1024]{1,0:T(8,128)(2,1)S(1)}, u32[]{:S(2)}, u32[]{:S(2)}) collective-permute-start(bf16[48,1024]{1,0:T(8,128)(2,1)S(1)} %shard_map.92.kept_ref), channel_id=1, source_target_pairs={{0,1},{1,0},{2,3},{3,2},{4,5},{5,4},{6,7},{7,6},{8,9},{9,8},{10,11... | collective-permute-start | bytes 294920 | tf_op jit(solution)/shard_map/ppermute | solution.py:23
  26.4 2.5 %collective-permute-start.11 = (bf16[48,1024]{1,0:T(8,128)(2,1)S(1)}, bf16[48,1024]{1,0:T(8,128)(2,1)S(1)}, u32[]{:S(2)}, u32[]{:S(2)}) collective-permute-start(bf16[48,1024]{1,0:T(8,128)(2,1)S(1)} %shard_map.91.kept_ref), channel_id=1, source_target_pairs={{0,1},{1,0},{2,3},{3,2},{4,5},{5,4},{6,7},{7,6},{8,9},{9,8},{10,11... | collective-permute-start | bytes 294920 | tf_op jit(solution)/shard_map/ppermute | solution.py:23
  28.1 1.4 %collective-permute-start.8 = (bf16[48,1024]{1,0:T(8,128)(2,1)S(1)}, bf16[48,1024]{1,0:T(8,128)(2,1)S(1)}, u32[]{:S(2)}, u32[]{:S(2)}) collective-permute-start(bf16[48,1024]{1,0:T(8,128)(2,1)S(1)} %shard_map.88.kept_ref), channel_id=1, source_target_pairs={{0,1},{1,0},{2,3},{3,2},{4,5},{5,4},{6,7},{7,6},{8,9},{9,8},{10,11... | collective-permute-start | bytes 294920 | tf_op jit(solution)/shard_map/ppermute | solution.py:23
  29.5 10.4 %copy-start.4 = (s32[12]{0:T(128)S(1)}, s32[12]{0:T(128)}, u32[]{:S(2)}) copy-start(s32[12]{0:T(128)} %param.10) | copy-start | bytes 148
  29.5 13.3 %copy-start.3 = (f32[1536]{0:T(1024)S(1)}, f32[1536]{0:T(1024)}, u32[]{:S(2)}) copy-start(f32[1536]{0:T(1024)} %param.15) | copy-start | bytes 18436
  30.2 5.0 %collective-permute-start.13 = (bf16[24,1536]{1,0:T(8,128)(2,1)S(1)}, bf16[24,1536]{1,0:T(8,128)(2,1)S(1)}, u32[]{:S(2)}, u32[]{:S(2)}) collective-permute-start(bf16[24,1536]{1,0:T(8,128)(2,1)S(1)} %pad_maximum_fusion.1), channel_id=1, source_target_pairs={{0,4},{4,0},{8,12},{12,8},{16,20},{20,16},{24,28},{28,24},{1,5},{5... | collective-permute-start | bytes 221192 | tf_op jit(solution)/shard_map/ppermute | solution.py:23
  31.9 5.8 %collective-permute-start.16 = (bf16[24,1536]{1,0:T(8,128)(2,1)S(1)}, bf16[24,1536]{1,0:T(8,128)(2,1)S(1)}, u32[]{:S(2)}, u32[]{:S(2)}) collective-permute-start(bf16[24,1536]{1,0:T(8,128)(2,1)S(1)} %pad_maximum_fusion.2), channel_id=1, source_target_pairs={{0,4},{4,0},{8,12},{12,8},{16,20},{20,16},{24,28},{28,24},{1,5},{5... | collective-permute-start | bytes 221192 | tf_op jit(solution)/shard_map/ppermute | solution.py:23
  35.3 6.1 %collective-permute-start.14 = (bf16[12,1536]{1,0:T(8,128)(2,1)S(1)}, bf16[12,1536]{1,0:T(8,128)(2,1)S(1)}, u32[]{:S(2)}, u32[]{:S(2)}) collective-permute-start(bf16[12,1536]{1,0:T(8,128)(2,1)S(1)} %get-tuple-element.60), channel_id=1, source_target_pairs={{0,24},{4,28},{8,16},{12,20},{16,8},{20,12},{24,0},{28,4},{1,25},{... | collective-permute-start | bytes 110600 | tf_op jit(solution)/shard_map/ppermute | solution.py:23
  37.7 5.1 %collective-permute-start.15 = (bf16[12,1536]{1,0:T(8,128)(2,1)S(1)}, bf16[12,1536]{1,0:T(8,128)(2,1)S(1)}, u32[]{:S(2)}, u32[]{:S(2)}) collective-permute-start(bf16[12,1536]{1,0:T(8,128)(2,1)S(1)} %get-tuple-element.59), channel_id=1, source_target_pairs={{0,16},{4,20},{8,24},{12,28},{16,0},{20,4},{24,8},{28,12},{1,17},{... | collective-permute-start | bytes 110600 | tf_op jit(solution)/shard_map/ppermute | solution.py:23
  37.7 5.0 %collective-permute-start.17 = (bf16[12,1536]{1,0:T(8,128)(2,1)S(1)}, bf16[12,1536]{1,0:T(8,128)(2,1)S(1)}, u32[]{:S(2)}, u32[]{:S(2)}) collective-permute-start(bf16[12,1536]{1,0:T(8,128)(2,1)S(1)} %slice.63), channel_id=1, source_target_pairs={{0,8},{4,12},{8,0},{12,4},{16,24},{20,28},{24,16},{28,20},{1,9},{5... | collective-permute-start | bytes 110600 | tf_op jit(solution)/shard_map/ppermute | solution.py:23

commit v8 on v7

--- a/solution.py
+++ b/solution.py
@@ -197,18 +197,20 @@
         out_ref[:, cut] = active.astype(jnp.bfloat16)
 
 
-def down_kernel(start, last, kept_ref, given_ref, weight_ref, *refs):
-    half, depth = kept_ref.shape
+def down_kernel(start, count, last, *refs):
+    actives, weight_ref, refs = refs[:2 * count], refs[2 * count], refs[2 * count + 1:]
+    half, width = actives[0].shape
     rows_ref = refs[-1]
-    rows_ref[:half] = kept_ref[...]
-    rows_ref[half:] = given_ref[...]
+    for part in range(count):
+        cut = slice(part * width, (part + 1) * width)
+        rows_ref[:half, cut] = actives[2 * part][...]
+        rows_ref[half:, cut] = actives[2 * part + 1][...]
     first = is_first_core()
-    width = weight_ref.shape[1]
-    tile = tile_of(width)
-    for at in range(0, width, tile):
+    tile = tile_of(weight_ref.shape[1])
+    for at in range(0, weight_ref.shape[1], tile):
         cut = slice(at, at + tile)
         product = jnp.dot(
-            rows_ref[...], weight_ref[start:start + depth, cut], preferred_element_type=jnp.float32
+            rows_ref[...], weight_ref[start:start + count * width, cut], preferred_element_type=jnp.float32
         )
         if start:
             product = product + refs[0][:, cut]
@@ -295,7 +297,7 @@
         sums.append(pair_sum)
         sents.append(sent)
     arrived = [[swap(sent, "feat", mask) for mask in peers] for sent in sents]
-    total = ()
+    total, actives = (), {}
     for start, pair_sum, partners in zip(starts, sums, arrived):
         partners = partners if start else []
         (active,) = call(
@@ -304,16 +306,19 @@
             [in_vmem] * (3 + len(peers) + len(partners)),
             [pltpu.VMEM((1 + len(peers), half, side), f32)],
         )(up_bias[None, :], pair_sum, sents[0], *arrived[0], *partners)
-        last = start == starts[-1]
-        total = call(
-            functools.partial(down_kernel, start, last),
-            [((half, block_width), f32), ((half, block_width), bf16)]
-            if last
-            else [((2 * half, block_width), f32)],
-            [in_vmem] * (3 + len(total)),
-            [pltpu.VMEM((2 * half, width), bf16)],
-            flops=4 * half * width * block_width,
-        )(active, swap(active, "feat", 1), down_weight, *total)
+        actives[start] = (active, swap(active, "feat", 1))
+    for group in (starts[:-1], starts[-1:]):
+        last = starts[-1] in group
+        if len(group) > 0:
+            total = call(
+                functools.partial(down_kernel, group[0], len(group), last),
+                [((half, block_width), f32), ((half, block_width), bf16)]
+                if last
+                else [((2 * half, block_width), f32)],
+                [in_vmem] * (2 * len(group) + 1 + len(total)),
+                [pltpu.VMEM((2 * half, len(group) * width), bf16)],
+                flops=4 * half * len(group) * width * block_width,
+            )(*[block for start in group for block in actives[start]], down_weight, *total)
     near_sum, far_sum = total
 
     def rows_of(array, masks):

time: 43.6 us -> 43.7 us (level)
  starting transfers between devices: 18 us -> 18.5 us
    ppermute x18, starting transfers between devices: 18 us -> 18.5 us  [swap(): return lax.ppermute(block, axis, [(i, i ^ mask) for i in range(size)])]
    pallas_call x3 -> x2, Pallas kernels: 1.93 us -> 1.76 us  [per_device(): call(functools.partial(down_kernel, group[0], len(group), last), [((half,...]
  transfers between devices with their start and end apart: 18 -> 18, of which waited for: 10 -> 9; matrix products, arithmetic and copies ran while one was open for 0% -> 0% of each run, Pallas kernels for 21% -> 21%
where the time goes in v8:
time: 43.7 us; the launch traced here: 43.5 us
  starting transfers between devices  18.5 us (42%)
  waiting for transfers between devices  12.8 us (29%)
  Pallas kernels  10.4 us (24%)
  between operations  0.93 us (2%)
  other arithmetic  0.85 us (2%)
    ppermute x18, starting transfers between devices, swap(): return lax.ppermute(block, axis, [(i, i ^ mask) for i in range(size)])  18.5 us
    ppermute x18, waiting for transfers between devices, swap(): return lax.ppermute(block, axis, [(i, i ^ mask) for i in range(size)])  12.8 us
    pallas_call x1, Pallas kernels, per_device(): call(load_rest_kernel, [((block_width, width), bf16)] * (parts - 1) + [((...  3.27 us
    pallas_call x1, Pallas kernels, per_device(): call(functools.partial(load_kernel, 0), [((block_width, width), bf16)], [...  1.9 us
    pallas_call x2, Pallas kernels, per_device(): call(functools.partial(down_kernel, group[0], len(group), last), [((half,...  1.76 us
    pallas_call x2, Pallas kernels, per_device(): call(up_products, outs, [in_vmem] * 2, flops=flops)(rows, weight)  1.26 us
    pallas_call x3, Pallas kernels, per_device(): call(functools.partial(gelu_kernel, start, hidden_width, block_width, ful...  0.93 us
  transfers between devices with their start and end apart: 18, of which 9 were waited for; matrix products, arithmetic and copies ran while one was open for 0% of the time, Pallas kernels for 21%

profile of v8, /device:TPU:0, one launch (start us, length us, event | category | flops | bytes accessed | tf_op | source)
XLA Modules:
  0.0 43.5 jit_solution(4622173692027441461)
XLA Ops:
  0.0 0.0 copy-start.2
  0.0 0.0 copy-start.1
  0.0 4.0 %collective-permute-start = (bf16[12,1536]{1,0:T(8,128)(2,1)}, bf16[12,1536]{1,0:T(8,128)(2,1)S(1)}, u32[]{:S(2)}, u32[]{:S(2)}) collective-permute-start(bf16[12,1536]{1,0:T(8,128)(2,1)} %param.8), channel_id=1, source_target_pairs={{0,16},{4,20},{8,24},{12,28},{16,0},{20,4},{24,8},{28,12},{1,17},{... | collective-permute-start | bytes 110600 | tf_op jit(solution)/shard_map/ppermute | solution.py:23
  4.0 1.3 %collective-permute-start.1 = (bf16[12,1536]{1,0:T(8,128)(2,1)}, bf16[12,1536]{1,0:T(8,128)(2,1)S(1)}, u32[]{:S(2)}, u32[]{:S(2)}) collective-permute-start(bf16[12,1536]{1,0:T(8,128)(2,1)} %param.8), channel_id=1, source_target_pairs={{0,24},{4,28},{8,16},{12,20},{16,8},{20,12},{24,0},{28,4},{1,25},{... | collective-permute-start | bytes 110600 | tf_op jit(solution)/shard_map/ppermute | solution.py:23
  5.4 0.2 collective-permute-start.2
  5.6 1.9 %shard_map.82.first_ref.weight_ref = bf16[1536,1024]{1,0:T(8,128)(2,1)S(1)} custom-call(bf16[1536,3072]{1,0:T(8,128)(2,1)} %weight_ref.3), custom_call_target="tpu_custom_call" | custom-call | tf_op jit(solution)/shard_map/pallas_call | solution.py:245
  7.5 0.0 collective-permute-done
  7.5 2.7 %collective-permute-done.1 = bf16[12,1536]{1,0:T(8,128)(2,1)S(1)} collective-permute-done((bf16[12,1536]{1,0:T(8,128)(2,1)}, bf16[12,1536]{1,0:T(8,128)(2,1)S(1)}, u32[]{:S(2)}, u32[]{:S(2)}) %collective-permute-start.1) | collective-permute-done | bytes 36896 | tf_op jit(solution)/shard_map/ppermute | solution.py:23
  10.2 0.0 collective-permute-done.2
  10.2 0.0 copy-done.2
  10.3 1.6 %collective-permute-start.3 = (bf16[48,1536]{1,0:T(8,128)(2,1)S(1)}, bf16[48,1536]{1,0:T(8,128)(2,1)S(1)}, u32[]{:S(2)}, u32[]{:S(2)}) collective-permute-start(bf16[48,1536]{1,0:T(8,128)(2,1)S(1)} %pad_maximum_fusion.near_ref), channel_id=1, source_target_pairs={{0,4},{4,0},{8,12},{12,8},{16,20},{20,16},{24,28},{28,24},{1,5},{5... | collective-permute-start | bytes 442376 | tf_op jit(solution)/shard_map/ppermute | solution.py:23
  11.8 0.0 copy-done.1
  11.8 3.3 %shard_map.83 = (bf16[1536,1024]{1,0:T(8,128)(2,1)S(1)}, bf16[1536,1024]{1,0:T(8,128)(2,1)S(1)}, f32[1,3072]{1,0:T(1,128)S(1)}, bf16[48,128]{1,0:T(8,128)(2,1)S(1)}) custom-call(f32[1536]{0:T(1024)S(1)} %copy-done.1, bf16[1536,1024]{1,0:T(8,128)(2,1)S(1)} %shard_map.82.first_ref.weight_ref, bf16[1536,3072]{1,0:T(8,128)(2,1)} %weight_ref.3), custom_call_target="tpu_custom_call" | custom-call | flops 1207959552 | tf_op jit(solution)/shard_map/pallas_call | solution.py:257
  15.1 0.4 collective-permute-done.3.far_ref
  15.5 0.8 %shard_map.84 = (bf16[96,1536]{1,0:T(8,128)(2,1)S(1)}, bf16[48,128]{1,0:T(8,128)(2,1)S(1)}, f32[48,1024]{1,0:T(8,128)S(1)}, bf16[48,1280]{1,0:T(8,128)(2,1)S(1)}) custom-call(bf16[48,1536]{1,0:T(8,128)(2,1)S(1)} %pad_maximum_fusion.near_ref, bf16[48,1536]{1,0:T(8,128)(2,1)S(1)} %collective-permute-done.3.far_ref, f32[1536]{0:T(1024)S(1)} %copy-done.1, ...), custom_call_target="tpu_custom_call" | custom-call | flops 2415919104 | tf_op jit(solution)/shard_map/pallas_call | solution.py:276
  16.3 0.1 collective-permute-start.4
  16.3 0.0 slice-start
  16.3 0.0 slice-start.1
  16.4 0.6 %shard_map.90 = (f32[48,1024]{1,0:T(8,128)S(1)}, bf16[48,1024]{1,0:T(8,128)(2,1)S(1)}) custom-call(bf16[96,1536]{1,0:T(8,128)(2,1)S(1)} %get-tuple-element.32.rows_ref, bf16[1536,1024]{1,0:T(8,128)(2,1)S(1)} %get-tuple-element.44.weight_ref), custom_call_target="tpu_custom_call" | custom-call | flops 2415919104 | tf_op jit(solution)/shard_map/pallas_call | solution.py:283
  17.0 0.5 %collective-permute-start.10 = (bf16[48,1024]{1,0:T(8,128)(2,1)S(1)}, bf16[48,1024]{1,0:T(8,128)(2,1)S(1)}, u32[]{:S(2)}, u32[]{:S(2)}) collective-permute-start(bf16[48,1024]{1,0:T(8,128)(2,1)S(1)} %get-tuple-element.46), channel_id=1, source_target_pairs={{0,1},{1,0},{2,3},{3,2},{4,5},{5,4},{6,7},{7,6},{8,9},{9,8},{10,11... | collective-permute-start | bytes 294920 | tf_op jit(solution)/shard_map/ppermute | solution.py:23
  17.5 0.1 collective-permute-done.4.packed_ref.other_ref
  17.7 0.2 shard_map.87
  17.8 1.6 %collective-permute-start.6 = (bf16[48,1280]{1,0:T(8,128)(2,1)S(1)}, bf16[48,1280]{1,0:T(8,128)(2,1)S(1)}, u32[]{:S(2)}, u32[]{:S(2)}) collective-permute-start(bf16[48,1280]{1,0:T(8,128)(2,1)S(1)} %get-tuple-element.41.refs_0_), channel_id=1, source_target_pairs={{0,2},{1,3},{2,0},{3,1},{4,6},{5,7},{6,4},{7,5},{8,10},{9,11},{10,... | collective-permute-start | bytes 368648 | tf_op jit(solution)/shard_map/ppermute | solution.py:23
  19.4 0.6 %shard_map.85 = (f32[48,1024]{1,0:T(8,128)S(1)}, bf16[48,1024]{1,0:T(8,128)(2,1)S(1)}) custom-call(bf16[96,1536]{1,0:T(8,128)(2,1)S(1)} %get-tuple-element.32.rows_ref, bf16[1536,1024]{1,0:T(8,128)(2,1)S(1)} %get-tuple-element.33.weight_ref), custom_call_target="tpu_custom_call" | custom-call | flops 2415919104 | tf_op jit(solution)/shard_map/pallas_call | solution.py:283
  20.1 0.1 collective-permute-start.5
  20.2 0.0 collective-permute-done.10.other_ref
  20.2 0.2 shard_map.91
  20.3 0.6 %collective-permute-start.11 = (bf16[48,1024]{1,0:T(8,128)(2,1)S(1)}, bf16[48,1024]{1,0:T(8,128)(2,1)S(1)}, u32[]{:S(2)}, u32[]{:S(2)}) collective-permute-start(bf16[48,1024]{1,0:T(8,128)(2,1)S(1)} %get-tuple-element.48), channel_id=1, source_target_pairs={{0,2},{1,3},{2,0},{3,1},{4,6},{5,7},{6,4},{7,5},{8,10},{9,11},{10,... | collective-permute-start | bytes 294920 | tf_op jit(solution)/shard_map/ppermute | solution.py:23
  20.9 0.5 %collective-permute-done.5.other_ref = bf16[48,1024]{1,0:T(8,128)(2,1)S(1)} collective-permute-done((bf16[48,1024]{1,0:T(8,128)(2,1)S(1)}, bf16[48,1024]{1,0:T(8,128)(2,1)S(1)}, u32[]{:S(2)}, u32[]{:S(2)}) %collective-permute-start.5) | collective-permute-done | bytes 98336 | tf_op jit(solution)/shard_map/ppermute | solution.py:23
  21.4 0.2 shard_map.86
  21.6 1.1 %collective-permute-start.7 = (bf16[48,1024]{1,0:T(8,128)(2,1)S(1)}, bf16[48,1024]{1,0:T(8,128)(2,1)S(1)}, u32[]{:S(2)}, u32[]{:S(2)}) collective-permute-start(bf16[48,1024]{1,0:T(8,128)(2,1)S(1)} %get-tuple-element.42), channel_id=1, source_target_pairs={{0,2},{1,3},{2,0},{3,1},{4,6},{5,7},{6,4},{7,5},{8,10},{9,11},{10,... | collective-permute-start | bytes 294920 | tf_op jit(solution)/shard_map/ppermute | solution.py:23
  22.7 3.3 %collective-permute-done.11.refs_2_ = bf16[48,1024]{1,0:T(8,128)(2,1)S(1)} collective-permute-done((bf16[48,1024]{1,0:T(8,128)(2,1)S(1)}, bf16[48,1024]{1,0:T(8,128)(2,1)S(1)}, u32[]{:S(2)}, u32[]{:S(2)}) %collective-permute-start.11) | collective-permute-done | bytes 98336 | tf_op jit(solution)/shard_map/ppermute | solution.py:23
  26.0 0.0 collective-permute-done.6.refs_1_
  26.0 0.0 copy-done
  26.0 0.3 shard_map.92.refs_2_
  26.3 0.1 collective-permute-start.12
  26.4 0.3 shard_map.89.refs_0_
  26.7 0.6 %collective-permute-start.9 = (bf16[48,1024]{1,0:T(8,128)(2,1)S(1)}, bf16[48,1024]{1,0:T(8,128)(2,1)S(1)}, u32[]{:S(2)}, u32[]{:S(2)}) collective-permute-start(bf16[48,1024]{1,0:T(8,128)(2,1)S(1)} %shard_map.89.refs_0_), channel_id=1, source_target_pairs={{0,1},{1,0},{2,3},{3,2},{4,5},{5,4},{6,7},{7,6},{8,9},{9,8},{10,11... | collective-permute-start | bytes 294920 | tf_op jit(solution)/shard_map/ppermute | solution.py:23
  27.9 0.0 collective-permute-done.7.refs_2_
  27.9 0.3 shard_map.88.refs_0_
  28.2 0.1 collective-permute-start.8
  28.3 0.0 collective-permute-done.12.refs_3_
  28.3 0.0 collective-permute-done.9.refs_1_
  28.4 0.0 slice-done
  28.4 0.0 slice-done.1
  28.4 0.0 slice-done.2
  28.4 1.1 %shard_map.93.refs_3_ = f32[96,1536]{1,0:T(8,128)S(1)} custom-call(bf16[48,1024]{1,0:T(8,128)(2,1)S(1)} %shard_map.89.refs_0_, bf16[48,1024]{1,0:T(8,128)(2,1)S(1)} %collective-permute-done.9.refs_1_, bf16[48,1024]{1,0:T(8,128)(2,1)S(1)} %shard_map.92.refs_2_, bf16[48,1024]{1,0:T(8,128)(2,1)S(1)} %collective-permute-done.12.refs_3_, ...), custom_call_target="tpu_custom_call" | custom-call | flops 4831838208 | tf_op jit(solution)/shard_map/pallas_call | solution.py:313
  29.5 0.0 copy-start.4
  29.5 0.0 copy-start.3
  29.5 0.1 collective-permute-done.8.refs_1_
  29.6 0.6 %shard_map.94 = (f32[48,1536]{1,0:T(8,128)S(1)}, bf16[48,1536]{1,0:T(8,128)(2,1)S(1)}) custom-call(bf16[48,1024]{1,0:T(8,128)(2,1)S(1)} %shard_map.88.refs_0_, bf16[48,1024]{1,0:T(8,128)(2,1)S(1)} %collective-permute-done.8.refs_1_, bf16[3072,1536]{1,0:T(8,128)(2,1)S(1)} %bitcast.4, f32[96,1536]{1,0:T(8,128)S(1)} %shard_map.93.refs_3_), custom_call_target="tpu_custom_call" | custom-call | flops 2415919104 | tf_op jit(solution)/shard_map/pallas_call | solution.py:313
  30.3 1.6 %collective-permute-start.13 = (bf16[24,1536]{1,0:T(8,128)(2,1)S(1)}, bf16[24,1536]{1,0:T(8,128)(2,1)S(1)}, u32[]{:S(2)}, u32[]{:S(2)}) collective-permute-start(bf16[24,1536]{1,0:T(8,128)(2,1)S(1)} %pad_maximum_fusion.1), channel_id=1, source_target_pairs={{0,4},{4,0},{8,12},{12,8},{16,20},{20,16},{24,28},{28,24},{1,5},{5... | collective-permute-start | bytes 221192 | tf_op jit(solution)/shard_map/ppermute | solution.py:23
  32.0 0.6 %collective-permute-start.16 = (bf16[24,1536]{1,0:T(8,128)(2,1)S(1)}, bf16[24,1536]{1,0:T(8,128)(2,1)S(1)}, u32[]{:S(2)}, u32[]{:S(2)}) collective-permute-start(bf16[24,1536]{1,0:T(8,128)(2,1)S(1)} %pad_maximum_fusion.2), channel_id=1, source_target_pairs={{0,4},{4,0},{8,12},{12,8},{16,20},{20,16},{24,28},{28,24},{1,5},{5... | collective-permute-start | bytes 221192 | tf_op jit(solution)/shard_map/ppermute | solution.py:23
  32.6 2.7 %collective-permute-done.13 = bf16[24,1536]{1,0:T(8,128)(2,1)S(1)} collective-permute-done((bf16[24,1536]{1,0:T(8,128)(2,1)S(1)}, bf16[24,1536]{1,0:T(8,128)(2,1)S(1)}, u32[]{:S(2)}, u32[]{:S(2)}) %collective-permute-start.13) | collective-permute-done | bytes 73760 | tf_op jit(solution)/shard_map/ppermute | solution.py:23
  35.3 2.4 %collective-permute-start.14 = (bf16[12,1536]{1,0:T(8,128)(2,1)S(1)}, bf16[12,1536]{1,0:T(8,128)(2,1)S(1)}, u32[]{:S(2)}, u32[]{:S(2)}) collective-permute-start(bf16[12,1536]{1,0:T(8,128)(2,1)S(1)} %get-tuple-element.60), channel_id=1, source_target_pairs={{0,24},{4,28},{8,16},{12,20},{16,8},{20,12},{24,0},{28,4},{1,25},{... | collective-permute-start | bytes 110600 | tf_op jit(solution)/shard_map/ppermute | solution.py:23
  37.7 0.0 collective-permute-start.15
  37.7 0.0 collective-permute-done.16
  37.8 2.1 %collective-permute-start.17 = (bf16[12,1536]{1,0:T(8,128)(2,1)S(1)}, bf16[12,1536]{1,0:T(8,128)(2,1)S(1)}, u32[]{:S(2)}, u32[]{:S(2)}) collective-permute-start(bf16[12,1536]{1,0:T(8,128)(2,1)S(1)} %slice.63), channel_id=1, source_target_pairs={{0,8},{4,12},{8,0},{12,4},{16,24},{20,28},{24,16},{28,20},{1,9},{5... | collective-permute-start | bytes 110600 | tf_op jit(solution)/shard_map/ppermute | solution.py:23
  39.9 0.0 copy-done.4
  39.9 1.4 %collective-permute-done.14 = bf16[12,1536]{1,0:T(8,128)(2,1)S(1)} collective-permute-done((bf16[12,1536]{1,0:T(8,128)(2,1)S(1)}, bf16[12,1536]{1,0:T(8,128)(2,1)S(1)}, u32[]{:S(2)}, u32[]{:S(2)}) %collective-permute-start.14) | collective-permute-done | bytes 36896 | tf_op jit(solution)/shard_map/ppermute | solution.py:23
  41.4 1.5 %collective-permute-done.15 = bf16[12,1536]{1,0:T(8,128)(2,1)S(1)} collective-permute-done((bf16[12,1536]{1,0:T(8,128)(2,1)S(1)}, bf16[12,1536]{1,0:T(8,128)(2,1)S(1)}, u32[]{:S(2)}, u32[]{:S(2)}) %collective-permute-start.15) | collective-permute-done | bytes 36896 | tf_op jit(solution)/shard_map/ppermute | solution.py:23
  42.8 0.0 collective-permute-done.17
  42.8 0.0 copy-done.3
  42.8 0.7 %fusion.3 = bf16[12,1536]{1,0:T(8,128)(2,1)} fusion(f32[24,1536]{1,0:T(8,128)S(1)} %maximum_add_fusion.1, f32[1536]{0:T(1024)S(1)} %copy-done.3, bf16[12,1536]{1,0:T(8,128)(2,1)S(1)} %collective-permute-done.17, bf16[12,1536]{1,0:T(8,128)(2,1)S(1)} %collective-permute-done.14, bf16[12,1536]{1,0:T(8,128)(2,1)S(1)} %collective-permute-done.15, ...), kind=kLoop, calls=%fused_computation.7 | loop fusion | flops 129024 | bytes 227376 | tf_op jit(solution)/shard_map/convert_element_type | solution.py:338
  (13 shorter events, 0.2 us)
Async XLA Ops:
  0.0 10.2 %copy-start.2 = (bf16[12,1536]{1,0:T(8,128)(2,1)S(1)}, bf16[12,1536]{1,0:T(8,128)(2,1)}, u32[]{:S(2)}) copy-start(bf16[12,1536]{1,0:T(8,128)(2,1)} %param.8) | copy-start | bytes 110596
  0.0 11.8 %copy-start.1 = (f32[1536]{0:T(1024)S(1)}, f32[1536]{0:T(1024)}, u32[]{:S(2)}) copy-start(f32[1536]{0:T(1024)} %gain_ref.1) | copy-start | bytes 18436
  0.0 7.5 %collective-permute-start = (bf16[12,1536]{1,0:T(8,128)(2,1)}, bf16[12,1536]{1,0:T(8,128)(2,1)S(1)}, u32[]{:S(2)}, u32[]{:S(2)}) collective-permute-start(bf16[12,1536]{1,0:T(8,128)(2,1)} %param.8), channel_id=1, source_target_pairs={{0,16},{4,20},{8,24},{12,28},{16,0},{20,4},{24,8},{28,12},{1,17},{... | collective-permute-start | bytes 110600 | tf_op jit(solution)/shard_map/ppermute | solution.py:23
  4.0 6.2 %collective-permute-start.1 = (bf16[12,1536]{1,0:T(8,128)(2,1)}, bf16[12,1536]{1,0:T(8,128)(2,1)S(1)}, u32[]{:S(2)}, u32[]{:S(2)}) collective-permute-start(bf16[12,1536]{1,0:T(8,128)(2,1)} %param.8), channel_id=1, source_target_pairs={{0,24},{4,28},{8,16},{12,20},{16,8},{20,12},{24,0},{28,4},{1,25},{... | collective-permute-start | bytes 110600 | tf_op jit(solution)/shard_map/ppermute | solution.py:23
  5.4 4.8 %collective-permute-start.2 = (bf16[12,1536]{1,0:T(8,128)(2,1)}, bf16[12,1536]{1,0:T(8,128)(2,1)S(1)}, u32[]{:S(2)}, u32[]{:S(2)}) collective-permute-start(bf16[12,1536]{1,0:T(8,128)(2,1)} %param.8), channel_id=1, source_target_pairs={{0,8},{4,12},{8,0},{12,4},{16,24},{20,28},{24,16},{28,20},{1,9},{5... | collective-permute-start | bytes 110600 | tf_op jit(solution)/shard_map/ppermute | solution.py:23
  10.3 5.2 %collective-permute-start.3 = (bf16[48,1536]{1,0:T(8,128)(2,1)S(1)}, bf16[48,1536]{1,0:T(8,128)(2,1)S(1)}, u32[]{:S(2)}, u32[]{:S(2)}) collective-permute-start(bf16[48,1536]{1,0:T(8,128)(2,1)S(1)} %pad_maximum_fusion.near_ref), channel_id=1, source_target_pairs={{0,4},{4,0},{8,12},{12,8},{16,20},{20,16},{24,28},{28,24},{1,5},{5... | collective-permute-start | bytes 442376 | tf_op jit(solution)/shard_map/ppermute | solution.py:23
  16.3 1.4 %collective-permute-start.4 = (bf16[48,1280]{1,0:T(8,128)(2,1)S(1)}, bf16[48,1280]{1,0:T(8,128)(2,1)S(1)}, u32[]{:S(2)}, u32[]{:S(2)}) collective-permute-start(bf16[48,1280]{1,0:T(8,128)(2,1)S(1)} %get-tuple-element.37), channel_id=1, source_target_pairs={{0,1},{1,0},{2,3},{3,2},{4,5},{5,4},{6,7},{7,6},{8,9},{9,8},{10,11... | collective-permute-start | bytes 368648 | tf_op jit(solution)/shard_map/ppermute | solution.py:23
  16.3 12.0 %slice-start = ((s8[9437184]{0:T(1024)(128)(4,1)}), s8[4194304]{0:T(1024)(128)(4,1)S(1)}, s32[]{:S(2)}) async-start(s8[9437184]{0:T(1024)(128)(4,1)} %bitcast.3), calls=%async_computation | async-start | bytes 8388608
  16.3 12.0 %slice-start.1 = ((s8[9437184]{0:T(1024)(128)(4,1)}), s8[4194304]{0:T(1024)(128)(4,1)S(1)}, s32[]{:S(2)}) async-start(s8[9437184]{0:T(1024)(128)(4,1)} %bitcast.3), calls=%async_computation.1 | async-start | bytes 8388608
  17.0 3.2 %collective-permute-start.10 = (bf16[48,1024]{1,0:T(8,128)(2,1)S(1)}, bf16[48,1024]{1,0:T(8,128)(2,1)S(1)}, u32[]{:S(2)}, u32[]{:S(2)}) collective-permute-start(bf16[48,1024]{1,0:T(8,128)(2,1)S(1)} %get-tuple-element.46), channel_id=1, source_target_pairs={{0,1},{1,0},{2,3},{3,2},{4,5},{5,4},{6,7},{7,6},{8,9},{9,8},{10,11... | collective-permute-start | bytes 294920 | tf_op jit(solution)/shard_map/ppermute | solution.py:23
  17.8 8.2 %collective-permute-start.6 = (bf16[48,1280]{1,0:T(8,128)(2,1)S(1)}, bf16[48,1280]{1,0:T(8,128)(2,1)S(1)}, u32[]{:S(2)}, u32[]{:S(2)}) collective-permute-start(bf16[48,1280]{1,0:T(8,128)(2,1)S(1)} %get-tuple-element.41.refs_0_), channel_id=1, source_target_pairs={{0,2},{1,3},{2,0},{3,1},{4,6},{5,7},{6,4},{7,5},{8,10},{9,11},{10,... | collective-permute-start | bytes 368648 | tf_op jit(solution)/shard_map/ppermute | solution.py:23
  19.4 6.6 %copy-start = (f32[3072]{0:T(1024)S(1)}, f32[3072]{0:T(1024)}, u32[]{:S(2)}) copy-start(f32[3072]{0:T(1024)} %param.13) | copy-start | bytes 36868
  19.4 8.9 %slice-start.2 = ((s8[9437184]{0:T(1024)(128)(4,1)}), s8[1048576]{0:T(1024)(128)(4,1)S(1)}, s32[]{:S(2)}) async-start(s8[9437184]{0:T(1024)(128)(4,1)} %bitcast.3), calls=%async_computation.2 | async-start | bytes 2097152
  20.1 1.4 %collective-permute-start.5 = (bf16[48,1024]{1,0:T(8,128)(2,1)S(1)}, bf16[48,1024]{1,0:T(8,128)(2,1)S(1)}, u32[]{:S(2)}, u32[]{:S(2)}) collective-permute-start(bf16[48,1024]{1,0:T(8,128)(2,1)S(1)} %get-tuple-element.38), channel_id=1, source_target_pairs={{0,1},{1,0},{2,3},{3,2},{4,5},{5,4},{6,7},{7,6},{8,9},{9,8},{10,11... | collective-permute-start | bytes 294920 | tf_op jit(solution)/shard_map/ppermute | solution.py:23
  20.3 5.7 %collective-permute-start.11 = (bf16[48,1024]{1,0:T(8,128)(2,1)S(1)}, bf16[48,1024]{1,0:T(8,128)(2,1)S(1)}, u32[]{:S(2)}, u32[]{:S(2)}) collective-permute-start(bf16[48,1024]{1,0:T(8,128)(2,1)S(1)} %get-tuple-element.48), channel_id=1, source_target_pairs={{0,2},{1,3},{2,0},{3,1},{4,6},{5,7},{6,4},{7,5},{8,10},{9,11},{10,... | collective-permute-start | bytes 294920 | tf_op jit(solution)/shard_map/ppermute | solution.py:23
  21.6 6.3 %collective-permute-start.7 = (bf16[48,1024]{1,0:T(8,128)(2,1)S(1)}, bf16[48,1024]{1,0:T(8,128)(2,1)S(1)}, u32[]{:S(2)}, u32[]{:S(2)}) collective-permute-start(bf16[48,1024]{1,0:T(8,128)(2,1)S(1)} %get-tuple-element.42), channel_id=1, source_target_pairs={{0,2},{1,3},{2,0},{3,1},{4,6},{5,7},{6,4},{7,5},{8,10},{9,11},{10,... | collective-permute-start | bytes 294920 | tf_op jit(solution)/shard_map/ppermute | solution.py:23
  26.3 2.0 %collective-permute-start.12 = (bf16[48,1024]{1,0:T(8,128)(2,1)S(1)}, bf16[48,1024]{1,0:T(8,128)(2,1)S(1)}, u32[]{:S(2)}, u32[]{:S(2)}) collective-permute-start(bf16[48,1024]{1,0:T(8,128)(2,1)S(1)} %shard_map.92.refs_2_), channel_id=1, source_target_pairs={{0,1},{1,0},{2,3},{3,2},{4,5},{5,4},{6,7},{7,6},{8,9},{9,8},{10,11... | collective-permute-start | bytes 294920 | tf_op jit(solution)/shard_map/ppermute | solution.py:23
  26.7 1.6 %collective-permute-start.9 = (bf16[48,1024]{1,0:T(8,128)(2,1)S(1)}, bf16[48,1024]{1,0:T(8,128)(2,1)S(1)}, u32[]{:S(2)}, u32[]{:S(2)}) collective-permute-start(bf16[48,1024]{1,0:T(8,128)(2,1)S(1)} %shard_map.89.refs_0_), channel_id=1, source_target_pairs={{0,1},{1,0},{2,3},{3,2},{4,5},{5,4},{6,7},{7,6},{8,9},{9,8},{10,11... | collective-permute-start | bytes 294920 | tf_op jit(solution)/shard_map/ppermute | solution.py:23
  28.2 1.4 %collective-permute-start.8 = (bf16[48,1024]{1,0:T(8,128)(2,1)S(1)}, bf16[48,1024]{1,0:T(8,128)(2,1)S(1)}, u32[]{:S(2)}, u32[]{:S(2)}) collective-permute-start(bf16[48,1024]{1,0:T(8,128)(2,1)S(1)} %shard_map.88.refs_0_), channel_id=1, source_target_pairs={{0,1},{1,0},{2,3},{3,2},{4,5},{5,4},{6,7},{7,6},{8,9},{9,8},{10,11... | collective-permute-start | bytes 294920 | tf_op jit(solution)/shard_map/ppermute | solution.py:23
  29.5 10.4 %copy-start.4 = (s32[12]{0:T(128)S(1)}, s32[12]{0:T(128)}, u32[]{:S(2)}) copy-start(s32[12]{0:T(128)} %param.10) | copy-start | bytes 148
  29.5 13.3 %copy-start.3 = (f32[1536]{0:T(1024)S(1)}, f32[1536]{0:T(1024)}, u32[]{:S(2)}) copy-start(f32[1536]{0:T(1024)} %param.15) | copy-start | bytes 18436
  30.3 4.9 %collective-permute-start.13 = (bf16[24,1536]{1,0:T(8,128)(2,1)S(1)}, bf16[24,1536]{1,0:T(8,128)(2,1)S(1)}, u32[]{:S(2)}, u32[]{:S(2)}) collective-permute-start(bf16[24,1536]{1,0:T(8,128)(2,1)S(1)} %pad_maximum_fusion.1), channel_id=1, source_target_pairs={{0,4},{4,0},{8,12},{12,8},{16,20},{20,16},{24,28},{28,24},{1,5},{5... | collective-permute-start | bytes 221192 | tf_op jit(solution)/shard_map/ppermute | solution.py:23
  32.0 5.8 %collective-permute-start.16 = (bf16[24,1536]{1,0:T(8,128)(2,1)S(1)}, bf16[24,1536]{1,0:T(8,128)(2,1)S(1)}, u32[]{:S(2)}, u32[]{:S(2)}) collective-permute-start(bf16[24,1536]{1,0:T(8,128)(2,1)S(1)} %pad_maximum_fusion.2), channel_id=1, source_target_pairs={{0,4},{4,0},{8,12},{12,8},{16,20},{20,16},{24,28},{28,24},{1,5},{5... | collective-permute-start | bytes 221192 | tf_op jit(solution)/shard_map/ppermute | solution.py:23
  35.3 6.0 %collective-permute-start.14 = (bf16[12,1536]{1,0:T(8,128)(2,1)S(1)}, bf16[12,1536]{1,0:T(8,128)(2,1)S(1)}, u32[]{:S(2)}, u32[]{:S(2)}) collective-permute-start(bf16[12,1536]{1,0:T(8,128)(2,1)S(1)} %get-tuple-element.60), channel_id=1, source_target_pairs={{0,24},{4,28},{8,16},{12,20},{16,8},{20,12},{24,0},{28,4},{1,25},{... | collective-permute-start | bytes 110600 | tf_op jit(solution)/shard_map/ppermute | solution.py:23
  37.7 5.1 %collective-permute-start.15 = (bf16[12,1536]{1,0:T(8,128)(2,1)S(1)}, bf16[12,1536]{1,0:T(8,128)(2,1)S(1)}, u32[]{:S(2)}, u32[]{:S(2)}) collective-permute-start(bf16[12,1536]{1,0:T(8,128)(2,1)S(1)} %get-tuple-element.59), channel_id=1, source_target_pairs={{0,16},{4,20},{8,24},{12,28},{16,0},{20,4},{24,8},{28,12},{1,17},{... | collective-permute-start | bytes 110600 | tf_op jit(solution)/shard_map/ppermute | solution.py:23
  37.8 5.1 %collective-permute-start.17 = (bf16[12,1536]{1,0:T(8,128)(2,1)S(1)}, bf16[12,1536]{1,0:T(8,128)(2,1)S(1)}, u32[]{:S(2)}, u32[]{:S(2)}) collective-permute-start(bf16[12,1536]{1,0:T(8,128)(2,1)S(1)} %slice.63), channel_id=1, source_target_pairs={{0,8},{4,12},{8,0},{12,4},{16,24},{20,28},{24,16},{28,20},{1,9},{5... | collective-permute-start | bytes 110600 | tf_op jit(solution)/shard_map/ppermute | solution.py:23
